TPU v7x, 32 devices: a whole 2x2x4 slice. The times are simulated.
32 devices in a mesh: section: 4 (over z), dp: 8 (over y, x, core).
Axes of the slice: x: 2, y: 2, z: 4, core: 2. Of those that a mesh axis runs over, the one named last changes fastest.
Arguments:
- inputs: bfloat16 [4, 256, 6144], P(None, 'dp', 'section'), may hold values from -6 to 6
- gain: float32 [4, 6144], P('section'), may hold values from 0.1 to 1.9
- repeats: int32 [4], P('section'), may hold values from 0 to 3
- order: int32 [4], replicated, may hold values from 0 to 3, each once
- hidden_grad: bfloat16 [4, 4, 256, 12288], P('section', None, 'dp'), may hold values from -6 to 6
Outputs:
- feature_factor: float32 [4, 3072, 128], P('section', 'dp')
- hidden_factor: float32 [4, 12288, 128], P('section', 'dp')
Inputs may be any that keep to these rules, and one draw needn't show every extreme that they name: `order`: each micro-batch id once.
All inputs are finite; a program needn't handle non-finite values.
Results may differ from a plain program's by a relative error of at most 0.0085.
Values may be sent and summed in bfloat16 or wider, within the bound.
No kernel may reach another device: no remote copies, remote signals or barrier semaphores. Data moves between devices by JAX's collectives and lax.ppermute only.
A program may use at most 128 MiB of HBM per device.

v0:
```python
import jax
import jax.numpy as jnp
from jax import lax
from jax.sharding import PartitionSpec as P

AWIN = 3072
GWIN = 12288
BLK = 128


def from_behind(shard, axis, by):
    length = lax.axis_size(axis)
    pairs = [(i, i + by) for i in range(length) if 0 <= i + by < length]
    return lax.ppermute(shard, axis, pairs)


def normed(value, gain_row):
    wide = value.astype(jnp.float32)
    center = jnp.mean(wide, axis=-1, keepdims=True)
    spread = jnp.mean(jnp.square(wide - center), axis=-1, keepdims=True)
    return (wide - center) * lax.rsqrt(spread + 1e-05) * gain_row


def update(value, gain_row):
    return (value.astype(jnp.float32) + jax.nn.gelu(normed(value, gain_row))).astype(jnp.bfloat16)


def block_gram(feats, blocks, width):
    shaped = feats.reshape(feats.shape[0], blocks, width)
    return jnp.einsum("tbi,tbj->bij", shaped, shaped, preferred_element_type=jnp.float32)


def body(inputs, gain, repeats, order, hidden_grad):
    micro = inputs.shape[0]
    tok_rows = inputs.shape[1]
    dp_count = lax.axis_size("dp")
    total_tok = tok_rows * dp_count
    awin_blocks = AWIN // BLK
    gwin_blocks = GWIN // BLK
    section_id = lax.axis_index("section")
    gain_row = gain[0]
    slots = jnp.arange(micro, dtype=jnp.float32)
    slot_weight = 0.5 * jnp.power(0.5, micro - 1 - slots)
    onehot = (order[:, None] == jnp.arange(micro, dtype=jnp.int32)[None, :]).astype(jnp.float32)
    hidden_weight = jnp.dot(slot_weight, onehot, precision=lax.Precision.HIGHEST)
    hidden_acc = jnp.zeros((gwin_blocks, BLK, BLK), jnp.float32)
    for batch_id in range(micro):
        hidden_acc = hidden_acc + hidden_weight[batch_id] * block_gram(
            hidden_grad[0, batch_id], gwin_blocks, BLK
        )
    hidden_term = (hidden_acc / total_tok).reshape(GWIN, BLK)
    whole = lax.all_gather(inputs, "section", axis=2, tiled=True)
    ordered = jnp.take(whole, order, axis=0)

    def advance(step, carry):
        held, feature_acc = carry
        came = from_behind(held, "section", 1)
        fresh = lax.dynamic_index_in_dim(ordered, jnp.minimum(step, micro - 1), 0, keepdims=False)
        current = jnp.where(section_id == 0, fresh, came)
        current = lax.fori_loop(0, repeats[0] + 1, lambda i, v: update(v, gain_row), current)
        slot = step - section_id
        live = jnp.logical_and(slot >= 0, slot < micro)
        weight_now = jnp.where(live, slot_weight[jnp.clip(slot, 0, micro - 1)], 0.0)
        feats = normed(current, gain_row).astype(jnp.bfloat16)[:, :AWIN]
        return (current, feature_acc + weight_now * block_gram(feats, awin_blocks, BLK))

    start_held = jnp.zeros((tok_rows, whole.shape[2]), jnp.bfloat16)
    start_acc = jnp.zeros((awin_blocks, BLK, BLK), jnp.float32)
    steps_total = lax.axis_size("section") + micro - 1
    final_held, feature_acc = lax.fori_loop(0, steps_total, advance, (start_held, start_acc))
    feature_term = (feature_acc / total_tok).reshape(AWIN, BLK)
    feature_sum = lax.psum(feature_term.astype(jnp.bfloat16), "dp").astype(jnp.float32)
    own_rows = AWIN // dp_count
    feature_rows = lax.dynamic_slice_in_dim(
        feature_sum, lax.axis_index("dp") * own_rows, own_rows, 0
    )
    hidden_rows = lax.psum_scatter(
        hidden_term.astype(jnp.bfloat16), "dp", scatter_dimension=0, tiled=True
    ).astype(jnp.float32)
    return (feature_rows[None], hidden_rows[None])


def solution(mesh):
    placed = (
        P(None, "dp", "section"),
        P("section", None),
        P("section"),
        P(),
        P("section", None, "dp", None),
    )
    return jax.shard_map(
        body,
        mesh=mesh,
        in_specs=placed,
        out_specs=(P("section", "dp", None), P("section", "dp", None)),
        check_vma=False,
    )
```

profile of v0, /device:TPU:0, one launch (start us, length us, event | category | flops | bytes accessed | tf_op | source)
XLA Modules:
  0.0 284.1 jit_solution(1767536158065867050)
XLA Ops:
  7.2 0.7 all-gather.2.cloned.1.call-update
  8.0 2.1 slice_bitcast_fusion
  10.3 1.0 copy.18
  11.3 1.0 copy.21
  13.2 0.6 fusion.28
  13.9 3.7 %fusion.18 = f32[96,128,128]{2,1,0:T(8,128)} fusion(bf16[32,96,128]{2,1,0:T(8,128)(2,1)S(1)} %bitcast.65), kind=kOutput, calls=%fused_computation.37 | convolution fusion | flops 100663296 | bytes 7077888 | tf_op jit(solution)/shard_map/tbi,tbj->bij/dot_general | solution.py:30
  17.6 3.7 %fusion.20 = f32[96,128,128]{2,1,0:T(8,128)} fusion(bf16[32,96,128]{2,1,0:T(8,128)(2,1)S(1)} %bitcast.66), kind=kOutput, calls=%fused_computation.39 | convolution fusion | flops 100663296 | bytes 7077888 | tf_op jit(solution)/shard_map/tbi,tbj->bij/dot_general | solution.py:30
  21.3 3.6 %fusion.22 = f32[96,128,128]{2,1,0:T(8,128)} fusion(bf16[32,96,128]{2,1,0:T(8,128)(2,1)S(1)} %bitcast.67), kind=kOutput, calls=%fused_computation.41 | convolution fusion | flops 100663296 | bytes 7077888 | tf_op jit(solution)/shard_map/tbi,tbj->bij/dot_general | solution.py:30
  24.9 24.5 %all-gather.2.cloned.1.call-done = bf16[4,32,6144]{2,1,0:T(8,128)(2,1)} async-done(((bf16[4,32,1536]{2,1,0:T(8,128)(2,1)}), bf16[4,32,6144]{2,1,0:T(8,128)(2,1)}) %all-gather.2.cloned.1.call-update) | async-done | bytes 1572880 | tf_op jit(solution)/shard_map/all_gather | solution.py:52
  49.4 2.1 gather_fusion
  51.5 1.4 broadcast_select_fusion
  52.9 111.2 %while.44 = (s32[]{:T(128)}, bf16[32,6144]{1,0:T(8,128)(2,1)S(1)}, f32[24,128,128]{2,1,0:T(8,128)S(1)}, pred[]{:T(512)}, bf16[4,32,6144]{2,1,0:T(8,128)(2,1)}, /...) while((s32[]{:T(128)}, bf16[32,6144]{1,0:T(8,128)(2,1)S(1)}, ...), condition=%wide.region_7.8_spmd.clone, body=%wide.region_0.7_spmd.clone.sunk | while | flops 31948880 | bytes 9501629 | solution.py:70
  52.9 2.4 collective-permute-start
  55.3 0.6 dynamic_slice.31
  56.6 6.8 %collective-permute-done = bf16[32,6144]{1,0:T(8,128)(2,1)S(1)} collective-permute-done((bf16[32,6144]{1,0:T(8,128)(2,1)S(1)}, bf16[32,6144]{1,0:T(8,128)(2,1)S(1)}, u32[]{:S(2)}, u32[]{:S(2)}) %collective-permute-start) | collective-permute-done | bytes 393248 | tf_op jit(solution)/shard_map/while/body/eval_jaxpr/ppermute | solution.py:14
  63.4 1.1 bitcast_select_fusion.2
  64.4 2.9 %while.45 = (s32[]{:T(128)}, bf16[32,6144]{1,0:T(8,128)(2,1)S(1)}, s32[]{:T(128)}, f32[1,6144]{1,0:T(1,128)S(1)}, s32[]{:T(128)}) while((s32[]{:T(128)}, bf16[32,6144]{1,0:T(8,128)(2,1)S(1)}, s32[]{:T(128)}, f32[1,6144]{1,0:T(1,128)S(1)}, s32[]{:T(128)}) %tuple.69), condition=%wide.region_4.4_spmd, body=%wide.region_1.3_spmd.sunk | while | flops 3932194 | bytes 1598653 | solution.py:60
  65.9 0.5 fusion.38
  67.9 0.7 select_add_fusion.2
  68.6 2.4 collective-permute-start
  71.1 0.6 dynamic_slice.31
  72.4 5.9 %collective-permute-done = bf16[32,6144]{1,0:T(8,128)(2,1)S(1)} collective-permute-done((bf16[32,6144]{1,0:T(8,128)(2,1)S(1)}, bf16[32,6144]{1,0:T(8,128)(2,1)S(1)}, u32[]{:S(2)}, u32[]{:S(2)}) %collective-permute-start) | collective-permute-done | bytes 393248 | tf_op jit(solution)/shard_map/while/body/eval_jaxpr/ppermute | solution.py:14
  78.3 1.1 bitcast_select_fusion.2
  79.3 2.9 %while.45 = (s32[]{:T(128)}, bf16[32,6144]{1,0:T(8,128)(2,1)S(1)}, s32[]{:T(128)}, f32[1,6144]{1,0:T(1,128)S(1)}, s32[]{:T(128)}) while((s32[]{:T(128)}, bf16[32,6144]{1,0:T(8,128)(2,1)S(1)}, s32[]{:T(128)}, f32[1,6144]{1,0:T(1,128)S(1)}, s32[]{:T(128)}) %tuple.69), condition=%wide.region_4.4_spmd, body=%wide.region_1.3_spmd.sunk | while | flops 3932194 | bytes 1598653 | solution.py:60
  81.8 0.5 fusion.38
  82.8 0.7 select_add_fusion.2
  83.5 4.8 %collective-permute-start = (bf16[32,6144]{1,0:T(8,128)(2,1)S(1)}, bf16[32,6144]{1,0:T(8,128)(2,1)S(1)}, u32[]{:S(2)}, u32[]{:S(2)}) collective-permute-start(bf16[32,6144]{1,0:T(8,128)(2,1)S(1)} %get-tuple-element.421), channel_id=1, source_target_pairs={{0,8},{8,16},{16,24},{1,9},{9,17},{17,25},{2,10},{10,18},{18,26},{... | collective-permute-start | bytes 1179656 | tf_op jit(solution)/shard_map/while/body/eval_jaxpr/ppermute | solution.py:14
  88.4 0.6 dynamic_slice.31
  89.6 5.2 %collective-permute-done = bf16[32,6144]{1,0:T(8,128)(2,1)S(1)} collective-permute-done((bf16[32,6144]{1,0:T(8,128)(2,1)S(1)}, bf16[32,6144]{1,0:T(8,128)(2,1)S(1)}, u32[]{:S(2)}, u32[]{:S(2)}) %collective-permute-start) | collective-permute-done | bytes 393248 | tf_op jit(solution)/shard_map/while/body/eval_jaxpr/ppermute | solution.py:14
  94.8 1.1 bitcast_select_fusion.2
  95.9 2.9 %while.45 = (s32[]{:T(128)}, bf16[32,6144]{1,0:T(8,128)(2,1)S(1)}, s32[]{:T(128)}, f32[1,6144]{1,0:T(1,128)S(1)}, s32[]{:T(128)}) while((s32[]{:T(128)}, bf16[32,6144]{1,0:T(8,128)(2,1)S(1)}, s32[]{:T(128)}, f32[1,6144]{1,0:T(1,128)S(1)}, s32[]{:T(128)}) %tuple.69), condition=%wide.region_4.4_spmd, body=%wide.region_1.3_spmd.sunk | while | flops 3932194 | bytes 1598653 | solution.py:60
  96.4 0.5 fusion.38
  99.3 0.7 select_add_fusion.2
  100.1 5.4 %collective-permute-start = (bf16[32,6144]{1,0:T(8,128)(2,1)S(1)}, bf16[32,6144]{1,0:T(8,128)(2,1)S(1)}, u32[]{:S(2)}, u32[]{:S(2)}) collective-permute-start(bf16[32,6144]{1,0:T(8,128)(2,1)S(1)} %get-tuple-element.421), channel_id=1, source_target_pairs={{0,8},{8,16},{16,24},{1,9},{9,17},{17,25},{2,10},{10,18},{18,26},{... | collective-permute-start | bytes 1179656 | tf_op jit(solution)/shard_map/while/body/eval_jaxpr/ppermute | solution.py:14
  105.5 0.6 dynamic_slice.31
  106.8 4.3 %collective-permute-done = bf16[32,6144]{1,0:T(8,128)(2,1)S(1)} collective-permute-done((bf16[32,6144]{1,0:T(8,128)(2,1)S(1)}, bf16[32,6144]{1,0:T(8,128)(2,1)S(1)}, u32[]{:S(2)}, u32[]{:S(2)}) %collective-permute-start) | collective-permute-done | bytes 393248 | tf_op jit(solution)/shard_map/while/body/eval_jaxpr/ppermute | solution.py:14
  111.1 1.1 bitcast_select_fusion.2
  112.2 2.9 %while.45 = (s32[]{:T(128)}, bf16[32,6144]{1,0:T(8,128)(2,1)S(1)}, s32[]{:T(128)}, f32[1,6144]{1,0:T(1,128)S(1)}, s32[]{:T(128)}) while((s32[]{:T(128)}, bf16[32,6144]{1,0:T(8,128)(2,1)S(1)}, s32[]{:T(128)}, f32[1,6144]{1,0:T(1,128)S(1)}, s32[]{:T(128)}) %tuple.69), condition=%wide.region_4.4_spmd, body=%wide.region_1.3_spmd.sunk | while | flops 3932194 | bytes 1598653 | solution.py:60
  115.6 0.7 select_add_fusion.2
  116.3 5.4 %collective-permute-start = (bf16[32,6144]{1,0:T(8,128)(2,1)S(1)}, bf16[32,6144]{1,0:T(8,128)(2,1)S(1)}, u32[]{:S(2)}, u32[]{:S(2)}) collective-permute-start(bf16[32,6144]{1,0:T(8,128)(2,1)S(1)} %get-tuple-element.421), channel_id=1, source_target_pairs={{0,8},{8,16},{16,24},{1,9},{9,17},{17,25},{2,10},{10,18},{18,26},{... | collective-permute-start | bytes 1179656 | tf_op jit(solution)/shard_map/while/body/eval_jaxpr/ppermute | solution.py:14
  121.8 0.6 dynamic_slice.31
  123.0 4.0 %collective-permute-done = bf16[32,6144]{1,0:T(8,128)(2,1)S(1)} collective-permute-done((bf16[32,6144]{1,0:T(8,128)(2,1)S(1)}, bf16[32,6144]{1,0:T(8,128)(2,1)S(1)}, u32[]{:S(2)}, u32[]{:S(2)}) %collective-permute-start) | collective-permute-done | bytes 393248 | tf_op jit(solution)/shard_map/while/body/eval_jaxpr/ppermute | solution.py:14
  127.0 1.1 bitcast_select_fusion.2
  128.1 2.9 %while.45 = (s32[]{:T(128)}, bf16[32,6144]{1,0:T(8,128)(2,1)S(1)}, s32[]{:T(128)}, f32[1,6144]{1,0:T(1,128)S(1)}, s32[]{:T(128)}) while((s32[]{:T(128)}, bf16[32,6144]{1,0:T(8,128)(2,1)S(1)}, s32[]{:T(128)}, f32[1,6144]{1,0:T(1,128)S(1)}, s32[]{:T(128)}) %tuple.69), condition=%wide.region_4.4_spmd, body=%wide.region_1.3_spmd.sunk | while | flops 3932194 | bytes 1598653 | solution.py:60
  131.5 0.7 select_add_fusion.2
  132.2 5.4 %collective-permute-start = (bf16[32,6144]{1,0:T(8,128)(2,1)S(1)}, bf16[32,6144]{1,0:T(8,128)(2,1)S(1)}, u32[]{:S(2)}, u32[]{:S(2)}) collective-permute-start(bf16[32,6144]{1,0:T(8,128)(2,1)S(1)} %get-tuple-element.421), channel_id=1, source_target_pairs={{0,8},{8,16},{16,24},{1,9},{9,17},{17,25},{2,10},{10,18},{18,26},{... | collective-permute-start | bytes 1179656 | tf_op jit(solution)/shard_map/while/body/eval_jaxpr/ppermute | solution.py:14
  137.7 0.6 dynamic_slice.31
  138.9 4.0 %collective-permute-done = bf16[32,6144]{1,0:T(8,128)(2,1)S(1)} collective-permute-done((bf16[32,6144]{1,0:T(8,128)(2,1)S(1)}, bf16[32,6144]{1,0:T(8,128)(2,1)S(1)}, u32[]{:S(2)}, u32[]{:S(2)}) %collective-permute-start) | collective-permute-done | bytes 393248 | tf_op jit(solution)/shard_map/while/body/eval_jaxpr/ppermute | solution.py:14
  142.9 1.1 bitcast_select_fusion.2
  143.9 2.9 %while.45 = (s32[]{:T(128)}, bf16[32,6144]{1,0:T(8,128)(2,1)S(1)}, s32[]{:T(128)}, f32[1,6144]{1,0:T(1,128)S(1)}, s32[]{:T(128)}) while((s32[]{:T(128)}, bf16[32,6144]{1,0:T(8,128)(2,1)S(1)}, s32[]{:T(128)}, f32[1,6144]{1,0:T(1,128)S(1)}, s32[]{:T(128)}) %tuple.69), condition=%wide.region_4.4_spmd, body=%wide.region_1.3_spmd.sunk | while | flops 3932194 | bytes 1598653 | solution.py:60
  147.4 0.7 select_add_fusion.2
  148.1 5.4 %collective-permute-start = (bf16[32,6144]{1,0:T(8,128)(2,1)S(1)}, bf16[32,6144]{1,0:T(8,128)(2,1)S(1)}, u32[]{:S(2)}, u32[]{:S(2)}) collective-permute-start(bf16[32,6144]{1,0:T(8,128)(2,1)S(1)} %get-tuple-element.421), channel_id=1, source_target_pairs={{0,8},{8,16},{16,24},{1,9},{9,17},{17,25},{2,10},{10,18},{18,26},{... | collective-permute-start | bytes 1179656 | tf_op jit(solution)/shard_map/while/body/eval_jaxpr/ppermute | solution.py:14
  153.6 0.6 dynamic_slice.31
  154.8 4.0 %collective-permute-done = bf16[32,6144]{1,0:T(8,128)(2,1)S(1)} collective-permute-done((bf16[32,6144]{1,0:T(8,128)(2,1)S(1)}, bf16[32,6144]{1,0:T(8,128)(2,1)S(1)}, u32[]{:S(2)}, u32[]{:S(2)}) %collective-permute-start) | collective-permute-done | bytes 393248 | tf_op jit(solution)/shard_map/while/body/eval_jaxpr/ppermute | solution.py:14
  158.8 1.1 bitcast_select_fusion.2
  159.8 2.9 %while.45 = (s32[]{:T(128)}, bf16[32,6144]{1,0:T(8,128)(2,1)S(1)}, s32[]{:T(128)}, f32[1,6144]{1,0:T(1,128)S(1)}, s32[]{:T(128)}) while((s32[]{:T(128)}, bf16[32,6144]{1,0:T(8,128)(2,1)S(1)}, s32[]{:T(128)}, f32[1,6144]{1,0:T(1,128)S(1)}, s32[]{:T(128)}) %tuple.69), condition=%wide.region_4.4_spmd, body=%wide.region_1.3_spmd.sunk | while | flops 3932194 | bytes 1598653 | solution.py:60
  160.4 0.5 fusion.38
  163.3 0.7 select_add_fusion.2
  164.0 1.1 multiply_convert_fusion.1
  165.2 11.9 %multiply_convert_fusion = bf16[96,128,128]{2,1,0:T(8,128)(2,1)} fusion(f32[96,128,128]{2,1,0:T(8,128)} %fusion.18, f32[96,128,128]{2,1,0:T(8,128)} %fusion.20, f32[96,128,128]{2,1,0:T(8,128)} %fusion.22, f32[]{:T(128)} %bitcast.9, f32[]{:T(128)} %bitcast.8, f32[]{:T(128)} %bitcast.7, f32[]{:T(128)} %bitcast.6, bf16[32,96,128]{2,1,0:T(8,128)(2,1)S(1)} %bitcast.64), kind=kOutput, calls=%fused_computation.32 | convolution fusion | flops 114819072 | bytes 22806544 | tf_op jit(solution)/shard_map/tbi,tbj->bij/dot_general | solution.py:30
  177.1 49.6 %all-reduce.2.cloned.1.call-done = bf16[3072,128]{1,0:T(8,128)(2,1)} async-done(((bf16[3072,128]{1,0:T(8,128)(2,1)}), bf16[3072,128]{1,0:T(8,128)(2,1)}) %all-reduce.2.cloned.1.call-update) | async-done | bytes 786448 | tf_op jit(solution)/shard_map/psum | solution.py:72
  226.7 1.6 convert_bitcast_fusion
  228.3 47.3 %reduce-scatter.2.cloned.1.call-done = bf16[1536,128]{1,0:T(8,128)(2,1)} async-done(((bf16[12288,128]{1,0:T(8,128)(2,1)}), bf16[1536,128]{1,0:T(8,128)(2,1)}) %reduce-scatter.2.cloned.1.call-update) | async-done | bytes 393232 | tf_op jit(solution)/shard_map/reduce_scatter | solution.py:77
  275.6 1.9 bitcast_convert_fusion
  (158 shorter events, 22.4 us)
Async XLA Ops:
  7.2 42.2 %all-gather.2.cloned.1.call-start = ((), (), s32[]{:S(2)}) async-start(), calls=%async_computation.1 | async-start | bytes 1966080 | tf_op jit(solution)/shard_map/all_gather | solution.py:52
  7.9 218.8 %all-reduce.2.cloned.1.call-start = ((), (), s32[]{:S(2)}) async-start(), calls=%async_computation.2 | async-start | bytes 1572864 | tf_op jit(solution)/shard_map/psum | solution.py:72
  10.0 3.0 %copy-start.3 = (s32[4]{0:T(128)S(1)}, s32[4]{0:T(128)}, u32[]{:S(2)}) copy-start(s32[4]{0:T(128)} %param.12) | copy-start | bytes 52
  17.6 3.7 %copy-start.2 = (bf16[4,8,96,128]{3,2,1,0:T(8,128)(2,1)S(1)}, bf16[4,8,96,128]{3,2,1,0:T(8,128)(2,1)}, u32[]{:S(2)}) copy-start(bf16[4,8,96,128]{3,2,1,0:T(8,128)(2,1)} %copy.18) | copy-start | bytes 2359300
  24.9 28.0 %copy-start = (f32[1,6144]{1,0:T(1,128)S(1)}, f32[1,6144]{1,0:T(1,128)}, u32[]{:S(2)}) copy-start(f32[1,6144]{1,0:T(1,128)} %param.10) | copy-start | bytes 73732
  52.9 10.5 %collective-permute-start = (bf16[32,6144]{1,0:T(8,128)(2,1)S(1)}, bf16[32,6144]{1,0:T(8,128)(2,1)S(1)}, u32[]{:S(2)}, u32[]{:S(2)}) collective-permute-start(bf16[32,6144]{1,0:T(8,128)(2,1)S(1)} %get-tuple-element.421), channel_id=1, source_target_pairs={{0,8},{8,16},{16,24},{1,9},{9,17},{17,25},{2,10},{10,18},{18,26},{... | collective-permute-start | bytes 1179656 | tf_op jit(solution)/shard_map/while/body/eval_jaxpr/ppermute | solution.py:14
  68.6 9.7 %collective-permute-start = (bf16[32,6144]{1,0:T(8,128)(2,1)S(1)}, bf16[32,6144]{1,0:T(8,128)(2,1)S(1)}, u32[]{:S(2)}, u32[]{:S(2)}) collective-permute-start(bf16[32,6144]{1,0:T(8,128)(2,1)S(1)} %get-tuple-element.421), channel_id=1, source_target_pairs={{0,8},{8,16},{16,24},{1,9},{9,17},{17,25},{2,10},{10,18},{18,26},{... | collective-permute-start | bytes 1179656 | tf_op jit(solution)/shard_map/while/body/eval_jaxpr/ppermute | solution.py:14
  83.5 11.3 %collective-permute-start = (bf16[32,6144]{1,0:T(8,128)(2,1)S(1)}, bf16[32,6144]{1,0:T(8,128)(2,1)S(1)}, u32[]{:S(2)}, u32[]{:S(2)}) collective-permute-start(bf16[32,6144]{1,0:T(8,128)(2,1)S(1)} %get-tuple-element.421), channel_id=1, source_target_pairs={{0,8},{8,16},{16,24},{1,9},{9,17},{17,25},{2,10},{10,18},{18,26},{... | collective-permute-start | bytes 1179656 | tf_op jit(solution)/shard_map/while/body/eval_jaxpr/ppermute | solution.py:14
  100.1 11.0 %collective-permute-start = (bf16[32,6144]{1,0:T(8,128)(2,1)S(1)}, bf16[32,6144]{1,0:T(8,128)(2,1)S(1)}, u32[]{:S(2)}, u32[]{:S(2)}) collective-permute-start(bf16[32,6144]{1,0:T(8,128)(2,1)S(1)} %get-tuple-element.421), channel_id=1, source_target_pairs={{0,8},{8,16},{16,24},{1,9},{9,17},{17,25},{2,10},{10,18},{18,26},{... | collective-permute-start | bytes 1179656 | tf_op jit(solution)/shard_map/while/body/eval_jaxpr/ppermute | solution.py:14
  116.3 10.7 %collective-permute-start = (bf16[32,6144]{1,0:T(8,128)(2,1)S(1)}, bf16[32,6144]{1,0:T(8,128)(2,1)S(1)}, u32[]{:S(2)}, u32[]{:S(2)}) collective-permute-start(bf16[32,6144]{1,0:T(8,128)(2,1)S(1)} %get-tuple-element.421), channel_id=1, source_target_pairs={{0,8},{8,16},{16,24},{1,9},{9,17},{17,25},{2,10},{10,18},{18,26},{... | collective-permute-start | bytes 1179656 | tf_op jit(solution)/shard_map/while/body/eval_jaxpr/ppermute | solution.py:14
  132.2 10.7 %collective-permute-start = (bf16[32,6144]{1,0:T(8,128)(2,1)S(1)}, bf16[32,6144]{1,0:T(8,128)(2,1)S(1)}, u32[]{:S(2)}, u32[]{:S(2)}) collective-permute-start(bf16[32,6144]{1,0:T(8,128)(2,1)S(1)} %get-tuple-element.421), channel_id=1, source_target_pairs={{0,8},{8,16},{16,24},{1,9},{9,17},{17,25},{2,10},{10,18},{18,26},{... | collective-permute-start | bytes 1179656 | tf_op jit(solution)/shard_map/while/body/eval_jaxpr/ppermute | solution.py:14
  148.1 10.7 %collective-permute-start = (bf16[32,6144]{1,0:T(8,128)(2,1)S(1)}, bf16[32,6144]{1,0:T(8,128)(2,1)S(1)}, u32[]{:S(2)}, u32[]{:S(2)}) collective-permute-start(bf16[32,6144]{1,0:T(8,128)(2,1)S(1)} %get-tuple-element.421), channel_id=1, source_target_pairs={{0,8},{8,16},{16,24},{1,9},{9,17},{17,25},{2,10},{10,18},{18,26},{... | collective-permute-start | bytes 1179656 | tf_op jit(solution)/shard_map/while/body/eval_jaxpr/ppermute | solution.py:14
  164.0 1.2 copy-start.1
  165.1 110.5 %reduce-scatter.2.cloned.1.call-start = ((), (), s32[]{:S(2)}) async-start(), calls=%async_computation.3 | async-start | bytes 3538944 | tf_op jit(solution)/shard_map/reduce_scatter | solution.py:77
Sparse Core Ops, SparseCore 0:
  9.6 39.7 all-gather.1
  165.3 61.4 all-reduce.1
  230.1 45.4 reduce-scatter.1
where the time goes:
time: 285 us; the launch traced here: 284 us
  waiting for transfers between devices  156 us (55%)
  other arithmetic  36.8 us (13%)
  starting transfers between devices  31.3 us (11%)
  matrix products  28.1 us (10%)
  between operations  14.5 us (5%)
  local copies, waits for them, and re-layouts  11.4 us (4%)
  loops' own time  5.63 us (2%)
    psum x1, waiting for transfers between devices, body(): lax.psum(feature_term.astype(jnp.bfloat16), 'dp').astype(jnp.float32)  49.6 us
    reduce_scatter x1, waiting for transfers between devices, body(): lax.psum_scatter(hidden_term.astype(jnp.bfloat16), 'dp', scatter_dimensio...  47.3 us
    ppermute x7, waiting for transfers between devices, from_behind(): return lax.ppermute(shard, axis, pairs)  34.2 us
    ppermute x7, starting transfers between devices, from_behind(): return lax.ppermute(shard, axis, pairs)  31.2 us
    dot_general x11, matrix products, block_gram(): jnp.einsum('tbi,tbj->bij', shaped, shaped, preferred_element_type=jnp.flo...  27.9 us
    all_gather x1, waiting for transfers between devices, body(): whole = lax.all_gather(inputs, 'section', axis=2, tiled=True)  24.5 us
    convert_element_type x21, other arithmetic, update(): (value.astype(jnp.float32) + jax.nn.gelu(normed(value, gain_row))).astype...  9.85 us
    reduce_sum x28, other arithmetic, normed(): spread = jnp.mean(jnp.square(wide - center), axis=-1, keepdims=True)  8.27 us
  transfers between devices with their start and end apart: 10, of which 10 were waited for; matrix products, arithmetic and copies ran while one was open for 12% of the time, Pallas kernels for 0%

commit v1 on v0

v1 whole, which is shorter than its diff:
```python
import functools

import jax
import jax.numpy as jnp
from jax import lax
from jax.experimental import pallas as pl
from jax.experimental.pallas import tpu as pltpu
from jax.sharding import PartitionSpec as P

AWIN = 3072
GWIN = 12288
BLK = 128
VMEM_LIMIT = 48 * 1024 * 1024

SMEM_SPEC = pl.BlockSpec(memory_space=pltpu.SMEM)
VMEM_SPEC = pl.BlockSpec(memory_space=pltpu.VMEM)


def params():
    return pltpu.CompilerParams(vmem_limit_bytes=VMEM_LIMIT)


def gelu(x):
    inner = 0.7978845608028654 * (x + 0.044715 * (x * x * x))
    return x * (0.5 * (1.0 + jnp.tanh(inner)))


def batch_weight(order_ref, batch_id, micro):
    weight = jnp.float32(0.0)
    for slot in range(micro):
        weight = jnp.where(order_ref[slot] == batch_id, jnp.float32(0.5 * 0.5 ** (micro - 1 - slot)), weight)
    return weight


def gram(left, right):
    return lax.dot_general(left, right, (((0,), (0,)), ((), ())), preferred_element_type=jnp.float32)


def iotas():
    row = lax.broadcasted_iota(jnp.int32, (BLK, BLK), 0)
    col = lax.broadcasted_iota(jnp.int32, (BLK, BLK), 1)
    return row, col


def packed_rows(pairs):
    return pairs * BLK + -(-pairs // 16) * 16


def hidden_kernel(micro, pairs, scale, order_ref, grad_ref, out_ref):
    row, col = iotas()
    weights = [batch_weight(order_ref, m, micro) for m in range(micro)]
    diagonals = []
    for pair in range(pairs):
        cols = slice(pair * 2 * BLK, (pair + 1) * 2 * BLK)
        parts = [grad_ref[0, m, :, cols] for m in range(micro)]
        plain = jnp.concatenate(parts, axis=0)
        scaled = jnp.concatenate(
            [(part.astype(jnp.float32) * weight).astype(jnp.bfloat16) for part, weight in zip(parts, weights)], axis=0
        )
        both = gram(scaled, plain) * scale
        first, second = both[:BLK, :BLK], both[BLK:, BLK:]
        out_ref[0, pair * BLK:(pair + 1) * BLK] = jnp.where(col >= row, first, second).astype(jnp.bfloat16)
        diagonals.append(jnp.sum(jnp.where(col == row, second, 0.0), axis=0, keepdims=True))
    rest = packed_rows(pairs) - pairs * BLK - pairs
    diagonals.append(jnp.zeros((rest, BLK), jnp.float32))
    out_ref[0, pairs * BLK:] = jnp.concatenate(diagonals, axis=0).astype(jnp.bfloat16)


def hidden_packed(order, hidden_grad, owners, scale):
    _, micro, rows, width = hidden_grad.shape
    own = width // owners
    pairs = own // (2 * BLK)
    return pl.pallas_call(
        functools.partial(hidden_kernel, micro, pairs, scale),
        grid=(owners,),
        out_shape=jax.ShapeDtypeStruct((owners, packed_rows(pairs), BLK), jnp.bfloat16),
        in_specs=[SMEM_SPEC, pl.BlockSpec((1, micro, rows, own), lambda i: (0, 0, 0, i))],
        out_specs=pl.BlockSpec((1, packed_rows(pairs), BLK), lambda i: (i, 0, 0)),
        compiler_params=params(),
        cost_estimate=pl.CostEstimate(flops=2 * micro * rows * width * 2 * BLK, bytes_accessed=6 << 20, transcendentals=0),
    )(order, hidden_grad)


def unpack_kernel(sources, pairs, in_ref, out_ref):
    row, col = iotas()
    tail = in_ref[0, pairs * BLK:].astype(jnp.float32)
    for source in range(1, sources):
        tail = tail + in_ref[source, pairs * BLK:].astype(jnp.float32)
    for pair in range(pairs):
        rows = slice(pair * BLK, (pair + 1) * BLK)
        total = in_ref[0, rows].astype(jnp.float32)
        for source in range(1, sources):
            total = total + in_ref[source, rows].astype(jnp.float32)
        turned = total.T
        out_ref[0, 2 * pair * BLK:(2 * pair + 1) * BLK] = jnp.where(col >= row, total, turned)
        second = jnp.where(col == row, tail[pair:pair + 1], turned)
        out_ref[0, (2 * pair + 1) * BLK:(2 * pair + 2) * BLK] = jnp.where(col < row, total, second)


def hidden_unpacked(packed, pairs):
    return pl.pallas_call(
        functools.partial(unpack_kernel, packed.shape[0], pairs),
        out_shape=jax.ShapeDtypeStruct((1, pairs * 2 * BLK, BLK), jnp.float32),
        in_specs=[VMEM_SPEC],
        out_specs=VMEM_SPEC,
        compiler_params=params(),
        cost_estimate=pl.CostEstimate(flops=4 << 20, bytes_accessed=3 << 20, transcendentals=0),
    )(packed)


def relay_kernel(sections, owners, chunk, in_ref, gain_ref, out_ref, held):
    rows, width = held.shape
    own = out_ref.shape[3]
    part = in_ref.shape[2]
    step = 512 if part % 512 == 0 else BLK

    def folded(value):
        return sum(value[:, i * BLK:(i + 1) * BLK] for i in range(value.shape[1] // BLK))

    def stats(total):
        center = jnp.sum(total, axis=-1, keepdims=True) * (1.0 / width)
        square = jnp.zeros((rows, BLK), jnp.float32)
        for at in range(0, width, step):
            square = square + folded(jnp.square(held[:, at:at + step] - center))
        spread = jnp.sum(square, axis=-1, keepdims=True) * (1.0 / width)
        return center, lax.rsqrt(spread + 1e-05)

    total = jnp.zeros((rows, BLK), jnp.float32)
    for source in range(sections):
        for at in range(0, part, step):
            value = in_ref[source, :, at:at + step].astype(jnp.float32)
            held[:, source * part + at:source * part + at + step] = value
            total = total + folded(value)

    def section(s, total):
        repeats = jnp.max(gain_ref[s, 0:1, width:width + BLK]).astype(jnp.int32)

        def apply(_, total):
            center, scale = stats(total)
            total = jnp.zeros((rows, BLK), jnp.float32)
            for at in range(0, width, step):
                value = held[:, at:at + step]
                normed = (value - center) * scale * gain_ref[s, 0:1, at:at + step]
                value = (value + gelu(normed)).astype(jnp.bfloat16).astype(jnp.float32)
                held[:, at:at + step] = value
                total = total + folded(value)
            return total

        total = lax.fori_loop(0, repeats + 1, apply, total)
        center, scale = stats(total)
        for owner in range(owners):
            cols = slice(owner * own, (owner + 1) * own)
            normed = (held[:, cols] - center) * scale * gain_ref[s, 0:1, cols]
            out_ref[owner, s] = normed.astype(jnp.bfloat16)
        return total

    lax.fori_loop(0, sections, section, total)


def relay(pieces, gains, owners):
    sections, rows, part = pieces.shape
    width = sections * part
    own = AWIN // owners
    return pl.pallas_call(
        functools.partial(relay_kernel, sections, owners, part),
        out_shape=jax.ShapeDtypeStruct((owners, sections, rows, own), jnp.bfloat16),
        in_specs=[VMEM_SPEC, VMEM_SPEC],
        out_specs=VMEM_SPEC,
        scratch_shapes=[pltpu.VMEM((rows, width), jnp.float32)],
        compiler_params=params(),
        cost_estimate=pl.CostEstimate(flops=40 * rows * width * 14, bytes_accessed=2 << 20, transcendentals=rows * width * 10),
    )(pieces, gains)


def feature_kernel(micro, blocks, scale, order_ref, in_ref, out_ref):
    weight = batch_weight(order_ref, lax.axis_index("section"), micro) * scale
    sources, sections = in_ref.shape[0], in_ref.shape[1]
    for s in range(sections):
        for block in range(blocks):
            cols = slice(block * BLK, (block + 1) * BLK)
            feats = jnp.concatenate([in_ref[source, s, :, cols] for source in range(sources)], axis=0)
            out_ref[s, cols] = (gram(feats, feats) * weight).astype(jnp.bfloat16)


def feature_terms(order, gathered, micro, scale):
    sources, sections, rows, own = gathered.shape
    return pl.pallas_call(
        functools.partial(feature_kernel, micro, own // BLK, scale),
        out_shape=jax.ShapeDtypeStruct((sections, own, BLK), jnp.bfloat16),
        in_specs=[SMEM_SPEC, VMEM_SPEC],
        out_specs=VMEM_SPEC,
        compiler_params=params(),
        cost_estimate=pl.CostEstimate(flops=2 * sources * sections * rows * own * BLK, bytes_accessed=2 << 20, transcendentals=0),
    )(order, gathered)


def fast_body(inputs, gain, repeats, order, hidden_grad):
    micro, tok_rows, _ = inputs.shape
    dp_count = lax.axis_size("dp")
    scale = 1.0 / (tok_rows * dp_count)
    told = jnp.concatenate([gain, jnp.broadcast_to(repeats.astype(jnp.float32)[:, None], (1, BLK))], axis=1)
    gains = lax.all_gather(told, "section", axis=0)
    pieces = lax.all_to_all(inputs, "section", 0, 0, tiled=True)
    packed = hidden_packed(order, hidden_grad, dp_count, scale)
    packed = lax.all_to_all(packed, "dp", 0, 0, tiled=True)
    feats = relay(pieces, gains, dp_count)
    feats = lax.all_to_all(feats, "dp", 0, 0, tiled=True)
    terms = feature_terms(order, feats, micro, scale)
    terms = lax.all_to_all(terms, "section", 0, 0, tiled=True)
    feature_rows = jnp.sum(terms.astype(jnp.float32), axis=0)
    hidden_rows = hidden_unpacked(packed, GWIN // dp_count // (2 * BLK))
    return (feature_rows[None], hidden_rows)


def normed(value, gain_row):
    center = jnp.mean(value, axis=-1, keepdims=True)
    spread = jnp.mean(jnp.square(value - center), axis=-1, keepdims=True)
    return (value - center) * lax.rsqrt(spread + 1e-05) * gain_row


def weighted_gram(feats, weights):
    shaped = feats.reshape(feats.shape[0], -1, BLK)
    scaled = shaped * weights[:, None, None].astype(shaped.dtype)
    return jnp.einsum("tbi,tbj->bij", scaled, shaped, preferred_element_type=jnp.float32)


def plain_body(inputs, gain, repeats, order, hidden_grad):
    micro, tok_rows, part = inputs.shape
    sections = lax.axis_size("section")
    total_tok = tok_rows * lax.axis_size("dp")
    slot_weight = 0.5 * jnp.power(0.5, micro - 1 - jnp.arange(micro, dtype=jnp.float32))
    hidden_weight = jnp.zeros((micro,), jnp.float32).at[order].set(slot_weight)
    row_weight = jnp.repeat(hidden_weight, tok_rows)
    hidden = weighted_gram(hidden_grad.reshape(micro * tok_rows, GWIN), row_weight) / total_tok
    gains = lax.all_gather(gain[0], "section", axis=0)
    counts = lax.all_gather(repeats[0], "section", axis=0)
    pieces = lax.all_to_all(inputs.reshape(micro * tok_rows, part), "section", 0, 1, tiled=True)

    def section(s, carry):
        value, feats = carry
        value = lax.fori_loop(
            0,
            counts[s] + 1,
            lambda i, v: (v + gelu(normed(v, gains[s]))).astype(jnp.bfloat16).astype(jnp.float32),
            value,
        )
        now = normed(value, gains[s]).astype(jnp.bfloat16)[:, :AWIN]
        return value, lax.dynamic_update_index_in_dim(feats, now, s, 0)

    start = jnp.zeros((sections, pieces.shape[0], AWIN), jnp.bfloat16)
    _, feats = lax.fori_loop(0, sections, section, (pieces.astype(jnp.float32), start))
    feats = lax.all_to_all(feats, "section", 0, 0, tiled=True).reshape(micro * tok_rows, AWIN)
    feature = weighted_gram(feats, row_weight) / total_tok

    def shared(term):
        term = term.reshape(-1, BLK).astype(jnp.bfloat16)
        return lax.psum_scatter(term, "dp", scatter_dimension=0, tiled=True).astype(jnp.float32)[None]

    return (shared(feature), shared(hidden))


def solution(mesh):
    sections, dp_count = mesh.shape["section"], mesh.shape["dp"]

    def body(inputs, gain, repeats, order, hidden_grad):
        aligned = (
            inputs.shape[0] == sections
            and inputs.shape[1] % 16 == 0
            and AWIN % (dp_count * BLK) == 0
            and GWIN % (dp_count * 2 * BLK) == 0
        )
        return (fast_body if aligned else plain_body)(inputs, gain, repeats, order, hidden_grad)

    placed = (
        P(None, "dp", "section"),
        P("section", None),
        P("section"),
        P(),
        P("section", None, "dp", None),
    )
    return jax.shard_map(
        body,
        mesh=mesh,
        in_specs=placed,
        out_specs=(P("section", "dp", None), P("section", "dp", None)),
        check_vma=False,
    )
```

time: 285 us -> 92.2 us (0.32)
  waiting for transfers between devices: 156 us -> 34 us
  other arithmetic: 36.8 us -> 0.72 us
  matrix products: 28.1 us -> 0 us
  Pallas kernels: 0 us -> 18.3 us
  blocking collectives: 0 us -> 17.5 us
  starting transfers between devices: 31.3 us -> 17.6 us
  between operations: 14.5 us -> 1.35 us
  local copies, waits for them, and re-layouts: 11.4 us -> 2.54 us
  loops' own time: 5.63 us -> 0 us
    psum x1 -> x0, waiting for transfers between devices: 49.6 us -> none  [body(): lax.psum(feature_term.astype(jnp.bfloat16), 'dp').astype(jnp.float32)]
    reduce_scatter x1 -> x0, waiting for transfers between devices: 47.3 us -> none  [body(): lax.psum_scatter(hidden_term.astype(jnp.bfloat16), 'dp', scatter_dimensio...]
    ppermute x7 -> x0, waiting for transfers between devices: 34.2 us -> none  [from_behind(): return lax.ppermute(shard, axis, pairs)]
    all_to_all x0 -> x4, waiting for transfers between devices: none -> 34 us  [the longest x1 19 us: fast_body(): packed = lax.all_to_all(packed, 'dp', 0, 0, tiled=True)]
    ppermute x7 -> x0, starting transfers between devices: 31.2 us -> none  [from_behind(): return lax.ppermute(shard, axis, pairs)]
    dot_general x12 -> x0, matrix products: 28.1 us -> none  [the longest x11 27.9 us: block_gram(): jnp.einsum('tbi,tbj->bij', shaped, shaped, preferred_element_type=jnp.flo...]
    all_gather x1 -> x0, waiting for transfers between devices: 24.5 us -> none  [body(): whole = lax.all_gather(inputs, 'section', axis=2, tiled=True)]
    pallas_call x0 -> x4, Pallas kernels: none -> 18.3 us  [the longest x1 9.31 us: relay(): pl.pallas_call(functools.partial(relay_kernel, sections, owners, part), o...]
  transfers between devices with their start and end apart: 10 -> 4, of which waited for: 10 -> 3; matrix products, arithmetic and copies ran while one was open for 12% -> 1% of each run, Pallas kernels for 0% -> 10%
where the time goes in v1:
time: 92.2 us; the launch traced here: 92 us
  waiting for transfers between devices  34 us (37%)
  Pallas kernels  18.3 us (20%)
  starting transfers between devices  17.6 us (19%)
  blocking collectives  17.5 us (19%)
  local copies, waits for them, and re-layouts  2.54 us (3%)
  between operations  1.35 us (1%)
    all_to_all x1, waiting for transfers between devices, fast_body(): packed = lax.all_to_all(packed, 'dp', 0, 0, tiled=True)  19 us
    all_gather x1, blocking collectives, fast_body(): gains = lax.all_gather(told, 'section', axis=0)  17.5 us
    pallas_call x1, Pallas kernels, relay(): pl.pallas_call(functools.partial(relay_kernel, sections, owners, part), o...  9.31 us
    all_to_all x1, waiting for transfers between devices, fast_body(): terms = lax.all_to_all(terms, 'section', 0, 0, tiled=True)  7.88 us
    all_to_all x1, waiting for transfers between devices, fast_body(): feats = lax.all_to_all(feats, 'dp', 0, 0, tiled=True)  7.07 us
    all_to_all x1, starting transfers between devices, fast_body(): pieces = lax.all_to_all(inputs, 'section', 0, 0, tiled=True)  6.33 us
    pallas_call x1, Pallas kernels, hidden_packed(): pl.pallas_call(functools.partial(hidden_kernel, micro, pairs, scale), gri...  5.52 us
    all_to_all x1, starting transfers between devices, fast_body(): feats = lax.all_to_all(feats, 'dp', 0, 0, tiled=True)  4.22 us
  transfers between devices with their start and end apart: 4, of which 3 were waited for; matrix products, arithmetic and copies ran while one was open for 1% of the time, Pallas kernels for 10%

profile of v1, /device:TPU:0, one launch (start us, length us, event | category | flops | bytes accessed | tf_op | source)
XLA Modules:
  0.0 92.0 jit_solution(12515378667970926104)
XLA Ops:
  0.6 6.3 %all-to-all-start = ((bf16[4,32,1536]{2,1,0:T(8,128)(2,1)}), bf16[4,32,1536]{2,1,0:T(8,128)(2,1)S(1)}, u32[]{:S(2)}, u32[]{:S(2)}) async-start(bf16[4,32,1536]{2,1,0:T(8,128)(2,1)} %param.5), calls=%async_computation | async-start | bytes 786432 | tf_op jit(solution)/shard_map/all_to_all | solution.py:203
  7.6 0.8 pad_bitcast_fusion
  8.4 17.5 %all-gather.1.gain_ref = f32[4,1,6272]{2,1,0:T(1,128)} all-gather(f32[1,1,6272]{2,1,0:T(1,128)S(1)} %pad_bitcast_fusion), channel_id=2, replica_groups=mesh['section'=4,'dp'=8] {'section'}, dimensions={0}, use_global_device_ids=true | all-gather | bytes 125440 | tf_op jit(solution)/shard_map/all_gather | solution.py:202
  25.9 0.0 all-to-all-done.in_ref
  25.9 0.0 copy-start.2
  25.9 0.9 copy-done.2
  26.8 0.0 copy-start
  26.8 0.0 copy-start.3
  26.8 9.3 %shard_map.68 = bf16[8,4,32,384]{3,2,1,0:T(8,128)(2,1)S(1)} custom-call(bf16[4,32,1536]{2,1,0:T(8,128)(2,1)S(1)} %all-to-all-done.in_ref, f32[4,1,6272]{2,1,0:T(1,128)S(1)} %copy-done.2), custom_call_target="tpu_custom_call" | custom-call | flops 110100480 | bytes 2097152 | tf_op jit(solution)/shard_map/pallas_call | solution.py:164
  36.1 0.0 copy-start.1
  36.1 0.9 copy-done.1
  37.0 4.2 %all-to-all-start.1 = ((bf16[8,4,32,384]{3,2,1,0:T(8,128)(2,1)}), bf16[8,4,32,384]{3,2,1,0:T(8,128)(2,1)}, u32[]{:S(2)}, u32[]{:S(2)}) async-start(bf16[8,4,32,384]{3,2,1,0:T(8,128)(2,1)} %copy-done.1), calls=%async_computation.1 | async-start | bytes 1572864 | tf_op jit(solution)/shard_map/all_to_all | solution.py:207
  41.2 0.0 copy-done
  41.2 0.0 copy-done.3
  41.2 5.5 %shard_map.70 = bf16[8,784,128]{2,1,0:T(8,128)(2,1)} custom-call(s32[4]{0:T(128)S(1)} %copy-done.3, bf16[1,4,32,12288]{3,2,1,0:T(8,128)(2,1)S(1)} %copy-done), custom_call_target="tpu_custom_call" | custom-call | flops 805306368 | bytes 6291456 | tf_op jit(solution)/shard_map/pallas_call | solution.py:73
  46.7 7.1 %all-to-all-done.1.in_ref = bf16[8,4,32,384]{3,2,1,0:T(8,128)(2,1)} async-done(((bf16[8,4,32,384]{3,2,1,0:T(8,128)(2,1)}), bf16[8,4,32,384]{3,2,1,0:T(8,128)(2,1)}, u32[]{:S(2)}, u32[]{:S(2)}) %all-to-all-start.1) | async-done | bytes 786464 | tf_op jit(solution)/shard_map/all_to_all | solution.py:207
  53.8 3.6 %all-to-all-start.3 = ((bf16[8,784,128]{2,1,0:T(8,128)(2,1)}), bf16[8,784,128]{2,1,0:T(8,128)(2,1)S(1)}, u32[]{:S(2)}, u32[]{:S(2)}) async-start(bf16[8,784,128]{2,1,0:T(8,128)(2,1)} %shard_map.70), calls=%async_computation.3 | async-start | bytes 3211264 | tf_op jit(solution)/shard_map/all_to_all | solution.py:205
  57.4 2.3 %shard_map.69 = bf16[4,384,128]{2,1,0:T(8,128)(2,1)} custom-call(s32[4]{0:T(128)S(1)} %copy-done.3, bf16[8,4,32,384]{3,2,1,0:T(8,128)(2,1)} %all-to-all-done.1.in_ref), custom_call_target="tpu_custom_call" | custom-call | flops 100663296 | bytes 2097152 | tf_op jit(solution)/shard_map/pallas_call | solution.py:187
  59.7 19.0 %all-to-all-done.3.in_ref = bf16[8,784,128]{2,1,0:T(8,128)(2,1)S(1)} async-done(((bf16[8,784,128]{2,1,0:T(8,128)(2,1)}), bf16[8,784,128]{2,1,0:T(8,128)(2,1)S(1)}, u32[]{:S(2)}, u32[]{:S(2)}) %all-to-all-start.3) | async-done | bytes 1605664 | tf_op jit(solution)/shard_map/all_to_all | solution.py:205
  78.7 3.5 %all-to-all-start.2 = ((bf16[4,384,128]{2,1,0:T(8,128)(2,1)}), bf16[4,384,128]{2,1,0:T(8,128)(2,1)S(1)}, u32[]{:S(2)}, u32[]{:S(2)}) async-start(bf16[4,384,128]{2,1,0:T(8,128)(2,1)} %shard_map.69), calls=%async_computation.2 | async-start | bytes 786432 | tf_op jit(solution)/shard_map/all_to_all | solution.py:209
  82.2 1.2 %shard_map.71 = f32[1,1536,128]{2,1,0:T(8,128)} custom-call(bf16[8,784,128]{2,1,0:T(8,128)(2,1)S(1)} %all-to-all-done.3.in_ref), custom_call_target="tpu_custom_call" | custom-call | flops 4194304 | bytes 3145728 | tf_op jit(solution)/shard_map/pallas_call | solution.py:101
  83.3 7.9 %all-to-all-done.2 = bf16[4,384,128]{2,1,0:T(8,128)(2,1)S(1)} async-done(((bf16[4,384,128]{2,1,0:T(8,128)(2,1)}), bf16[4,384,128]{2,1,0:T(8,128)(2,1)S(1)}, u32[]{:S(2)}, u32[]{:S(2)}) %all-to-all-start.2) | async-done | bytes 393248 | tf_op jit(solution)/shard_map/all_to_all | solution.py:209
  91.2 0.7 convert_reduce_fusion
Async XLA Ops:
  0.6 25.2 %all-to-all-start = ((bf16[4,32,1536]{2,1,0:T(8,128)(2,1)}), bf16[4,32,1536]{2,1,0:T(8,128)(2,1)S(1)}, u32[]{:S(2)}, u32[]{:S(2)}) async-start(bf16[4,32,1536]{2,1,0:T(8,128)(2,1)} %param.5), calls=%async_computation | async-start | bytes 786432 | tf_op jit(solution)/shard_map/all_to_all | solution.py:203
  25.9 0.9 copy-start.2
  26.8 14.4 %copy-start = (bf16[1,4,32,12288]{3,2,1,0:T(8,128)(2,1)S(1)}, bf16[1,4,32,12288]{3,2,1,0:T(8,128)(2,1)}, u32[]{:S(2)}) copy-start(bf16[1,4,32,12288]{3,2,1,0:T(8,128)(2,1)} %grad_ref.1) | copy-start | bytes 9437188
  26.8 14.4 %copy-start.3 = (s32[4]{0:T(128)S(1)}, s32[4]{0:T(128)}, u32[]{:S(2)}) copy-start(s32[4]{0:T(128)} %order_ref.3) | copy-start | bytes 52
  36.1 0.9 copy-start.1
  37.0 16.8 %all-to-all-start.1 = ((bf16[8,4,32,384]{3,2,1,0:T(8,128)(2,1)}), bf16[8,4,32,384]{3,2,1,0:T(8,128)(2,1)}, u32[]{:S(2)}, u32[]{:S(2)}) async-start(bf16[8,4,32,384]{3,2,1,0:T(8,128)(2,1)} %copy-done.1), calls=%async_computation.1 | async-start | bytes 1572864 | tf_op jit(solution)/shard_map/all_to_all | solution.py:207
  53.8 24.9 %all-to-all-start.3 = ((bf16[8,784,128]{2,1,0:T(8,128)(2,1)}), bf16[8,784,128]{2,1,0:T(8,128)(2,1)S(1)}, u32[]{:S(2)}, u32[]{:S(2)}) async-start(bf16[8,784,128]{2,1,0:T(8,128)(2,1)} %shard_map.70), calls=%async_computation.3 | async-start | bytes 3211264 | tf_op jit(solution)/shard_map/all_to_all | solution.py:205
  78.7 12.5 %all-to-all-start.2 = ((bf16[4,384,128]{2,1,0:T(8,128)(2,1)}), bf16[4,384,128]{2,1,0:T(8,128)(2,1)S(1)}, u32[]{:S(2)}, u32[]{:S(2)}) async-start(bf16[4,384,128]{2,1,0:T(8,128)(2,1)} %shard_map.69), calls=%async_computation.2 | async-start | bytes 786432 | tf_op jit(solution)/shard_map/all_to_all | solution.py:209

commit v2 on v1

--- a/solution.py
+++ b/solution.py
@@ -11,17 +11,18 @@
 GWIN = 12288
 BLK = 128
 VMEM_LIMIT = 48 * 1024 * 1024
+ROOT = 0.7978845608028654
 
 SMEM_SPEC = pl.BlockSpec(memory_space=pltpu.SMEM)
 VMEM_SPEC = pl.BlockSpec(memory_space=pltpu.VMEM)
 
 
-def params():
-    return pltpu.CompilerParams(vmem_limit_bytes=VMEM_LIMIT)
+def params(limit=VMEM_LIMIT):
+    return pltpu.CompilerParams(vmem_limit_bytes=limit)
 
 
 def gelu(x):
-    inner = 0.7978845608028654 * (x + 0.044715 * (x * x * x))
+    inner = ROOT * (x + 0.044715 * (x * x * x))
     return x * (0.5 * (1.0 + jnp.tanh(inner)))
 
 
@@ -76,7 +77,7 @@
         out_shape=jax.ShapeDtypeStruct((owners, packed_rows(pairs), BLK), jnp.bfloat16),
         in_specs=[SMEM_SPEC, pl.BlockSpec((1, micro, rows, own), lambda i: (0, 0, 0, i))],
         out_specs=pl.BlockSpec((1, packed_rows(pairs), BLK), lambda i: (i, 0, 0)),
-        compiler_params=params(),
+        compiler_params=params(60 * 1024 * 1024),
         cost_estimate=pl.CostEstimate(flops=2 * micro * rows * width * 2 * BLK, bytes_accessed=6 << 20, transcendentals=0),
     )(order, hidden_grad)
 
@@ -108,108 +109,144 @@
     )(packed)
 
 
-def relay_kernel(sections, owners, chunk, in_ref, gain_ref, out_ref, held):
-    rows, width = held.shape
-    own = out_ref.shape[3]
-    part = in_ref.shape[2]
-    step = 512 if part % 512 == 0 else BLK
-
-    def folded(value):
-        return sum(value[:, i * BLK:(i + 1) * BLK] for i in range(value.shape[1] // BLK))
-
-    def stats(total):
-        center = jnp.sum(total, axis=-1, keepdims=True) * (1.0 / width)
-        square = jnp.zeros((rows, BLK), jnp.float32)
-        for at in range(0, width, step):
-            square = square + folded(jnp.square(held[:, at:at + step] - center))
-        spread = jnp.sum(square, axis=-1, keepdims=True) * (1.0 / width)
-        return center, lax.rsqrt(spread + 1e-05)
-
-    total = jnp.zeros((rows, BLK), jnp.float32)
+def message_kernel(in_ref, gain_ref, repeats_ref, out_ref):
+    micro, rows, part = in_ref.shape
+    chunks, gain_rows = part // BLK, gain_ref.shape[0]
+    gain = gain_ref[...]
+    high = gain.astype(jnp.bfloat16)
+    low = (gain - high.astype(jnp.float32)).astype(jnp.bfloat16)
+    count = jnp.full((16, BLK), repeats_ref[0], jnp.int32).astype(jnp.float32).astype(jnp.bfloat16)
+    at = chunks * rows
+    for m in range(micro):
+        for chunk in range(chunks):
+            out_ref[m, chunk * rows:(chunk + 1) * rows] = in_ref[m, :, chunk * BLK:(chunk + 1) * BLK]
+        out_ref[m, at:at + gain_rows] = high
+        out_ref[m, at + gain_rows:at + 2 * gain_rows] = low
+        out_ref[m, at + 2 * gain_rows:] = count
+
+
+def messages(inputs, gain, repeats):
+    micro, rows, part = inputs.shape
+    gain_rows = gain.shape[1] // BLK
+    return pl.pallas_call(
+        message_kernel,
+        out_shape=jax.ShapeDtypeStruct((micro, part // BLK * rows + 2 * gain_rows + 16, BLK), jnp.bfloat16),
+        in_specs=[VMEM_SPEC, VMEM_SPEC, SMEM_SPEC],
+        out_specs=VMEM_SPEC,
+        compiler_params=params(),
+        cost_estimate=pl.CostEstimate(flops=1 << 20, bytes_accessed=1 << 20, transcendentals=0),
+    )(inputs, gain.reshape(gain_rows, BLK), repeats)
+
+
+def relay_kernel(sections, rows, owners, in_ref, out_ref, held, gains):
+    chunks, own = held.shape[0], out_ref.shape[3]
+    width = chunks * BLK
+    part = chunks // sections
+    at = part * rows
+    none = jnp.zeros((rows, BLK), jnp.float32)
+
+    def mean(total):
+        return jnp.sum(total, axis=-1, keepdims=True) * (1.0 / width)
+
+    total = none
     for source in range(sections):
-        for at in range(0, part, step):
-            value = in_ref[source, :, at:at + step].astype(jnp.float32)
-            held[:, source * part + at:source * part + at + step] = value
-            total = total + folded(value)
-
-    def section(s, total):
-        repeats = jnp.max(gain_ref[s, 0:1, width:width + BLK]).astype(jnp.int32)
-
-        def apply(_, total):
-            center, scale = stats(total)
-            total = jnp.zeros((rows, BLK), jnp.float32)
-            for at in range(0, width, step):
-                value = held[:, at:at + step]
-                normed = (value - center) * scale * gain_ref[s, 0:1, at:at + step]
-                value = (value + gelu(normed)).astype(jnp.bfloat16).astype(jnp.float32)
-                held[:, at:at + step] = value
-                total = total + folded(value)
-            return total
-
-        total = lax.fori_loop(0, repeats + 1, apply, total)
-        center, scale = stats(total)
-        for owner in range(owners):
-            cols = slice(owner * own, (owner + 1) * own)
-            normed = (held[:, cols] - center) * scale * gain_ref[s, 0:1, cols]
-            out_ref[owner, s] = normed.astype(jnp.bfloat16)
-        return total
-
-    lax.fori_loop(0, sections, section, total)
-
-
-def relay(pieces, gains, owners):
-    sections, rows, part = pieces.shape
-    width = sections * part
+        gains[source] = in_ref[source, at:at + chunks].astype(jnp.float32) + in_ref[
+            source, at + chunks:at + 2 * chunks
+        ].astype(jnp.float32)
+        for chunk in range(part):
+            value = in_ref[source, chunk * rows:(chunk + 1) * rows].astype(jnp.float32)
+            held[source * part + chunk] = value
+            total = total + value
+    center = mean(total)
+    square = none
+    for chunk in range(chunks):
+        square = square + jnp.square(held[chunk] - center)
+    start = (center, lax.rsqrt(mean(square) + 1e-05))
+
+    def section(s, carry):
+        repeats = jnp.max(in_ref[s, at + 2 * chunks:].astype(jnp.float32)).astype(jnp.int32)
+
+        def apply(_, carry):
+            center, scale = carry
+            half = 0.5 * scale
+            total, square = none, none
+            for chunk in range(chunks):
+                value = held[chunk]
+                y = (value - center) * half * gains[s, chunk:chunk + 1]
+                inner = y * (2.0 * ROOT + (8.0 * 0.044715 * ROOT) * (y * y))
+                value = (value + (y + y * jnp.tanh(inner))).astype(jnp.bfloat16).astype(jnp.float32)
+                held[chunk] = value
+                moved = value - center
+                total = total + moved
+                square = square + moved * moved
+            shift = mean(total)
+            spread = jnp.maximum(mean(square) - shift * shift, 0.0)
+            return center + shift, lax.rsqrt(spread + 1e-05)
+
+        carry = lax.fori_loop(0, repeats + 1, apply, carry)
+        center, scale = carry
+        for chunk in range(owners * own // BLK):
+            normed = (held[chunk] - center) * scale * gains[s, chunk:chunk + 1]
+            owner, col = chunk * BLK // own, chunk * BLK % own
+            out_ref[s, owner, :, col:col + BLK] = normed.astype(jnp.bfloat16)
+        return carry
+
+    lax.fori_loop(0, sections, section, start)
+
+
+def relay(pieces, rows, part, owners):
+    sections = pieces.shape[0]
+    chunks = sections * part // BLK
     own = AWIN // owners
     return pl.pallas_call(
-        functools.partial(relay_kernel, sections, owners, part),
-        out_shape=jax.ShapeDtypeStruct((owners, sections, rows, own), jnp.bfloat16),
-        in_specs=[VMEM_SPEC, VMEM_SPEC],
+        functools.partial(relay_kernel, sections, rows, owners),
+        out_shape=jax.ShapeDtypeStruct((sections, owners, rows, own), jnp.bfloat16),
+        in_specs=[VMEM_SPEC],
         out_specs=VMEM_SPEC,
-        scratch_shapes=[pltpu.VMEM((rows, width), jnp.float32)],
+        scratch_shapes=[pltpu.VMEM((chunks, rows, BLK), jnp.float32), pltpu.VMEM((sections, chunks, BLK), jnp.float32)],
         compiler_params=params(),
-        cost_estimate=pl.CostEstimate(flops=40 * rows * width * 14, bytes_accessed=2 << 20, transcendentals=rows * width * 10),
-    )(pieces, gains)
-
-
-def feature_kernel(micro, blocks, scale, order_ref, in_ref, out_ref):
-    weight = batch_weight(order_ref, lax.axis_index("section"), micro) * scale
-    sources, sections = in_ref.shape[0], in_ref.shape[1]
-    for s in range(sections):
-        for block in range(blocks):
-            cols = slice(block * BLK, (block + 1) * BLK)
-            feats = jnp.concatenate([in_ref[source, s, :, cols] for source in range(sources)], axis=0)
-            out_ref[s, cols] = (gram(feats, feats) * weight).astype(jnp.bfloat16)
-
-
-def feature_terms(order, gathered, micro, scale):
-    sources, sections, rows, own = gathered.shape
-    return pl.pallas_call(
-        functools.partial(feature_kernel, micro, own // BLK, scale),
-        out_shape=jax.ShapeDtypeStruct((sections, own, BLK), jnp.bfloat16),
+        cost_estimate=pl.CostEstimate(flops=1 << 34, bytes_accessed=2 << 20, transcendentals=0),
+    )(pieces)
+
+
+def feature_kernel(micro, scale, order_ref, in_ref, out_ref):
+    sources, rows, own = in_ref.shape
+    group = sources // micro
+    weights = [batch_weight(order_ref, m, micro) * scale for m in range(micro)]
+    for at in range(0, own, BLK):
+        total = jnp.zeros((BLK, BLK), jnp.float32)
+        for m in range(micro):
+            feats = in_ref[m * group:(m + 1) * group, :, at:at + BLK].reshape(group * rows, BLK)
+            total = total + gram(feats, feats) * weights[m]
+        out_ref[0, at:at + BLK] = total
+
+
+def feature_factor(order, gathered, micro, scale):
+    sources, rows, own = gathered.shape
+    return pl.pallas_call(
+        functools.partial(feature_kernel, micro, scale),
+        out_shape=jax.ShapeDtypeStruct((1, own, BLK), jnp.float32),
         in_specs=[SMEM_SPEC, VMEM_SPEC],
         out_specs=VMEM_SPEC,
         compiler_params=params(),
-        cost_estimate=pl.CostEstimate(flops=2 * sources * sections * rows * own * BLK, bytes_accessed=2 << 20, transcendentals=0),
+        cost_estimate=pl.CostEstimate(flops=2 * sources * rows * own * BLK, bytes_accessed=1 << 20, transcendentals=0),
     )(order, gathered)
 
 
 def fast_body(inputs, gain, repeats, order, hidden_grad):
-    micro, tok_rows, _ = inputs.shape
+    micro, tok_rows, part = inputs.shape
     dp_count = lax.axis_size("dp")
     scale = 1.0 / (tok_rows * dp_count)
-    told = jnp.concatenate([gain, jnp.broadcast_to(repeats.astype(jnp.float32)[:, None], (1, BLK))], axis=1)
-    gains = lax.all_gather(told, "section", axis=0)
-    pieces = lax.all_to_all(inputs, "section", 0, 0, tiled=True)
+    pieces = lax.all_to_all(messages(inputs, gain, repeats), "section", 0, 0, tiled=True)
     packed = hidden_packed(order, hidden_grad, dp_count, scale)
-    packed = lax.all_to_all(packed, "dp", 0, 0, tiled=True)
-    feats = relay(pieces, gains, dp_count)
-    feats = lax.all_to_all(feats, "dp", 0, 0, tiled=True)
-    terms = feature_terms(order, feats, micro, scale)
-    terms = lax.all_to_all(terms, "section", 0, 0, tiled=True)
-    feature_rows = jnp.sum(terms.astype(jnp.float32), axis=0)
-    hidden_rows = hidden_unpacked(packed, GWIN // dp_count // (2 * BLK))
-    return (feature_rows[None], hidden_rows)
+    pieces, _ = lax.optimization_barrier((pieces, packed))
+    packed = lax.psum_scatter(packed.reshape(-1, BLK), "dp", scatter_dimension=0, tiled=True)
+    feats = relay(pieces, tok_rows, part, dp_count)
+    feats = feats.reshape((-1,) + feats.shape[2:])
+    feats = lax.all_to_all(feats, ("section", "dp"), 0, 0, tiled=True)
+    feature_rows = feature_factor(order, feats, micro, scale)
+    hidden_rows = hidden_unpacked(packed[None], GWIN // dp_count // (2 * BLK))
+    return (feature_rows, hidden_rows)
 
 
 def normed(value, gain_row):
@@ -265,6 +302,7 @@
     def body(inputs, gain, repeats, order, hidden_grad):
         aligned = (
             inputs.shape[0] == sections
+            and inputs.shape[2] * sections % (16 * BLK) == 0
             and inputs.shape[1] % 16 == 0
             and AWIN % (dp_count * BLK) == 0
             and GWIN % (dp_count * 2 * BLK) == 0

time: 92.2 us -> 76.6 us (0.83)
  waiting for transfers between devices: 34 us -> 11.9 us
  between operations: 1.35 us -> 14.7 us
  starting transfers between devices: 17.6 us -> 6.32 us
  blocking collectives: 17.5 us -> 24.1 us
  Pallas kernels: 18.3 us -> 16 us
    all_to_all x4 -> x1, waiting for transfers between devices: 34 us -> 6.79 us  [fast_body(): lax.all_to_all(messages(inputs, gain, repeats), 'section', 0, 0, tiled=True)]
    all_to_all x0 -> x1, blocking collectives: none -> 24.1 us  [fast_body(): feats = lax.all_to_all(feats, ('section', 'dp'), 0, 0, tiled=True)]
    all_gather x1 -> x0, blocking collectives: 17.5 us -> none  [fast_body(): gains = lax.all_gather(told, 'section', axis=0)]
    all_to_all x4 -> x1, starting transfers between devices: 17.6 us -> 6.32 us  [fast_body(): lax.all_to_all(messages(inputs, gain, repeats), 'section', 0, 0, tiled=True)]
    reduce_scatter x0 -> x1, waiting for transfers between devices: none -> 5.05 us  [fast_body(): lax.psum_scatter(packed.reshape(-1, BLK), 'dp', scatter_dimension=0, tile...]
    pallas_call x2 -> x3, Pallas kernels: 11.6 us -> 7.64 us  [the longest x1 5.16 us: relay(): pl.pallas_call(functools.partial(relay_kernel, sections, rows, owners), o...]
    pallas_call x1, Pallas kernels: 5.52 us -> 7.31 us  [hidden_packed(): pl.pallas_call(functools.partial(hidden_kernel, micro, pairs, scale), gri...]
    unnamed x9 -> x8, local copies, waits for them, and re-layouts: 2.54 us -> 2.66 us
  transfers between devices with their start and end apart: 4 -> 2, of which waited for: 3 -> 2; matrix products, arithmetic and copies ran while one was open for 1% -> 0% of each run, Pallas kernels for 10% -> 19%
where the time goes in v2:
time: 76.6 us; the launch traced here: 75.6 us
  blocking collectives  24.1 us (31%)
  Pallas kernels  16 us (21%)
  between operations  14.7 us (19%)
  waiting for transfers between devices  11.9 us (16%)
  starting transfers between devices  6.32 us (8%)
  local copies, waits for them, and re-layouts  2.66 us (3%)
    all_to_all x1, blocking collectives, fast_body(): feats = lax.all_to_all(feats, ('section', 'dp'), 0, 0, tiled=True)  24.1 us
    pallas_call x1, Pallas kernels, hidden_packed(): pl.pallas_call(functools.partial(hidden_kernel, micro, pairs, scale), gri...  7.31 us
    all_to_all x1, waiting for transfers between devices, fast_body(): lax.all_to_all(messages(inputs, gain, repeats), 'section', 0, 0, tiled=True)  6.79 us
    all_to_all x1, starting transfers between devices, fast_body(): lax.all_to_all(messages(inputs, gain, repeats), 'section', 0, 0, tiled=True)  6.32 us
    pallas_call x1, Pallas kernels, relay(): pl.pallas_call(functools.partial(relay_kernel, sections, rows, owners), o...  5.16 us
    reduce_scatter x1, waiting for transfers between devices, fast_body(): lax.psum_scatter(packed.reshape(-1, BLK), 'dp', scatter_dimension=0, tile...  5.05 us
    unnamed x8, local copies, waits for them, and re-layouts  2.66 us
    pallas_call x1, Pallas kernels, feature_factor(): pl.pallas_call(functools.partial(feature_kernel, micro, scale), out_shape...  1.63 us
  transfers between devices with their start and end apart: 2, of which 2 were waited for; matrix products, arithmetic and copies ran while one was open for 0% of the time, Pallas kernels for 19%

profile of v2, /device:TPU:0, one launch (start us, length us, event | category | flops | bytes accessed | tf_op | source)
XLA Modules:
  0.0 75.6 jit_solution(2263524198991350108)
XLA Ops:
  7.8 0.0 copy-start
  7.8 1.0 %copy-done = bf16[4,32,1536]{2,1,0:T(8,128)(2,1)S(1)} copy-done((bf16[4,32,1536]{2,1,0:T(8,128)(2,1)S(1)}, bf16[4,32,1536]{2,1,0:T(8,128)(2,1)}, u32[]{:S(2)}) %copy-start) | copy-done | bytes 393240
  8.8 0.0 copy-start.2
  8.8 0.7 copy-done.2
  9.5 0.9 %shard_map.68 = bf16[4,496,128]{2,1,0:T(8,128)(2,1)} custom-call(bf16[4,32,1536]{2,1,0:T(8,128)(2,1)S(1)} %copy-done, f32[48,128]{1,0:T(8,128)S(1)} %bitcast.6, s32[1]{0:T(128)S(6)} %copy.7.repeats_ref), custom_call_target="tpu_custom_call" | custom-call | flops 1048576 | bytes 1048576 | tf_op jit(solution)/shard_map/pallas_call | solution.py:131
  10.4 6.3 %all-to-all-start = ((bf16[4,496,128]{2,1,0:T(8,128)(2,1)}), bf16[4,496,128]{2,1,0:T(8,128)(2,1)S(1)}, u32[]{:S(2)}, u32[]{:S(2)}) async-start(bf16[4,496,128]{2,1,0:T(8,128)(2,1)} %shard_map.68), calls=%async_computation | async-start | bytes 1015808 | tf_op jit(solution)/shard_map/all_to_all | solution.py:240
  16.7 0.0 reduce-scatter.2.cloned.1.call-start
  16.7 7.3 %shard_map.69 = bf16[8,784,128]{2,1,0:T(8,128)(2,1)} custom-call(s32[4]{0:T(128)} %order_ref.3, bf16[1,4,32,12288]{3,2,1,0:T(8,128)(2,1)} %grad_ref.1), custom_call_target="tpu_custom_call" | custom-call | flops 805306368 | bytes 6291456 | tf_op jit(solution)/shard_map/pallas_call | solution.py:74
  24.0 0.0 reduce-scatter.2.cloned.1.call-update
  24.1 0.0 copy-start.3
  24.1 6.8 %all-to-all-done.in_ref = bf16[4,496,128]{2,1,0:T(8,128)(2,1)S(1)} async-done(((bf16[4,496,128]{2,1,0:T(8,128)(2,1)}), bf16[4,496,128]{2,1,0:T(8,128)(2,1)S(1)}, u32[]{:S(2)}, u32[]{:S(2)}) %all-to-all-start) | async-done | bytes 507936 | tf_op jit(solution)/shard_map/all_to_all | solution.py:240
  30.9 5.2 %shard_map.70 = bf16[4,8,32,384]{3,2,1,0:T(8,128)(2,1)S(1)} custom-call(bf16[4,496,128]{2,1,0:T(8,128)(2,1)S(1)} %all-to-all-done.in_ref), custom_call_target="tpu_custom_call" | custom-call | flops 17179869184 | bytes 2097152 | tf_op jit(solution)/shard_map/pallas_call | solution.py:201
  36.0 24.1 %all_to_all.10.in_ref = bf16[32,32,384]{2,1,0:T(8,128)(2,1)S(1)} all-to-all(bf16[32,32,384]{2,1,0:T(8,128)(2,1)S(1)} %bitcast.4), channel_id=1, replica_groups=mesh['section'=4,'dp'=8] {'section','dp'}, dimensions={0} | all-to-all | bytes 1572864 | tf_op jit(solution)/shard_map/all_to_all | solution.py:246
  60.2 0.0 copy-done.3
  60.2 1.6 %shard_map.71 = f32[1,384,128]{2,1,0:T(8,128)} custom-call(s32[4]{0:T(128)S(1)} %copy-done.3, bf16[32,32,384]{2,1,0:T(8,128)(2,1)S(1)} %all_to_all.10.in_ref), custom_call_target="tpu_custom_call" | custom-call | flops 100663296 | bytes 1048576 | tf_op jit(solution)/shard_map/pallas_call | solution.py:226
  61.8 5.0 %reduce-scatter.2.cloned.1.call-done = bf16[784,128]{1,0:T(8,128)(2,1)} async-done(((bf16[6272,128]{1,0:T(8,128)(2,1)}), bf16[784,128]{1,0:T(8,128)(2,1)}) %reduce-scatter.2.cloned.1.call-update) | async-done | bytes 200720 | tf_op jit(solution)/shard_map/reduce_scatter | solution.py:243
  66.8 0.0 copy-start.1
  66.8 0.9 %copy-done.1 = bf16[784,128]{1,0:T(8,128)(2,1)S(1)} copy-done((bf16[784,128]{1,0:T(8,128)(2,1)S(1)}, bf16[784,128]{1,0:T(8,128)(2,1)}, u32[]{:S(2)}) %copy-start.1) | copy-done | bytes 200728
  67.8 1.0 %shard_map.72 = f32[1,1536,128]{2,1,0:T(8,128)} custom-call(bf16[1,784,128]{2,1,0:T(8,128)(2,1)S(1)} %bitcast.5), custom_call_target="tpu_custom_call" | custom-call | flops 4194304 | bytes 3145728 | tf_op jit(solution)/shard_map/pallas_call | solution.py:102
Async XLA Ops:
  7.8 1.0 %copy-start = (bf16[4,32,1536]{2,1,0:T(8,128)(2,1)S(1)}, bf16[4,32,1536]{2,1,0:T(8,128)(2,1)}, u32[]{:S(2)}) copy-start(bf16[4,32,1536]{2,1,0:T(8,128)(2,1)} %in_ref.1) | copy-start | bytes 1179652
  8.8 0.7 copy-start.2
  10.4 20.5 %all-to-all-start = ((bf16[4,496,128]{2,1,0:T(8,128)(2,1)}), bf16[4,496,128]{2,1,0:T(8,128)(2,1)S(1)}, u32[]{:S(2)}, u32[]{:S(2)}) async-start(bf16[4,496,128]{2,1,0:T(8,128)(2,1)} %shard_map.68), calls=%async_computation | async-start | bytes 1015808 | tf_op jit(solution)/shard_map/all_to_all | solution.py:240
  16.7 50.1 %reduce-scatter.2.cloned.1.call-start = ((), (), s32[]{:S(2)}) async-start(), calls=%async_computation.3 | async-start | bytes 1806336 | tf_op jit(solution)/shard_map/reduce_scatter | solution.py:243
  24.1 36.1 %copy-start.3 = (s32[4]{0:T(128)S(1)}, s32[4]{0:T(128)}, u32[]{:S(2)}) copy-start(s32[4]{0:T(128)} %order_ref.3) | copy-start | bytes 52
  66.8 0.9 %copy-start.1 = (bf16[784,128]{1,0:T(8,128)(2,1)S(1)}, bf16[784,128]{1,0:T(8,128)(2,1)}, u32[]{:S(2)}) copy-start(bf16[784,128]{1,0:T(8,128)(2,1)} %reduce-scatter.2.cloned.1.call-done) | copy-start | bytes 602116
Sparse Core Ops, SparseCore 0:
  24.2 42.6 reduce-scatter.1

commit v3 on v2

--- a/solution.py
+++ b/solution.py
@@ -10,7 +10,7 @@
 AWIN = 3072
 GWIN = 12288
 BLK = 128
-VMEM_LIMIT = 48 * 1024 * 1024
+VMEM_LIMIT = 16 * 1024 * 1024
 ROOT = 0.7978845608028654
 
 SMEM_SPEC = pl.BlockSpec(memory_space=pltpu.SMEM)
@@ -47,66 +47,85 @@
     return pairs * BLK + -(-pairs // 16) * 16
 
 
-def hidden_kernel(micro, pairs, scale, order_ref, grad_ref, out_ref):
+def hidden_kernel(micro, pairs, scale, order_ref, _, grad_ref, *refs):
+    received, out_ref = refs[:-1], refs[-1]
     row, col = iotas()
     weights = [batch_weight(order_ref, m, micro) for m in range(micro)]
-    diagonals = []
+    tail = jnp.zeros((packed_rows(pairs) - pairs * BLK, BLK), jnp.float32)
+    tail_row = lax.broadcasted_iota(jnp.int32, tail.shape, 0)
     for pair in range(pairs):
-        cols = slice(pair * 2 * BLK, (pair + 1) * 2 * BLK)
-        parts = [grad_ref[0, m, :, cols] for m in range(micro)]
-        plain = jnp.concatenate(parts, axis=0)
-        scaled = jnp.concatenate(
-            [(part.astype(jnp.float32) * weight).astype(jnp.bfloat16) for part, weight in zip(parts, weights)], axis=0
-        )
-        both = gram(scaled, plain) * scale
-        first, second = both[:BLK, :BLK], both[BLK:, BLK:]
-        out_ref[0, pair * BLK:(pair + 1) * BLK] = jnp.where(col >= row, first, second).astype(jnp.bfloat16)
-        diagonals.append(jnp.sum(jnp.where(col == row, second, 0.0), axis=0, keepdims=True))
-    rest = packed_rows(pairs) - pairs * BLK - pairs
-    diagonals.append(jnp.zeros((rest, BLK), jnp.float32))
-    out_ref[0, pairs * BLK:] = jnp.concatenate(diagonals, axis=0).astype(jnp.bfloat16)
-
-
-def hidden_packed(order, hidden_grad, owners, scale):
+        both = []
+        for at in (pair * 2 * BLK, pair * 2 * BLK + BLK):
+            parts = [grad_ref[0, m, :, at:at + BLK] for m in range(micro)]
+            scaled = [(part.astype(jnp.float32) * weight).astype(jnp.bfloat16) for part, weight in zip(parts, weights)]
+            both.append(gram(jnp.concatenate(scaled, axis=0), jnp.concatenate(parts, axis=0)) * scale)
+        first, second = both
+        rows = slice(pair * BLK, (pair + 1) * BLK)
+        packed = jnp.where(col >= row, first, second)
+        for ref in received:
+            packed = packed + ref[0, rows].astype(jnp.float32)
+        out_ref[0, rows] = packed.astype(jnp.bfloat16)
+        diagonal = jnp.sum(jnp.where(col == row, second, 0.0), axis=0, keepdims=True)
+        tail = jnp.where(tail_row == pair, diagonal, tail)
+    for ref in received:
+        tail = tail + ref[0, pairs * BLK:].astype(jnp.float32)
+    out_ref[0, pairs * BLK:] = tail.astype(jnp.bfloat16)
+
+
+def hidden_terms(order, hidden_grad, me, flip, dp_count, scale, received=()):
     _, micro, rows, width = hidden_grad.shape
-    own = width // owners
+    own = width // dp_count
     pairs = own // (2 * BLK)
+    high = packed_rows(pairs)
+    packed_spec = pl.BlockSpec((1, high, BLK), lambda i, order, me: (i, 0, 0))
+
+    def owner(i, order, me):
+        return 0, 0, 0, jnp.bitwise_xor(me[0], flip + 4 - 4 * i)
+
     return pl.pallas_call(
         functools.partial(hidden_kernel, micro, pairs, scale),
-        grid=(owners,),
-        out_shape=jax.ShapeDtypeStruct((owners, packed_rows(pairs), BLK), jnp.bfloat16),
-        in_specs=[SMEM_SPEC, pl.BlockSpec((1, micro, rows, own), lambda i: (0, 0, 0, i))],
-        out_specs=pl.BlockSpec((1, packed_rows(pairs), BLK), lambda i: (i, 0, 0)),
+        out_shape=jax.ShapeDtypeStruct((2, high, BLK), jnp.bfloat16),
+        grid_spec=pltpu.PrefetchScalarGridSpec(
+            num_scalar_prefetch=2,
+            grid=(2,),
+            in_specs=[pl.BlockSpec((1, micro, rows, own), owner)] + [packed_spec] * len(received),
+            out_specs=packed_spec,
+        ),
         compiler_params=params(60 * 1024 * 1024),
-        cost_estimate=pl.CostEstimate(flops=2 * micro * rows * width * 2 * BLK, bytes_accessed=6 << 20, transcendentals=0),
-    )(order, hidden_grad)
-
-
-def unpack_kernel(sources, pairs, in_ref, out_ref):
+        cost_estimate=pl.CostEstimate(flops=1 << 20, bytes_accessed=1 << 10, transcendentals=0),
+    )(order, me, hidden_grad, *received)
+
+
+def unpack_kernel(pairs, own_ref, received_ref, out_ref):
     row, col = iotas()
-    tail = in_ref[0, pairs * BLK:].astype(jnp.float32)
-    for source in range(1, sources):
-        tail = tail + in_ref[source, pairs * BLK:].astype(jnp.float32)
+
+    def total(rows):
+        return own_ref[0, rows].astype(jnp.float32) + received_ref[0, rows].astype(jnp.float32)
+
+    tail = total(slice(pairs * BLK, None))
     for pair in range(pairs):
-        rows = slice(pair * BLK, (pair + 1) * BLK)
-        total = in_ref[0, rows].astype(jnp.float32)
-        for source in range(1, sources):
-            total = total + in_ref[source, rows].astype(jnp.float32)
-        turned = total.T
-        out_ref[0, 2 * pair * BLK:(2 * pair + 1) * BLK] = jnp.where(col >= row, total, turned)
+        value = total(slice(pair * BLK, (pair + 1) * BLK))
+        turned = value.T
+        out_ref[0, 2 * pair * BLK:(2 * pair + 1) * BLK] = jnp.where(col >= row, value, turned)
         second = jnp.where(col == row, tail[pair:pair + 1], turned)
-        out_ref[0, (2 * pair + 1) * BLK:(2 * pair + 2) * BLK] = jnp.where(col < row, total, second)
-
-
-def hidden_unpacked(packed, pairs):
-    return pl.pallas_call(
-        functools.partial(unpack_kernel, packed.shape[0], pairs),
+        out_ref[0, (2 * pair + 1) * BLK:(2 * pair + 2) * BLK] = jnp.where(col < row, value, second)
+
+
+def unpacked(both, received, pairs):
+    high = packed_rows(pairs)
+    return pl.pallas_call(
+        functools.partial(unpack_kernel, pairs),
+        grid=(1,),
         out_shape=jax.ShapeDtypeStruct((1, pairs * 2 * BLK, BLK), jnp.float32),
-        in_specs=[VMEM_SPEC],
-        out_specs=VMEM_SPEC,
+        in_specs=[pl.BlockSpec((1, high, BLK), lambda i: (1, 0, 0)), pl.BlockSpec((1, high, BLK), lambda i: (0, 0, 0))],
+        out_specs=pl.BlockSpec((1, pairs * 2 * BLK, BLK), lambda i: (0, 0, 0)),
         compiler_params=params(),
-        cost_estimate=pl.CostEstimate(flops=4 << 20, bytes_accessed=3 << 20, transcendentals=0),
-    )(packed)
+        cost_estimate=pl.CostEstimate(flops=1 << 20, bytes_accessed=1 << 10, transcendentals=0),
+    )(both, received)
+
+
+def swapped(shard, mask):
+    return lax.ppermute(shard, "dp", [(i, i ^ mask) for i in range(lax.axis_size("dp"))])
 
 
 def message_kernel(in_ref, gain_ref, repeats_ref, out_ref):
@@ -133,7 +152,7 @@
         out_shape=jax.ShapeDtypeStruct((micro, part // BLK * rows + 2 * gain_rows + 16, BLK), jnp.bfloat16),
         in_specs=[VMEM_SPEC, VMEM_SPEC, SMEM_SPEC],
         out_specs=VMEM_SPEC,
-        compiler_params=params(),
+        compiler_params=params(60 * 1024 * 1024),
         cost_estimate=pl.CostEstimate(flops=1 << 20, bytes_accessed=1 << 20, transcendentals=0),
     )(inputs, gain.reshape(gain_rows, BLK), repeats)
 
@@ -205,7 +224,7 @@
         out_specs=VMEM_SPEC,
         scratch_shapes=[pltpu.VMEM((chunks, rows, BLK), jnp.float32), pltpu.VMEM((sections, chunks, BLK), jnp.float32)],
         compiler_params=params(),
-        cost_estimate=pl.CostEstimate(flops=1 << 34, bytes_accessed=2 << 20, transcendentals=0),
+        cost_estimate=pl.CostEstimate(flops=1 << 33, bytes_accessed=2 << 20, transcendentals=0),
     )(pieces)
 
 
@@ -237,15 +256,20 @@
     micro, tok_rows, part = inputs.shape
     dp_count = lax.axis_size("dp")
     scale = 1.0 / (tok_rows * dp_count)
-    pieces = lax.all_to_all(messages(inputs, gain, repeats), "section", 0, 0, tiled=True)
-    packed = hidden_packed(order, hidden_grad, dp_count, scale)
-    pieces, _ = lax.optimization_barrier((pieces, packed))
-    packed = lax.psum_scatter(packed.reshape(-1, BLK), "dp", scatter_dimension=0, tiled=True)
-    feats = relay(pieces, tok_rows, part, dp_count)
+    told, order = lax.optimization_barrier((messages(inputs, gain, repeats), order))
+    pieces = lax.all_to_all(told, "section", 0, 0, tiled=True)
+
+    me = lax.axis_index("dp").reshape(1)
+    terms = functools.partial(hidden_terms, hidden_grad=hidden_grad, dp_count=dp_count, scale=scale)
+    sent = terms(order, me=me, flip=2, received=(swapped(terms(order, me=me, flip=3), 1),))
+    came = swapped(sent, 2)
+    pieces, _ = lax.optimization_barrier((pieces, sent))
+    feats, came, order = lax.optimization_barrier((relay(pieces, tok_rows, part, dp_count), came, order))
     feats = feats.reshape((-1,) + feats.shape[2:])
     feats = lax.all_to_all(feats, ("section", "dp"), 0, 0, tiled=True)
+    both = terms(order, me=me, flip=0, received=(swapped(terms(order, me=me, flip=1), 1), came))
+    hidden_rows = unpacked(both, swapped(both[:1], 4), GWIN // dp_count // (2 * BLK))
     feature_rows = feature_factor(order, feats, micro, scale)
-    hidden_rows = hidden_unpacked(packed[None], GWIN // dp_count // (2 * BLK))
     return (feature_rows, hidden_rows)
 
 
@@ -304,6 +328,7 @@
             inputs.shape[0] == sections
             and inputs.shape[2] * sections % (16 * BLK) == 0
             and inputs.shape[1] % 16 == 0
+            and dp_count == 8
             and AWIN % (dp_count * BLK) == 0
             and GWIN % (dp_count * 2 * BLK) == 0
         )

time: 76.6 us -> 59 us (0.77)
  blocking collectives: 24.1 us -> 0 us
  between operations: 14.7 us -> 1.3 us
  Pallas kernels: 16 us -> 25.9 us
  starting transfers between devices: 6.32 us -> 13.6 us
  waiting for transfers between devices: 11.9 us -> 14.4 us
  local copies, waits for them, and re-layouts: 2.66 us -> 3.45 us
    all_to_all x1 -> x0, blocking collectives: 24.1 us -> none  [fast_body(): feats = lax.all_to_all(feats, ('section', 'dp'), 0, 0, tiled=True)]
    ppermute x0 -> x4, waiting for transfers between devices: none -> 10.6 us  [swapped(): lax.ppermute(shard, 'dp', [(i, i ^ mask) for i in range(lax.axis_size('dp...]
    pallas_call x2 -> x5, Pallas kernels: 8.34 us -> 13.5 us  [the longest x4 12.5 us: hidden_terms(): pl.pallas_call(functools.partial(hidden_kernel, micro, pairs, scale), out...]
    reduce_scatter x1 -> x0, waiting for transfers between devices: 5.05 us -> none  [fast_body(): lax.psum_scatter(packed.reshape(-1, BLK), 'dp', scatter_dimension=0, tile...]
    pallas_call x1, Pallas kernels: 5.16 us -> 8.92 us  [relay(): pl.pallas_call(functools.partial(relay_kernel, sections, rows, owners), o...]
    all_to_all x1 -> x2, starting transfers between devices: 6.32 us -> 10 us  [the longest x1 6.32 us: fast_body(): pieces = lax.all_to_all(told, 'section', 0, 0, tiled=True)]
    ppermute x0 -> x4, starting transfers between devices: none -> 3.58 us  [swapped(): lax.ppermute(shard, 'dp', [(i, i ^ mask) for i in range(lax.axis_size('dp...]
    all_to_all x1 -> x2, waiting for transfers between devices: 6.79 us -> 3.81 us  [the longest x1 3.81 us: fast_body(): pieces = lax.all_to_all(told, 'section', 0, 0, tiled=True)]
  transfers between devices with their start and end apart: 2 -> 6, of which waited for: 2 -> 4; matrix products, arithmetic and copies ran while one was open for 0% -> 2% of each run, Pallas kernels for 19% -> 38%
where the time goes in v3:
time: 59 us; the launch traced here: 58.7 us
  Pallas kernels  25.9 us (44%)
  waiting for transfers between devices  14.4 us (24%)
  starting transfers between devices  13.6 us (23%)
  local copies, waits for them, and re-layouts  3.45 us (6%)
  between operations  1.3 us (2%)
    pallas_call x4, Pallas kernels, hidden_terms(): pl.pallas_call(functools.partial(hidden_kernel, micro, pairs, scale), out...  12.5 us
    ppermute x4, waiting for transfers between devices, swapped(): lax.ppermute(shard, 'dp', [(i, i ^ mask) for i in range(lax.axis_size('dp...  10.6 us
    pallas_call x1, Pallas kernels, relay(): pl.pallas_call(functools.partial(relay_kernel, sections, rows, owners), o...  8.92 us
    all_to_all x1, starting transfers between devices, fast_body(): pieces = lax.all_to_all(told, 'section', 0, 0, tiled=True)  6.32 us
    all_to_all x1, waiting for transfers between devices, fast_body(): pieces = lax.all_to_all(told, 'section', 0, 0, tiled=True)  3.81 us
    all_to_all x1, starting transfers between devices, fast_body(): feats = lax.all_to_all(feats, ('section', 'dp'), 0, 0, tiled=True)  3.71 us
    ppermute x4, starting transfers between devices, swapped(): lax.ppermute(shard, 'dp', [(i, i ^ mask) for i in range(lax.axis_size('dp...  3.58 us
    unnamed x10, local copies, waits for them, and re-layouts  2.5 us
  transfers between devices with their start and end apart: 6, of which 4 were waited for; matrix products, arithmetic and copies ran while one was open for 2% of the time, Pallas kernels for 38%

profile of v3, /device:TPU:0, one launch (start us, length us, event | category | flops | bytes accessed | tf_op | source)
XLA Modules:
  0.0 58.7 jit_solution(8728124351356656167)
XLA Ops:
  1.3 1.9 %shard_map.68 = bf16[4,496,128]{2,1,0:T(8,128)(2,1)} custom-call(bf16[4,32,1536]{2,1,0:T(8,128)(2,1)} %in_ref.1, f32[48,128]{1,0:T(8,128)} %bitcast.3, s32[1]{0:T(128)S(6)} %copy.7.repeats_ref), custom_call_target="tpu_custom_call" | custom-call | flops 1048576 | bytes 1048576 | tf_op jit(solution)/shard_map/pallas_call | solution.py:150
  3.1 6.3 %all-to-all-start = ((bf16[4,496,128]{2,1,0:T(8,128)(2,1)}), bf16[4,496,128]{2,1,0:T(8,128)(2,1)S(1)}, u32[]{:S(2)}, u32[]{:S(2)}) async-start(bf16[4,496,128]{2,1,0:T(8,128)(2,1)} %shard_map.68), calls=%async_computation | async-start | bytes 1015808 | tf_op jit(solution)/shard_map/all_to_all | solution.py:260
  9.4 3.0 %shard_map.69 = bf16[2,784,128]{2,1,0:T(8,128)(2,1)} custom-call(s32[4]{0:T(128)} %order_ref.4, s32[1]{0:T(128)} %bitcast.1._, bf16[1,4,32,12288]{3,2,1,0:T(8,128)(2,1)} %grad_ref.7), custom_call_target="tpu_custom_call" | custom-call | flops 1048576 | bytes 1024 | tf_op jit(solution)/shard_map/pallas_call | solution.py:85
  12.5 0.0 collective-permute-start
  12.5 1.9 %collective-permute-done.refs_0_ = bf16[2,784,128]{2,1,0:T(8,128)(2,1)S(1)} collective-permute-done((bf16[2,784,128]{2,1,0:T(8,128)(2,1)}, bf16[2,784,128]{2,1,0:T(8,128)(2,1)S(1)}, u32[]{:S(2)}, u32[]{:S(2)}) %collective-permute-start) | collective-permute-done | bytes 401440 | tf_op jit(solution)/shard_map/ppermute | solution.py:128
  14.4 0.0 copy-start.4
  14.4 0.7 %copy-done.4 = bf16[2,784,128]{2,1,0:T(8,128)(2,1)} copy-done((bf16[2,784,128]{2,1,0:T(8,128)(2,1)}, bf16[2,784,128]{2,1,0:T(8,128)(2,1)S(1)}, u32[]{:S(2)}) %copy-start.4) | copy-done | bytes 401432
  15.2 3.1 %shard_map.70 = bf16[2,784,128]{2,1,0:T(8,128)(2,1)} custom-call(s32[4]{0:T(128)} %order_ref.4, s32[1]{0:T(128)} %bitcast.1._, bf16[1,4,32,12288]{3,2,1,0:T(8,128)(2,1)} %grad_ref.7, bf16[2,784,128]{2,1,0:T(8,128)(2,1)} %copy-done.4), custom_call_target="tpu_custom_call" | custom-call | flops 1048576 | bytes 1024 | tf_op jit(solution)/shard_map/pallas_call | solution.py:85
  18.3 1.5 %collective-permute-start.1 = (bf16[2,784,128]{2,1,0:T(8,128)(2,1)}, bf16[2,784,128]{2,1,0:T(8,128)(2,1)S(1)}, u32[]{:S(2)}, u32[]{:S(2)}) collective-permute-start(bf16[2,784,128]{2,1,0:T(8,128)(2,1)} %shard_map.70), channel_id=1, source_target_pairs={{0,2},{1,3},{2,0},{3,1},{4,6},{5,7},{6,4},{7,5},{8,10},{9,11},{10,... | collective-permute-start | bytes 1204232 | tf_op jit(solution)/shard_map/ppermute | solution.py:128
  19.8 3.8 %all-to-all-done.in_ref = bf16[4,496,128]{2,1,0:T(8,128)(2,1)S(1)} async-done(((bf16[4,496,128]{2,1,0:T(8,128)(2,1)}), bf16[4,496,128]{2,1,0:T(8,128)(2,1)S(1)}, u32[]{:S(2)}, u32[]{:S(2)}) %all-to-all-start) | async-done | bytes 507936 | tf_op jit(solution)/shard_map/all_to_all | solution.py:260
  23.6 8.9 %shard_map.71 = bf16[4,8,32,384]{3,2,1,0:T(8,128)(2,1)} custom-call(bf16[4,496,128]{2,1,0:T(8,128)(2,1)S(1)} %all-to-all-done.in_ref), custom_call_target="tpu_custom_call" | custom-call | flops 8589934592 | bytes 2097152 | tf_op jit(solution)/shard_map/pallas_call | solution.py:220
  32.5 0.0 collective-permute-done.1.refs_1_
  32.5 0.0 copy-start.2
  32.5 3.7 %all-to-all-start.1 = ((bf16[32,32,384]{2,1,0:T(8,128)(2,1)}), bf16[32,32,384]{2,1,0:T(8,128)(2,1)S(1)}, u32[]{:S(2)}, u32[]{:S(2)}) async-start(bf16[32,32,384]{2,1,0:T(8,128)(2,1)} %bitcast.2), calls=%async_computation.1 | async-start | bytes 1572864 | tf_op jit(solution)/shard_map/all_to_all | solution.py:269
  36.2 3.0 %shard_map.73 = bf16[2,784,128]{2,1,0:T(8,128)(2,1)} custom-call(s32[4]{0:T(128)} %order_ref.4, s32[1]{0:T(128)} %bitcast.1._, bf16[1,4,32,12288]{3,2,1,0:T(8,128)(2,1)} %grad_ref.7), custom_call_target="tpu_custom_call" | custom-call | flops 1048576 | bytes 1024 | tf_op jit(solution)/shard_map/pallas_call | solution.py:85
  39.3 0.0 copy-start.1
  39.3 0.3 collective-permute-start.2
  39.5 1.7 %collective-permute-done.2.refs_0_ = bf16[2,784,128]{2,1,0:T(8,128)(2,1)S(1)} collective-permute-done((bf16[2,784,128]{2,1,0:T(8,128)(2,1)}, bf16[2,784,128]{2,1,0:T(8,128)(2,1)S(1)}, u32[]{:S(2)}, u32[]{:S(2)}) %collective-permute-start.2) | collective-permute-done | bytes 401440 | tf_op jit(solution)/shard_map/ppermute | solution.py:128
  41.2 0.0 copy-done.2
  41.2 0.0 copy-start.3
  41.2 0.7 %copy-done.3 = bf16[2,784,128]{2,1,0:T(8,128)(2,1)} copy-done((bf16[2,784,128]{2,1,0:T(8,128)(2,1)}, bf16[2,784,128]{2,1,0:T(8,128)(2,1)S(1)}, u32[]{:S(2)}) %copy-start.3) | copy-done | bytes 401432
  42.0 3.3 %shard_map.74.own_ref = bf16[2,784,128]{2,1,0:T(8,128)(2,1)} custom-call(s32[4]{0:T(128)} %order_ref.4, s32[1]{0:T(128)} %bitcast.1._, bf16[1,4,32,12288]{3,2,1,0:T(8,128)(2,1)} %grad_ref.7, bf16[2,784,128]{2,1,0:T(8,128)(2,1)} %copy-done.3, bf16[2,784,128]{2,1,0:T(8,128)(2,1)} %copy-done.2), custom_call_target="tpu_custom_call" | custom-call | flops 1048576 | bytes 1024 | tf_op jit(solution)/shard_map/pallas_call | solution.py:85
  45.3 0.9 %slice.4 = bf16[1,784,128]{2,1,0:T(8,128)(2,1)S(1)} slice(bf16[2,784,128]{2,1,0:T(8,128)(2,1)} %shard_map.74.own_ref), slice={[0:1], [0:784], [0:128]} | slice | bytes 401408 | tf_op jit(solution)/shard_map/slice | solution.py:271
  46.2 1.8 %collective-permute-start.3 = (bf16[1,784,128]{2,1,0:T(8,128)(2,1)S(1)}, bf16[1,784,128]{2,1,0:T(8,128)(2,1)S(1)}, u32[]{:S(2)}, u32[]{:S(2)}) collective-permute-start(bf16[1,784,128]{2,1,0:T(8,128)(2,1)S(1)} %slice.4), channel_id=1, source_target_pairs={{0,4},{1,5},{2,6},{3,7},{4,0},{5,1},{6,2},{7,3},{8,12},{9,13},{10,... | collective-permute-start | bytes 602120 | tf_op jit(solution)/shard_map/ppermute | solution.py:128
  48.0 7.0 %collective-permute-done.3.received_ref = bf16[1,784,128]{2,1,0:T(8,128)(2,1)S(1)} collective-permute-done((bf16[1,784,128]{2,1,0:T(8,128)(2,1)S(1)}, bf16[1,784,128]{2,1,0:T(8,128)(2,1)S(1)}, u32[]{:S(2)}, u32[]{:S(2)}) %collective-permute-start.3) | collective-permute-done | bytes 200736 | tf_op jit(solution)/shard_map/ppermute | solution.py:128
  55.0 0.0 copy-start
  55.0 1.0 %copy-done = bf16[2,784,128]{2,1,0:T(8,128)(2,1)S(1)} copy-done((bf16[2,784,128]{2,1,0:T(8,128)(2,1)S(1)}, bf16[2,784,128]{2,1,0:T(8,128)(2,1)}, u32[]{:S(2)}) %copy-start) | copy-done | bytes 401432
  56.0 1.1 %shard_map.75 = f32[1,1536,128]{2,1,0:T(8,128)} custom-call(bf16[2,784,128]{2,1,0:T(8,128)(2,1)S(1)} %copy-done, bf16[1,784,128]{2,1,0:T(8,128)(2,1)S(1)} %collective-permute-done.3.received_ref), custom_call_target="tpu_custom_call" | custom-call | flops 1048576 | bytes 1024 | tf_op jit(solution)/shard_map/pallas_call | solution.py:116
  57.0 0.0 all-to-all-done.1.in_ref
  57.1 0.0 copy-done.1
  57.1 1.6 %shard_map.72 = f32[1,384,128]{2,1,0:T(8,128)} custom-call(s32[4]{0:T(128)S(1)} %copy-done.1, bf16[32,32,384]{2,1,0:T(8,128)(2,1)S(1)} %all-to-all-done.1.in_ref), custom_call_target="tpu_custom_call" | custom-call | flops 100663296 | bytes 1048576 | tf_op jit(solution)/shard_map/pallas_call | solution.py:245
Async XLA Ops:
  3.1 20.5 %all-to-all-start = ((bf16[4,496,128]{2,1,0:T(8,128)(2,1)}), bf16[4,496,128]{2,1,0:T(8,128)(2,1)S(1)}, u32[]{:S(2)}, u32[]{:S(2)}) async-start(bf16[4,496,128]{2,1,0:T(8,128)(2,1)} %shard_map.68), calls=%async_computation | async-start | bytes 1015808 | tf_op jit(solution)/shard_map/all_to_all | solution.py:260
  12.5 1.9 %collective-permute-start = (bf16[2,784,128]{2,1,0:T(8,128)(2,1)}, bf16[2,784,128]{2,1,0:T(8,128)(2,1)S(1)}, u32[]{:S(2)}, u32[]{:S(2)}) collective-permute-start(bf16[2,784,128]{2,1,0:T(8,128)(2,1)} %shard_map.69), channel_id=1, source_target_pairs={{0,1},{1,0},{2,3},{3,2},{4,5},{5,4},{6,7},{7,6},{8,9},{9,8},{10,11... | collective-permute-start | bytes 1204232 | tf_op jit(solution)/shard_map/ppermute | solution.py:128
  14.4 0.8 %copy-start.4 = (bf16[2,784,128]{2,1,0:T(8,128)(2,1)}, bf16[2,784,128]{2,1,0:T(8,128)(2,1)S(1)}, u32[]{:S(2)}) copy-start(bf16[2,784,128]{2,1,0:T(8,128)(2,1)S(1)} %collective-permute-done.refs_0_) | copy-start | bytes 1204228
  18.3 14.2 %collective-permute-start.1 = (bf16[2,784,128]{2,1,0:T(8,128)(2,1)}, bf16[2,784,128]{2,1,0:T(8,128)(2,1)S(1)}, u32[]{:S(2)}, u32[]{:S(2)}) collective-permute-start(bf16[2,784,128]{2,1,0:T(8,128)(2,1)} %shard_map.70), channel_id=1, source_target_pairs={{0,2},{1,3},{2,0},{3,1},{4,6},{5,7},{6,4},{7,5},{8,10},{9,11},{10,... | collective-permute-start | bytes 1204232 | tf_op jit(solution)/shard_map/ppermute | solution.py:128
  32.5 8.7 %copy-start.2 = (bf16[2,784,128]{2,1,0:T(8,128)(2,1)}, bf16[2,784,128]{2,1,0:T(8,128)(2,1)S(1)}, u32[]{:S(2)}) copy-start(bf16[2,784,128]{2,1,0:T(8,128)(2,1)S(1)} %collective-permute-done.1.refs_1_) | copy-start | bytes 1204228
  32.5 24.5 %all-to-all-start.1 = ((bf16[32,32,384]{2,1,0:T(8,128)(2,1)}), bf16[32,32,384]{2,1,0:T(8,128)(2,1)S(1)}, u32[]{:S(2)}, u32[]{:S(2)}) async-start(bf16[32,32,384]{2,1,0:T(8,128)(2,1)} %bitcast.2), calls=%async_computation.1 | async-start | bytes 1572864 | tf_op jit(solution)/shard_map/all_to_all | solution.py:269
  39.3 17.8 %copy-start.1 = (s32[4]{0:T(128)S(1)}, s32[4]{0:T(128)}, u32[]{:S(2)}) copy-start(s32[4]{0:T(128)} %order_ref.4) | copy-start | bytes 52
  39.3 1.9 %collective-permute-start.2 = (bf16[2,784,128]{2,1,0:T(8,128)(2,1)}, bf16[2,784,128]{2,1,0:T(8,128)(2,1)S(1)}, u32[]{:S(2)}, u32[]{:S(2)}) collective-permute-start(bf16[2,784,128]{2,1,0:T(8,128)(2,1)} %shard_map.73), channel_id=1, source_target_pairs={{0,1},{1,0},{2,3},{3,2},{4,5},{5,4},{6,7},{7,6},{8,9},{9,8},{10,11... | collective-permute-start | bytes 1204232 | tf_op jit(solution)/shard_map/ppermute | solution.py:128
  41.2 0.7 %copy-start.3 = (bf16[2,784,128]{2,1,0:T(8,128)(2,1)}, bf16[2,784,128]{2,1,0:T(8,128)(2,1)S(1)}, u32[]{:S(2)}) copy-start(bf16[2,784,128]{2,1,0:T(8,128)(2,1)S(1)} %collective-permute-done.2.refs_0_) | copy-start | bytes 1204228
  46.2 8.8 %collective-permute-start.3 = (bf16[1,784,128]{2,1,0:T(8,128)(2,1)S(1)}, bf16[1,784,128]{2,1,0:T(8,128)(2,1)S(1)}, u32[]{:S(2)}, u32[]{:S(2)}) collective-permute-start(bf16[1,784,128]{2,1,0:T(8,128)(2,1)S(1)} %slice.4), channel_id=1, source_target_pairs={{0,4},{1,5},{2,6},{3,7},{4,0},{5,1},{6,2},{7,3},{8,12},{9,13},{10,... | collective-permute-start | bytes 602120 | tf_op jit(solution)/shard_map/ppermute | solution.py:128
  55.0 1.0 %copy-start = (bf16[2,784,128]{2,1,0:T(8,128)(2,1)S(1)}, bf16[2,784,128]{2,1,0:T(8,128)(2,1)}, u32[]{:S(2)}) copy-start(bf16[2,784,128]{2,1,0:T(8,128)(2,1)} %shard_map.74.own_ref) | copy-start | bytes 1204228

commit v4 on v3

v4 whole, which is shorter than its diff:
```python
import functools

import jax
import jax.numpy as jnp
from jax import lax
from jax.experimental import pallas as pl
from jax.experimental.pallas import tpu as pltpu
from jax.sharding import PartitionSpec as P

AWIN = 3072
GWIN = 12288
BLK = 128
VMEM_LIMIT = 16 * 1024 * 1024
HIDDEN_COST = 1 << 31
ROOT = 0.7978845608028654

SMEM_SPEC = pl.BlockSpec(memory_space=pltpu.SMEM)
VMEM_SPEC = pl.BlockSpec(memory_space=pltpu.VMEM)


def params(limit=VMEM_LIMIT):
    return pltpu.CompilerParams(vmem_limit_bytes=limit)


def gelu(x):
    inner = ROOT * (x + 0.044715 * (x * x * x))
    return x * (0.5 * (1.0 + jnp.tanh(inner)))


def batch_weight(order_ref, batch_id, micro):
    weight = jnp.float32(0.0)
    for slot in range(micro):
        weight = jnp.where(order_ref[slot] == batch_id, jnp.float32(0.5 * 0.5 ** (micro - 1 - slot)), weight)
    return weight


def gram(left, right):
    return lax.dot_general(left, right, (((0,), (0,)), ((), ())), preferred_element_type=jnp.float32)


def iotas():
    row = lax.broadcasted_iota(jnp.int32, (BLK, BLK), 0)
    col = lax.broadcasted_iota(jnp.int32, (BLK, BLK), 1)
    return row, col


def packed_rows(pairs):
    return pairs * BLK + -(-pairs // 16) * 16


def hidden_kernel(micro, pairs, scale, order_ref, _, grad_ref, far_ref, near_ref):
    row, col = iotas()
    weights = [batch_weight(order_ref, m, micro) for m in range(micro)]
    far = pl.program_id(0) < pl.num_programs(0) // 2
    tail_row = lax.broadcasted_iota(jnp.int32, (packed_rows(pairs) - pairs * BLK, BLK), 0)

    def store(half, rows, value):
        @pl.when(far)
        def _():
            far_ref[0, half, rows] = value

        @pl.when(jnp.logical_not(far))
        def _():
            near_ref[0, half, rows] = value

    for half in range(2):
        tail = jnp.zeros(tail_row.shape, jnp.float32)
        for pair in range(pairs):
            at = (half * pairs + pair) * 2 * BLK
            parts = [grad_ref[0, m, :, at:at + 2 * BLK] for m in range(micro)]
            scaled = [(part.astype(jnp.float32) * weight).astype(jnp.bfloat16) for part, weight in zip(parts, weights)]
            both = gram(jnp.concatenate(scaled, axis=0), jnp.concatenate(parts, axis=0)) * scale
            first, second = both[:BLK, :BLK], both[BLK:, BLK:]
            packed = jnp.where(col >= row, first, second).astype(jnp.bfloat16)
            store(half, slice(pair * BLK, (pair + 1) * BLK), packed)
            diagonal = jnp.sum(jnp.where(col == row, second, 0.0), axis=0, keepdims=True)
            tail = jnp.where(tail_row == pair, diagonal, tail)
        store(half, slice(pairs * BLK, None), tail.astype(jnp.bfloat16))


def hidden_terms(order, hidden_grad, me, dp_count, scale):
    _, micro, rows, width = hidden_grad.shape
    own = width // dp_count
    pairs = own // (4 * BLK)
    shape, half = (2, packed_rows(pairs), BLK), dp_count // 2

    def owner(i, order, me):
        return 0, 0, 0, jnp.bitwise_xor(me[0], 7 - i // half - 2 * (i // 2 % 2) - 4 * (i % 2))

    return pl.pallas_call(
        functools.partial(hidden_kernel, micro, pairs, scale),
        out_shape=(jax.ShapeDtypeStruct((half,) + shape, jnp.bfloat16),) * 2,
        grid_spec=pltpu.PrefetchScalarGridSpec(
            num_scalar_prefetch=2,
            grid=(dp_count,),
            in_specs=[pl.BlockSpec((1, micro, rows, own), owner)],
            out_specs=(
                pl.BlockSpec((1,) + shape, lambda i, order, me: (jnp.minimum(i, half - 1), 0, 0, 0)),
                pl.BlockSpec((1,) + shape, lambda i, order, me: (jnp.maximum(i - half, 0), 0, 0, 0)),
            ),
        ),
        compiler_params=params(),
        cost_estimate=pl.CostEstimate(flops=HIDDEN_COST, bytes_accessed=1 << 10, transcendentals=0),
    )(order, me, hidden_grad)


def small_call(kernel, shapes, *operands):
    return pl.pallas_call(
        kernel,
        out_shape=shapes,
        in_specs=[VMEM_SPEC] * len(operands),
        out_specs=jax.tree.map(lambda _: VMEM_SPEC, shapes),
        compiler_params=params(),
        cost_estimate=pl.CostEstimate(flops=1 << 20, bytes_accessed=1 << 10, transcendentals=0),
    )(*operands)


def core_sum_kernel(near_ref, came_ref, along_x_ref, along_y_ref, first_ref, second_ref):
    def total(place, half):
        return near_ref[place, half].astype(jnp.float32) + came_ref[place, half].astype(jnp.float32)

    for i in range(2):
        along_x_ref[i] = total(i, 0).astype(jnp.bfloat16)
        along_y_ref[i] = total(2 * i, 1).astype(jnp.bfloat16)
        first_ref[i] = total(2 + i, 0)
        second_ref[i] = total(1 + 2 * i, 1)


def pair_sum_kernel(first_ref, came_x_ref, second_ref, came_y_ref, along_y_ref, along_x_ref, kept_ref):
    along_y_ref[...] = (first_ref[0] + came_x_ref[0].astype(jnp.float32)).astype(jnp.bfloat16)
    along_x_ref[...] = (second_ref[0] + came_y_ref[0].astype(jnp.float32)).astype(jnp.bfloat16)
    kept_ref[0] = first_ref[1] + came_x_ref[1].astype(jnp.float32)
    kept_ref[1] = second_ref[1] + came_y_ref[1].astype(jnp.float32)


def unpack_kernel(pairs, kept_ref, came_y_ref, came_x_ref, out_ref):
    row, col = iotas()
    for half, came_ref in enumerate((came_y_ref, came_x_ref)):

        def total(rows):
            return kept_ref[half, rows] + came_ref[rows].astype(jnp.float32)

        tail = total(slice(pairs * BLK, None))
        for pair in range(pairs):
            value = total(slice(pair * BLK, (pair + 1) * BLK))
            turned = value.T
            at = (half * pairs + pair) * 2 * BLK
            out_ref[0, at:at + BLK] = jnp.where(col >= row, value, turned)
            second = jnp.where(col == row, tail[pair:pair + 1], turned)
            out_ref[0, at + BLK:at + 2 * BLK] = jnp.where(col < row, value, second)


def hidden_factor(near, came):
    rows = near.shape[2]
    pairs = rows // BLK
    one = (rows, BLK)
    sent = jax.ShapeDtypeStruct((2,) + one, jnp.bfloat16)
    kept = jax.ShapeDtypeStruct((2,) + one, jnp.float32)
    along_x, along_y, first, second = small_call(core_sum_kernel, (sent, sent, kept, kept), near, came)
    last = jax.ShapeDtypeStruct(one, jnp.bfloat16)
    along_y, along_x, own = small_call(
        pair_sum_kernel, (last, last, kept), first, swapped(along_x, "dp", 2), second, swapped(along_y, "dp", 4)
    )
    out = jax.ShapeDtypeStruct((1, 4 * pairs * BLK, BLK), jnp.float32)
    return small_call(
        functools.partial(unpack_kernel, pairs), out, own, swapped(along_y, "dp", 4), swapped(along_x, "dp", 2)
    )


def swapped(shard, axis, mask):
    return lax.ppermute(shard, axis, [(i, i ^ mask) for i in range(lax.axis_size(axis))])


def message_kernel(in_ref, gain_ref, repeats_ref, me_ref, *out_refs):
    _, rows, part = in_ref.shape
    chunks, gain_rows = part // BLK, gain_ref.shape[0]
    gain = gain_ref[...]
    high = gain.astype(jnp.bfloat16)
    low = (gain - high.astype(jnp.float32)).astype(jnp.bfloat16)
    count = jnp.full((16, BLK), repeats_ref[0], jnp.int32).astype(jnp.float32).astype(jnp.bfloat16)
    at = chunks * rows
    for mask, out_ref in enumerate(out_refs, 1):
        target = jnp.bitwise_xor(me_ref[0], mask)
        for chunk in range(chunks):
            out_ref[chunk * rows:(chunk + 1) * rows] = in_ref[target, :, chunk * BLK:(chunk + 1) * BLK]
        out_ref[at:at + gain_rows] = high
        out_ref[at + gain_rows:at + 2 * gain_rows] = low
        out_ref[at + 2 * gain_rows:] = count


def messages(inputs, gain, repeats, me):
    micro, rows, part = inputs.shape
    shape = jax.ShapeDtypeStruct((part // BLK * rows + 2 * gain.shape[0] + 16, BLK), jnp.bfloat16)
    return pl.pallas_call(
        message_kernel,
        out_shape=(shape,) * (micro - 1),
        in_specs=[VMEM_SPEC, VMEM_SPEC, SMEM_SPEC, SMEM_SPEC],
        out_specs=(VMEM_SPEC,) * (micro - 1),
        compiler_params=params(60 * 1024 * 1024),
        cost_estimate=pl.CostEstimate(flops=1 << 20, bytes_accessed=1 << 20, transcendentals=0),
    )(inputs, gain, repeats, me)


def relay_kernel(sections, owners, own_ref, gain_ref, repeats_ref, me_ref, *refs):
    received, (out_ref, held, gains) = refs[:-3], refs[-3:]
    chunks, rows, _ = held.shape
    own = out_ref.shape[3]
    width = chunks * BLK
    part = chunks // sections
    at = part * rows
    me = me_ref[0]
    none = jnp.zeros((rows, BLK), jnp.float32)

    def mean(total):
        return jnp.sum(total, axis=-1, keepdims=True) * (1.0 / width)

    gains[me, :chunks] = gain_ref[...]
    gains[me, chunks:] = jnp.full((8, BLK), repeats_ref[0], jnp.int32).astype(jnp.float32)
    total = none
    for chunk in range(part):
        value = own_ref[me, :, chunk * BLK:(chunk + 1) * BLK].astype(jnp.float32)
        held[me * part + chunk] = value
        total = total + value
    for mask, ref in enumerate(received, 1):
        source = jnp.bitwise_xor(me, mask)
        gains[source, :chunks] = ref[at:at + chunks].astype(jnp.float32) + ref[at + chunks:at + 2 * chunks].astype(jnp.float32)
        gains[source, chunks:] = ref[at + 2 * chunks:].astype(jnp.float32)[:8]
        for chunk in range(part):
            value = ref[chunk * rows:(chunk + 1) * rows].astype(jnp.float32)
            held[source * part + chunk] = value
            total = total + value
    center = mean(total)
    square = none
    for chunk in range(chunks):
        square = square + jnp.square(held[chunk] - center)
    start = (center, lax.rsqrt(mean(square) + 1e-05))

    def section(s, carry):
        repeats = jnp.max(gains[s, chunks:]).astype(jnp.int32)

        def apply(_, carry):
            center, scale = carry
            half = 0.5 * scale
            total, square = none, none
            for chunk in range(chunks):
                value = held[chunk]
                y = (value - center) * half * gains[s, chunk:chunk + 1]
                inner = y * (2.0 * ROOT + (8.0 * 0.044715 * ROOT) * (y * y))
                value = (value + (y + y * jnp.tanh(inner))).astype(jnp.bfloat16).astype(jnp.float32)
                held[chunk] = value
                moved = value - center
                total = total + moved
                square = square + moved * moved
            shift = mean(total)
            spread = jnp.maximum(mean(square) - shift * shift, 0.0)
            return center + shift, lax.rsqrt(spread + 1e-05)

        carry = lax.fori_loop(0, repeats + 1, apply, carry)
        center, scale = carry
        for chunk in range(owners * own // BLK):
            normed = (held[chunk] - center) * scale * gains[s, chunk:chunk + 1]
            owner, col = chunk * BLK // own, chunk * BLK % own
            out_ref[s, owner, :, col:col + BLK] = normed.astype(jnp.bfloat16)
        return carry

    lax.fori_loop(0, sections, section, start)


def relay(inputs, gain, repeats, me, received, owners):
    sections, rows, part = inputs.shape
    chunks = sections * part // BLK
    own = AWIN // owners
    return pl.pallas_call(
        functools.partial(relay_kernel, sections, owners),
        out_shape=jax.ShapeDtypeStruct((sections, owners, rows, own), jnp.bfloat16),
        in_specs=[VMEM_SPEC, VMEM_SPEC, SMEM_SPEC, SMEM_SPEC] + [VMEM_SPEC] * len(received),
        out_specs=VMEM_SPEC,
        scratch_shapes=[pltpu.VMEM((chunks, rows, BLK), jnp.float32), pltpu.VMEM((sections, chunks + 8, BLK), jnp.float32)],
        compiler_params=params(),
        cost_estimate=pl.CostEstimate(flops=1 << 33, bytes_accessed=2 << 20, transcendentals=0),
    )(inputs, gain, repeats, me, *received)


def feature_kernel(micro, scale, order_ref, in_ref, out_ref):
    sources, rows, own = in_ref.shape
    group = sources // micro
    weights = [batch_weight(order_ref, m, micro) * scale for m in range(micro)]
    for at in range(0, own, BLK):
        total = jnp.zeros((BLK, BLK), jnp.float32)
        for m in range(micro):
            feats = in_ref[m * group:(m + 1) * group, :, at:at + BLK].reshape(group * rows, BLK)
            total = total + gram(feats, feats) * weights[m]
        out_ref[0, at:at + BLK] = total


def feature_factor(order, gathered, micro, scale):
    sources, rows, own = gathered.shape
    return pl.pallas_call(
        functools.partial(feature_kernel, micro, scale),
        out_shape=jax.ShapeDtypeStruct((1, own, BLK), jnp.float32),
        in_specs=[SMEM_SPEC, VMEM_SPEC],
        out_specs=VMEM_SPEC,
        compiler_params=params(),
        cost_estimate=pl.CostEstimate(flops=2 * sources * rows * own * BLK, bytes_accessed=1 << 20, transcendentals=0),
    )(order, gathered)


def fast_body(inputs, gain, repeats, order, hidden_grad):
    micro, tok_rows, _ = inputs.shape
    dp_count = lax.axis_size("dp")
    scale = 1.0 / (tok_rows * dp_count)
    gain = gain.reshape(-1, BLK)
    plane = lax.axis_index("section").reshape(1)
    told, order = lax.optimization_barrier((messages(inputs, gain, repeats, plane), order))
    pieces = tuple(swapped(one, "section", mask) for mask, one in enumerate(told, 1))

    far, near = hidden_terms(order, hidden_grad, lax.axis_index("dp").reshape(1), dp_count, scale)
    came = swapped(far, "dp", 1)
    pieces, near = lax.optimization_barrier((pieces, near))
    feats = relay(inputs, gain, repeats, plane, pieces, dp_count)
    feats, near, came, order = lax.optimization_barrier((feats, near, came, order))
    feats = feats.reshape((-1,) + feats.shape[2:])
    feats = lax.all_to_all(feats, ("section", "dp"), 0, 0, tiled=True)
    hidden_rows = hidden_factor(near, came)
    feature_rows = feature_factor(order, feats, micro, scale)
    return (feature_rows, hidden_rows)


def normed(value, gain_row):
    center = jnp.mean(value, axis=-1, keepdims=True)
    spread = jnp.mean(jnp.square(value - center), axis=-1, keepdims=True)
    return (value - center) * lax.rsqrt(spread + 1e-05) * gain_row


def weighted_gram(feats, weights):
    shaped = feats.reshape(feats.shape[0], -1, BLK)
    scaled = shaped * weights[:, None, None].astype(shaped.dtype)
    return jnp.einsum("tbi,tbj->bij", scaled, shaped, preferred_element_type=jnp.float32)


def plain_body(inputs, gain, repeats, order, hidden_grad):
    micro, tok_rows, part = inputs.shape
    sections = lax.axis_size("section")
    total_tok = tok_rows * lax.axis_size("dp")
    slot_weight = 0.5 * jnp.power(0.5, micro - 1 - jnp.arange(micro, dtype=jnp.float32))
    hidden_weight = jnp.zeros((micro,), jnp.float32).at[order].set(slot_weight)
    row_weight = jnp.repeat(hidden_weight, tok_rows)
    hidden = weighted_gram(hidden_grad.reshape(micro * tok_rows, GWIN), row_weight) / total_tok
    gains = lax.all_gather(gain[0], "section", axis=0)
    counts = lax.all_gather(repeats[0], "section", axis=0)
    pieces = lax.all_to_all(inputs.reshape(micro * tok_rows, part), "section", 0, 1, tiled=True)

    def section(s, carry):
        value, feats = carry
        value = lax.fori_loop(
            0,
            counts[s] + 1,
            lambda i, v: (v + gelu(normed(v, gains[s]))).astype(jnp.bfloat16).astype(jnp.float32),
            value,
        )
        now = normed(value, gains[s]).astype(jnp.bfloat16)[:, :AWIN]
        return value, lax.dynamic_update_index_in_dim(feats, now, s, 0)

    start = jnp.zeros((sections, pieces.shape[0], AWIN), jnp.bfloat16)
    _, feats = lax.fori_loop(0, sections, section, (pieces.astype(jnp.float32), start))
    feats = lax.all_to_all(feats, "section", 0, 0, tiled=True).reshape(micro * tok_rows, AWIN)
    feature = weighted_gram(feats, row_weight) / total_tok

    def shared(term):
        term = term.reshape(-1, BLK).astype(jnp.bfloat16)
        return lax.psum_scatter(term, "dp", scatter_dimension=0, tiled=True).astype(jnp.float32)[None]

    return (shared(feature), shared(hidden))


def solution(mesh):
    sections, dp_count = mesh.shape["section"], mesh.shape["dp"]

    def body(inputs, gain, repeats, order, hidden_grad):
        aligned = (
            inputs.shape[0] == sections == 4
            and inputs.shape[2] * sections % (16 * BLK) == 0
            and inputs.shape[1] % 16 == 0
            and dp_count == 8
            and AWIN % (dp_count * BLK) == 0
            and GWIN % (dp_count * 4 * BLK) == 0
        )
        return (fast_body if aligned else plain_body)(inputs, gain, repeats, order, hidden_grad)

    placed = (
        P(None, "dp", "section"),
        P("section", None),
        P("section"),
        P(),
        P("section", None, "dp", None),
    )
    return jax.shard_map(
        body,
        mesh=mesh,
        in_specs=placed,
        out_specs=(P("section", "dp", None), P("section", "dp", None)),
        check_vma=False,
    )
```

time: 59 us -> 61.4 us (1.041)
  starting transfers between devices: 13.6 us -> 17.8 us
  Pallas kernels: 25.9 us -> 24.5 us
  local copies, waits for them, and re-layouts: 3.45 us -> 2.56 us
    ppermute x4 -> x8, starting transfers between devices: 3.58 us -> 11.6 us  [swapped(): lax.ppermute(shard, axis, [(i, i ^ mask) for i in range(lax.axis_size(axi...]
    all_to_all x1 -> x0, starting transfers between devices: 6.32 us -> none  [fast_body(): pieces = lax.all_to_all(told, 'section', 0, 0, tiled=True)]
    ppermute x4 -> x8, waiting for transfers between devices: 10.6 us -> 14.7 us  [swapped(): lax.ppermute(shard, axis, [(i, i ^ mask) for i in range(lax.axis_size(axi...]
    all_to_all x1 -> x0, waiting for transfers between devices: 3.81 us -> none  [fast_body(): pieces = lax.all_to_all(told, 'section', 0, 0, tiled=True)]
    all_to_all x1, starting transfers between devices: 3.71 us -> 6.15 us  [fast_body(): feats = lax.all_to_all(feats, ('section', 'dp'), 0, 0, tiled=True)]
    pallas_call x3 -> x5, Pallas kernels: 11.8 us -> 9.69 us  [the longest x1 6.56 us: relay(): pl.pallas_call(functools.partial(relay_kernel, sections, owners), out_sha...]
    slice x1 -> x0, local copies, waits for them, and re-layouts: 0.94 us -> none  [fast_body(): both[:1]]
    pallas_call x4 -> x1, Pallas kernels: 12.5 us -> 13.1 us  [hidden_terms(): pl.pallas_call(functools.partial(hidden_kernel, micro, pairs, scale), out...]
  transfers between devices with their start and end apart: 6 -> 9, of which waited for: 4 -> 3; matrix products, arithmetic and copies ran while one was open for 2% -> 0% of each run, Pallas kernels for 38% -> 35%
where the time goes in v4:
time: 61.4 us; the launch traced here: 60.9 us
  Pallas kernels  24.5 us (40%)
  starting transfers between devices  17.8 us (29%)
  waiting for transfers between devices  14.7 us (24%)
  local copies, waits for them, and re-layouts  2.56 us (4%)
  between operations  1.37 us (2%)
    ppermute x8, waiting for transfers between devices, swapped(): lax.ppermute(shard, axis, [(i, i ^ mask) for i in range(lax.axis_size(axi...  14.7 us
    pallas_call x1, Pallas kernels, hidden_terms(): pl.pallas_call(functools.partial(hidden_kernel, micro, pairs, scale), out...  13.1 us
    ppermute x8, starting transfers between devices, swapped(): lax.ppermute(shard, axis, [(i, i ^ mask) for i in range(lax.axis_size(axi...  11.6 us
    pallas_call x1, Pallas kernels, relay(): pl.pallas_call(functools.partial(relay_kernel, sections, owners), out_sha...  6.56 us
    all_to_all x1, starting transfers between devices, fast_body(): feats = lax.all_to_all(feats, ('section', 'dp'), 0, 0, tiled=True)  6.15 us
    unnamed x10, local copies, waits for them, and re-layouts  2.56 us
    pallas_call x1, Pallas kernels, messages(): pl.pallas_call(message_kernel, out_shape=(shape,) * (micro - 1), in_specs...  1.81 us
    pallas_call x1, Pallas kernels, feature_factor(): pl.pallas_call(functools.partial(feature_kernel, micro, scale), out_shape...  1.63 us
  transfers between devices with their start and end apart: 9, of which 3 were waited for; matrix products, arithmetic and copies ran while one was open for 0% of the time, Pallas kernels for 35%

profile of v4, /device:TPU:0, one launch (start us, length us, event | category | flops | bytes accessed | tf_op | source)
XLA Modules:
  0.0 60.9 jit_solution(7284293276749757277)
XLA Ops:
  1.3 1.8 %shard_map.68 = (bf16[496,128]{1,0:T(8,128)(2,1)}, bf16[496,128]{1,0:T(8,128)(2,1)}, bf16[496,128]{1,0:T(8,128)(2,1)}) custom-call(bf16[4,32,1536]{2,1,0:T(8,128)(2,1)} %own_ref.1, f32[48,128]{1,0:T(8,128)} %bitcast.4, s32[1]{0:T(128)S(6)} %copy.7.repeats_ref, s32[1]{0:T(128)} %bitcast.1.me_ref), custom_call_target="tpu_custom_call" | custom-call | flops 1048576 | bytes 1048576 | tf_op jit(solution)/shard_map/pallas_call | solution.py:194
  3.1 3.0 %collective-permute-start = (bf16[496,128]{1,0:T(8,128)(2,1)}, bf16[496,128]{1,0:T(8,128)(2,1)S(1)}, u32[]{:S(2)}, u32[]{:S(2)}) collective-permute-start(bf16[496,128]{1,0:T(8,128)(2,1)} %get-tuple-element.29), channel_id=1, source_target_pairs={{0,8},{8,0},{16,24},{24,16},{1,9},{9,1},{17,25},{25,17},{2,10},{10... | collective-permute-start | bytes 380936 | tf_op jit(solution)/shard_map/ppermute | solution.py:171
  6.1 2.6 %collective-permute-start.1 = (bf16[496,128]{1,0:T(8,128)(2,1)}, bf16[496,128]{1,0:T(8,128)(2,1)S(1)}, u32[]{:S(2)}, u32[]{:S(2)}) collective-permute-start(bf16[496,128]{1,0:T(8,128)(2,1)} %get-tuple-element.30), channel_id=1, source_target_pairs={{0,16},{8,24},{16,0},{24,8},{1,17},{9,25},{17,1},{25,9},{2,18},{10... | collective-permute-start | bytes 380936 | tf_op jit(solution)/shard_map/ppermute | solution.py:171
  8.7 0.0 collective-permute-start.2
  8.7 0.0 copy-start.2
  8.7 0.7 %copy-done.2 = s32[4]{0:T(128)S(1)} copy-done((s32[4]{0:T(128)S(1)}, s32[4]{0:T(128)}, u32[]{:S(2)}) %copy-start.2) | copy-done | bytes 40
  9.4 0.0 copy-start.4
  9.4 1.9 %copy-done.4 = bf16[1,4,32,12288]{3,2,1,0:T(8,128)(2,1)S(1)} copy-done((bf16[1,4,32,12288]{3,2,1,0:T(8,128)(2,1)S(1)}, bf16[1,4,32,12288]{3,2,1,0:T(8,128)(2,1)}, u32[]{:S(2)}) %copy-start.4) | copy-done | bytes 3145752
  11.3 0.0 copy-start
  11.3 0.0 copy-start.1
  11.3 13.1 %shard_map.69 = (bf16[4,2,400,128]{3,2,1,0:T(8,128)(2,1)S(1)}, bf16[4,2,400,128]{3,2,1,0:T(8,128)(2,1)S(1)}) custom-call(s32[4]{0:T(128)S(1)} %copy-done.2, s32[1]{0:T(128)} %bitcast.2._, bf16[1,4,32,12288]{3,2,1,0:T(8,128)(2,1)S(1)} %copy-done.4), custom_call_target="tpu_custom_call" | custom-call | flops 2147483648 | bytes 1024 | tf_op jit(solution)/shard_map/pallas_call | solution.py:90
  24.4 0.1 collective-permute-start.3
  24.5 0.0 collective-permute-done.refs_0_
  24.5 0.0 collective-permute-done.1.refs_1_
  24.5 0.0 collective-permute-done.2.refs_2_
  24.5 0.0 copy-done
  24.5 0.0 copy-done.1
  24.5 6.6 %shard_map.70 = bf16[4,8,32,384]{3,2,1,0:T(8,128)(2,1)} custom-call(bf16[4,32,1536]{2,1,0:T(8,128)(2,1)S(1)} %copy-done, f32[48,128]{1,0:T(8,128)S(1)} %bitcast.5, s32[1]{0:T(128)S(6)} %copy.7.repeats_ref, s32[1]{0:T(128)} %bitcast.1.me_ref, bf16[496,128]{1,0:T(8,128)(2,1)S(1)} %collective-permute-done.refs_0_, ...), custom_call_target="tpu_custom_call" | custom-call | flops 8589934592 | bytes 2097152 | tf_op jit(solution)/shard_map/pallas_call | solution.py:273
  31.1 0.0 copy-start.3
  31.1 0.0 collective-permute-done.3.came_ref
  31.1 6.2 %all-to-all-start = ((bf16[32,32,384]{2,1,0:T(8,128)(2,1)}), bf16[32,32,384]{2,1,0:T(8,128)(2,1)S(1)}, u32[]{:S(2)}, u32[]{:S(2)}) async-start(bf16[32,32,384]{2,1,0:T(8,128)(2,1)} %bitcast.3), calls=%async_computation | async-start | bytes 1572864 | tf_op jit(solution)/shard_map/all_to_all | solution.py:323
  37.3 0.2 shard_map.72
  37.4 1.8 %collective-permute-start.4 = (bf16[2,400,128]{2,1,0:T(8,128)(2,1)S(1)}, bf16[2,400,128]{2,1,0:T(8,128)(2,1)S(1)}, u32[]{:S(2)}, u32[]{:S(2)}) collective-permute-start(bf16[2,400,128]{2,1,0:T(8,128)(2,1)S(1)} %get-tuple-element.44), channel_id=1, source_target_pairs={{0,2},{1,3},{2,0},{3,1},{4,6},{5,7},{6,4},{7,5},{8,10},{9,11},{10,... | collective-permute-start | bytes 614408 | tf_op jit(solution)/shard_map/ppermute | solution.py:171
  39.3 1.5 %collective-permute-start.5 = (bf16[2,400,128]{2,1,0:T(8,128)(2,1)S(1)}, bf16[2,400,128]{2,1,0:T(8,128)(2,1)S(1)}, u32[]{:S(2)}, u32[]{:S(2)}) collective-permute-start(bf16[2,400,128]{2,1,0:T(8,128)(2,1)S(1)} %get-tuple-element.46), channel_id=1, source_target_pairs={{0,4},{1,5},{2,6},{3,7},{4,0},{5,1},{6,2},{7,3},{8,12},{9,13},{10,... | collective-permute-start | bytes 614408 | tf_op jit(solution)/shard_map/ppermute | solution.py:171
  40.7 10.6 %collective-permute-done.4.came_x_ref = bf16[2,400,128]{2,1,0:T(8,128)(2,1)S(1)} collective-permute-done((bf16[2,400,128]{2,1,0:T(8,128)(2,1)S(1)}, bf16[2,400,128]{2,1,0:T(8,128)(2,1)S(1)}, u32[]{:S(2)}, u32[]{:S(2)}) %collective-permute-start.4) | collective-permute-done | bytes 204832 | tf_op jit(solution)/shard_map/ppermute | solution.py:171
  51.4 0.0 collective-permute-done.5.came_y_ref
  51.4 0.1 shard_map.73
  51.4 1.5 %collective-permute-start.6 = (bf16[400,128]{1,0:T(8,128)(2,1)S(1)}, bf16[400,128]{1,0:T(8,128)(2,1)S(1)}, u32[]{:S(2)}, u32[]{:S(2)}) collective-permute-start(bf16[400,128]{1,0:T(8,128)(2,1)S(1)} %get-tuple-element.48), channel_id=1, source_target_pairs={{0,4},{1,5},{2,6},{3,7},{4,0},{5,1},{6,2},{7,3},{8,12},{9,13},{10,... | collective-permute-start | bytes 307208 | tf_op jit(solution)/shard_map/ppermute | solution.py:171
  53.0 1.1 %collective-permute-start.7 = (bf16[400,128]{1,0:T(8,128)(2,1)S(1)}, bf16[400,128]{1,0:T(8,128)(2,1)S(1)}, u32[]{:S(2)}, u32[]{:S(2)}) collective-permute-start(bf16[400,128]{1,0:T(8,128)(2,1)S(1)} %get-tuple-element.49), channel_id=1, source_target_pairs={{0,2},{1,3},{2,0},{3,1},{4,6},{5,7},{6,4},{7,5},{8,10},{9,11},{10,... | collective-permute-start | bytes 307208 | tf_op jit(solution)/shard_map/ppermute | solution.py:171
  54.1 2.7 %collective-permute-done.6.came_y_ref = bf16[400,128]{1,0:T(8,128)(2,1)S(1)} collective-permute-done((bf16[400,128]{1,0:T(8,128)(2,1)S(1)}, bf16[400,128]{1,0:T(8,128)(2,1)S(1)}, u32[]{:S(2)}, u32[]{:S(2)}) %collective-permute-start.6) | collective-permute-done | bytes 102432 | tf_op jit(solution)/shard_map/ppermute | solution.py:171
  56.7 1.4 %collective-permute-done.7.came_x_ref = bf16[400,128]{1,0:T(8,128)(2,1)S(1)} collective-permute-done((bf16[400,128]{1,0:T(8,128)(2,1)S(1)}, bf16[400,128]{1,0:T(8,128)(2,1)S(1)}, u32[]{:S(2)}, u32[]{:S(2)}) %collective-permute-start.7) | collective-permute-done | bytes 102432 | tf_op jit(solution)/shard_map/ppermute | solution.py:171
  58.2 1.1 %shard_map.74 = f32[1,1536,128]{2,1,0:T(8,128)} custom-call(f32[2,400,128]{2,1,0:T(8,128)S(1)} %get-tuple-element.47.kept_ref, bf16[400,128]{1,0:T(8,128)(2,1)S(1)} %collective-permute-done.6.came_y_ref, bf16[400,128]{1,0:T(8,128)(2,1)S(1)} %collective-permute-done.7.came_x_ref), custom_call_target="tpu_custom_call" | custom-call | flops 1048576 | bytes 1024 | tf_op jit(solution)/shard_map/pallas_call | solution.py:108
  59.2 0.0 all-to-all-done.in_ref
  59.2 0.0 copy-done.3
  59.2 1.6 %shard_map.71 = f32[1,384,128]{2,1,0:T(8,128)} custom-call(s32[4]{0:T(128)S(1)} %copy-done.3, bf16[32,32,384]{2,1,0:T(8,128)(2,1)S(1)} %all-to-all-done.in_ref), custom_call_target="tpu_custom_call" | custom-call | flops 100663296 | bytes 1048576 | tf_op jit(solution)/shard_map/pallas_call | solution.py:298
Async XLA Ops:
  3.1 21.4 %collective-permute-start = (bf16[496,128]{1,0:T(8,128)(2,1)}, bf16[496,128]{1,0:T(8,128)(2,1)S(1)}, u32[]{:S(2)}, u32[]{:S(2)}) collective-permute-start(bf16[496,128]{1,0:T(8,128)(2,1)} %get-tuple-element.29), channel_id=1, source_target_pairs={{0,8},{8,0},{16,24},{24,16},{1,9},{9,1},{17,25},{25,17},{2,10},{10... | collective-permute-start | bytes 380936 | tf_op jit(solution)/shard_map/ppermute | solution.py:171
  6.1 18.4 %collective-permute-start.1 = (bf16[496,128]{1,0:T(8,128)(2,1)}, bf16[496,128]{1,0:T(8,128)(2,1)S(1)}, u32[]{:S(2)}, u32[]{:S(2)}) collective-permute-start(bf16[496,128]{1,0:T(8,128)(2,1)} %get-tuple-element.30), channel_id=1, source_target_pairs={{0,16},{8,24},{16,0},{24,8},{1,17},{9,25},{17,1},{25,9},{2,18},{10... | collective-permute-start | bytes 380936 | tf_op jit(solution)/shard_map/ppermute | solution.py:171
  8.7 15.8 %collective-permute-start.2 = (bf16[496,128]{1,0:T(8,128)(2,1)}, bf16[496,128]{1,0:T(8,128)(2,1)S(1)}, u32[]{:S(2)}, u32[]{:S(2)}) collective-permute-start(bf16[496,128]{1,0:T(8,128)(2,1)} %get-tuple-element.31), channel_id=1, source_target_pairs={{0,24},{8,16},{16,8},{24,0},{1,25},{9,17},{17,9},{25,1},{2,26},{10... | collective-permute-start | bytes 380936 | tf_op jit(solution)/shard_map/ppermute | solution.py:171
  8.7 0.7 %copy-start.2 = (s32[4]{0:T(128)S(1)}, s32[4]{0:T(128)}, u32[]{:S(2)}) copy-start(s32[4]{0:T(128)} %order_ref.1) | copy-start | bytes 52
  9.4 1.9 %copy-start.4 = (bf16[1,4,32,12288]{3,2,1,0:T(8,128)(2,1)S(1)}, bf16[1,4,32,12288]{3,2,1,0:T(8,128)(2,1)}, u32[]{:S(2)}) copy-start(bf16[1,4,32,12288]{3,2,1,0:T(8,128)(2,1)} %grad_ref.1) | copy-start | bytes 9437188
  11.3 13.3 %copy-start = (bf16[4,32,1536]{2,1,0:T(8,128)(2,1)S(1)}, bf16[4,32,1536]{2,1,0:T(8,128)(2,1)}, u32[]{:S(2)}) copy-start(bf16[4,32,1536]{2,1,0:T(8,128)(2,1)} %own_ref.1) | copy-start | bytes 1179652
  11.3 13.3 %copy-start.1 = (f32[1,6144]{1,0:T(1,128)S(1)}, f32[1,6144]{1,0:T(1,128)}, u32[]{:S(2)}) copy-start(f32[1,6144]{1,0:T(1,128)} %param.6) | copy-start | bytes 73732
  24.4 6.7 %collective-permute-start.3 = (bf16[4,2,400,128]{3,2,1,0:T(8,128)(2,1)S(1)}, bf16[4,2,400,128]{3,2,1,0:T(8,128)(2,1)S(1)}, u32[]{:S(2)}, u32[]{:S(2)}) collective-permute-start(bf16[4,2,400,128]{3,2,1,0:T(8,128)(2,1)S(1)} %get-tuple-element.38), channel_id=1, source_target_pairs={{0,1},{1,0},{2,3},{3,2},{4,5},{5,4},{6,7},{7,6},{8,9},{9,8},{10,11... | collective-permute-start | bytes 2457608 | tf_op jit(solution)/shard_map/ppermute | solution.py:171
  31.1 28.1 %copy-start.3 = (s32[4]{0:T(128)S(1)}, s32[4]{0:T(128)}, u32[]{:S(2)}) copy-start(s32[4]{0:T(128)} %order_ref.1) | copy-start | bytes 52
  31.1 28.1 %all-to-all-start = ((bf16[32,32,384]{2,1,0:T(8,128)(2,1)}), bf16[32,32,384]{2,1,0:T(8,128)(2,1)S(1)}, u32[]{:S(2)}, u32[]{:S(2)}) async-start(bf16[32,32,384]{2,1,0:T(8,128)(2,1)} %bitcast.3), calls=%async_computation | async-start | bytes 1572864 | tf_op jit(solution)/shard_map/all_to_all | solution.py:323
  37.4 13.9 %collective-permute-start.4 = (bf16[2,400,128]{2,1,0:T(8,128)(2,1)S(1)}, bf16[2,400,128]{2,1,0:T(8,128)(2,1)S(1)}, u32[]{:S(2)}, u32[]{:S(2)}) collective-permute-start(bf16[2,400,128]{2,1,0:T(8,128)(2,1)S(1)} %get-tuple-element.44), channel_id=1, source_target_pairs={{0,2},{1,3},{2,0},{3,1},{4,6},{5,7},{6,4},{7,5},{8,10},{9,11},{10,... | collective-permute-start | bytes 614408 | tf_op jit(solution)/shard_map/ppermute | solution.py:171
  39.3 12.1 %collective-permute-start.5 = (bf16[2,400,128]{2,1,0:T(8,128)(2,1)S(1)}, bf16[2,400,128]{2,1,0:T(8,128)(2,1)S(1)}, u32[]{:S(2)}, u32[]{:S(2)}) collective-permute-start(bf16[2,400,128]{2,1,0:T(8,128)(2,1)S(1)} %get-tuple-element.46), channel_id=1, source_target_pairs={{0,4},{1,5},{2,6},{3,7},{4,0},{5,1},{6,2},{7,3},{8,12},{9,13},{10,... | collective-permute-start | bytes 614408 | tf_op jit(solution)/shard_map/ppermute | solution.py:171
  51.4 5.3 %collective-permute-start.6 = (bf16[400,128]{1,0:T(8,128)(2,1)S(1)}, bf16[400,128]{1,0:T(8,128)(2,1)S(1)}, u32[]{:S(2)}, u32[]{:S(2)}) collective-permute-start(bf16[400,128]{1,0:T(8,128)(2,1)S(1)} %get-tuple-element.48), channel_id=1, source_target_pairs={{0,4},{1,5},{2,6},{3,7},{4,0},{5,1},{6,2},{7,3},{8,12},{9,13},{10,... | collective-permute-start | bytes 307208 | tf_op jit(solution)/shard_map/ppermute | solution.py:171
  53.0 5.2 %collective-permute-start.7 = (bf16[400,128]{1,0:T(8,128)(2,1)S(1)}, bf16[400,128]{1,0:T(8,128)(2,1)S(1)}, u32[]{:S(2)}, u32[]{:S(2)}) collective-permute-start(bf16[400,128]{1,0:T(8,128)(2,1)S(1)} %get-tuple-element.49), channel_id=1, source_target_pairs={{0,2},{1,3},{2,0},{3,1},{4,6},{5,7},{6,4},{7,5},{8,10},{9,11},{10,... | collective-permute-start | bytes 307208 | tf_op jit(solution)/shard_map/ppermute | solution.py:171

commit v5 on v4

--- a/solution.py
+++ b/solution.py
@@ -48,60 +48,47 @@
     return pairs * BLK + -(-pairs // 16) * 16
 
 
-def hidden_kernel(micro, pairs, scale, order_ref, _, grad_ref, far_ref, near_ref):
+def hidden_kernel(micro, pairs, scale, order_ref, _, far_grad_ref, near_grad_ref, far_ref, near_ref):
     row, col = iotas()
     weights = [batch_weight(order_ref, m, micro) for m in range(micro)]
-    far = pl.program_id(0) < pl.num_programs(0) // 2
     tail_row = lax.broadcasted_iota(jnp.int32, (packed_rows(pairs) - pairs * BLK, BLK), 0)
-
-    def store(half, rows, value):
-        @pl.when(far)
-        def _():
-            far_ref[0, half, rows] = value
-
-        @pl.when(jnp.logical_not(far))
-        def _():
-            near_ref[0, half, rows] = value
-
-    for half in range(2):
-        tail = jnp.zeros(tail_row.shape, jnp.float32)
-        for pair in range(pairs):
-            at = (half * pairs + pair) * 2 * BLK
-            parts = [grad_ref[0, m, :, at:at + 2 * BLK] for m in range(micro)]
-            scaled = [(part.astype(jnp.float32) * weight).astype(jnp.bfloat16) for part, weight in zip(parts, weights)]
-            both = gram(jnp.concatenate(scaled, axis=0), jnp.concatenate(parts, axis=0)) * scale
-            first, second = both[:BLK, :BLK], both[BLK:, BLK:]
-            packed = jnp.where(col >= row, first, second).astype(jnp.bfloat16)
-            store(half, slice(pair * BLK, (pair + 1) * BLK), packed)
-            diagonal = jnp.sum(jnp.where(col == row, second, 0.0), axis=0, keepdims=True)
-            tail = jnp.where(tail_row == pair, diagonal, tail)
-        store(half, slice(pairs * BLK, None), tail.astype(jnp.bfloat16))
+    for grad_ref, out_ref in ((far_grad_ref, far_ref), (near_grad_ref, near_ref)):
+        for half in range(2):
+            tail = jnp.zeros(tail_row.shape, jnp.float32)
+            for pair in range(pairs):
+                at = (half * pairs + pair) * 2 * BLK
+                parts = [grad_ref[0, m, :, at:at + 2 * BLK] for m in range(micro)]
+                scaled = [(part.astype(jnp.float32) * weight).astype(jnp.bfloat16) for part, weight in zip(parts, weights)]
+                both = gram(jnp.concatenate(scaled, axis=0), jnp.concatenate(parts, axis=0)) * scale
+                first, second = both[:BLK, :BLK], both[BLK:, BLK:]
+                out_ref[0, half, pair * BLK:(pair + 1) * BLK] = jnp.where(col >= row, first, second).astype(jnp.bfloat16)
+                diagonal = jnp.sum(jnp.where(col == row, second, 0.0), axis=0, keepdims=True)
+                tail = jnp.where(tail_row == pair, diagonal, tail)
+            out_ref[0, half, pairs * BLK:] = tail.astype(jnp.bfloat16)
 
 
 def hidden_terms(order, hidden_grad, me, dp_count, scale):
     _, micro, rows, width = hidden_grad.shape
     own = width // dp_count
     pairs = own // (4 * BLK)
-    shape, half = (2, packed_rows(pairs), BLK), dp_count // 2
-
-    def owner(i, order, me):
-        return 0, 0, 0, jnp.bitwise_xor(me[0], 7 - i // half - 2 * (i // 2 % 2) - 4 * (i % 2))
-
+    shape, count = (2, packed_rows(pairs), BLK), dp_count // 2
+
+    def owner(flip):
+        return lambda i, order, me: (0, 0, 0, jnp.bitwise_xor(me[0], 6 + flip - 2 * (i // 2) - 4 * (i % 2)))
+
+    out_spec = pl.BlockSpec((1,) + shape, lambda i, order, me: (i, 0, 0, 0))
     return pl.pallas_call(
         functools.partial(hidden_kernel, micro, pairs, scale),
-        out_shape=(jax.ShapeDtypeStruct((half,) + shape, jnp.bfloat16),) * 2,
+        out_shape=(jax.ShapeDtypeStruct((count,) + shape, jnp.bfloat16),) * 2,
         grid_spec=pltpu.PrefetchScalarGridSpec(
             num_scalar_prefetch=2,
-            grid=(dp_count,),
-            in_specs=[pl.BlockSpec((1, micro, rows, own), owner)],
-            out_specs=(
-                pl.BlockSpec((1,) + shape, lambda i, order, me: (jnp.minimum(i, half - 1), 0, 0, 0)),
-                pl.BlockSpec((1,) + shape, lambda i, order, me: (jnp.maximum(i - half, 0), 0, 0, 0)),
-            ),
+            grid=(count,),
+            in_specs=[pl.BlockSpec((1, micro, rows, own), owner(1)), pl.BlockSpec((1, micro, rows, own), owner(0))],
+            out_specs=(out_spec, out_spec),
         ),
         compiler_params=params(),
         cost_estimate=pl.CostEstimate(flops=HIDDEN_COST, bytes_accessed=1 << 10, transcendentals=0),
-    )(order, me, hidden_grad)
+    )(order, me, hidden_grad, hidden_grad)
 
 
 def small_call(kernel, shapes, *operands):
@@ -150,21 +137,22 @@
             out_ref[0, at + BLK:at + 2 * BLK] = jnp.where(col < row, value, second)
 
 
-def hidden_factor(near, came):
-    rows = near.shape[2]
-    pairs = rows // BLK
-    one = (rows, BLK)
+def core_sum(near, came):
+    one = near.shape[2:]
     sent = jax.ShapeDtypeStruct((2,) + one, jnp.bfloat16)
     kept = jax.ShapeDtypeStruct((2,) + one, jnp.float32)
-    along_x, along_y, first, second = small_call(core_sum_kernel, (sent, sent, kept, kept), near, came)
-    last = jax.ShapeDtypeStruct(one, jnp.bfloat16)
-    along_y, along_x, own = small_call(
-        pair_sum_kernel, (last, last, kept), first, swapped(along_x, "dp", 2), second, swapped(along_y, "dp", 4)
-    )
+    return small_call(core_sum_kernel, (sent, sent, kept, kept), near, came)
+
+
+def pair_sum(first, came_x, second, came_y):
+    last = jax.ShapeDtypeStruct(first.shape[1:], jnp.bfloat16)
+    return small_call(pair_sum_kernel, (last, last, first), first, came_x, second, came_y)
+
+
+def unpacked(kept, came_y, came_x):
+    pairs = kept.shape[1] // BLK
     out = jax.ShapeDtypeStruct((1, 4 * pairs * BLK, BLK), jnp.float32)
-    return small_call(
-        functools.partial(unpack_kernel, pairs), out, own, swapped(along_y, "dp", 4), swapped(along_x, "dp", 2)
-    )
+    return small_call(functools.partial(unpack_kernel, pairs), out, kept, came_y, came_x)
 
 
 def swapped(shard, axis, mask):
@@ -202,9 +190,9 @@
 
 
 def relay_kernel(sections, owners, own_ref, gain_ref, repeats_ref, me_ref, *refs):
-    received, (out_ref, held, gains) = refs[:-3], refs[-3:]
+    received, out_refs, (held, gains) = refs[:sections - 1], refs[sections - 1:-2], refs[-2:]
     chunks, rows, _ = held.shape
-    own = out_ref.shape[3]
+    own = AWIN // owners // BLK
     width = chunks * BLK
     part = chunks // sections
     at = part * rows
@@ -257,10 +245,11 @@
 
         carry = lax.fori_loop(0, repeats + 1, apply, carry)
         center, scale = carry
-        for chunk in range(owners * own // BLK):
-            normed = (held[chunk] - center) * scale * gains[s, chunk:chunk + 1]
-            owner, col = chunk * BLK // own, chunk * BLK % own
-            out_ref[s, owner, :, col:col + BLK] = normed.astype(jnp.bfloat16)
+        for mask, out_ref in enumerate(out_refs):
+            place = jnp.bitwise_xor(me_ref[1], mask) * own
+            for i in range(own):
+                normed = (held[place + i] - center) * scale * gains[s, pl.ds(place + i, 1)]
+                out_ref[s, :, i * BLK:(i + 1) * BLK] = normed.astype(jnp.bfloat16)
         return carry
 
     lax.fori_loop(0, sections, section, start)
@@ -269,40 +258,78 @@
 def relay(inputs, gain, repeats, me, received, owners):
     sections, rows, part = inputs.shape
     chunks = sections * part // BLK
-    own = AWIN // owners
+    shape = jax.ShapeDtypeStruct((sections, rows, AWIN // owners), jnp.bfloat16)
     return pl.pallas_call(
         functools.partial(relay_kernel, sections, owners),
-        out_shape=jax.ShapeDtypeStruct((sections, owners, rows, own), jnp.bfloat16),
+        out_shape=(shape,) * owners,
         in_specs=[VMEM_SPEC, VMEM_SPEC, SMEM_SPEC, SMEM_SPEC] + [VMEM_SPEC] * len(received),
-        out_specs=VMEM_SPEC,
+        out_specs=(VMEM_SPEC,) * owners,
         scratch_shapes=[pltpu.VMEM((chunks, rows, BLK), jnp.float32), pltpu.VMEM((sections, chunks + 8, BLK), jnp.float32)],
         compiler_params=params(),
         cost_estimate=pl.CostEstimate(flops=1 << 33, bytes_accessed=2 << 20, transcendentals=0),
     )(inputs, gain, repeats, me, *received)
 
 
-def feature_kernel(micro, scale, order_ref, in_ref, out_ref):
-    sources, rows, own = in_ref.shape
-    group = sources // micro
-    weights = [batch_weight(order_ref, m, micro) * scale for m in range(micro)]
-    for at in range(0, own, BLK):
-        total = jnp.zeros((BLK, BLK), jnp.float32)
-        for m in range(micro):
-            feats = in_ref[m * group:(m + 1) * group, :, at:at + BLK].reshape(group * rows, BLK)
-            total = total + gram(feats, feats) * weights[m]
-        out_ref[0, at:at + BLK] = total
-
-
-def feature_factor(order, gathered, micro, scale):
-    sources, rows, own = gathered.shape
+HALF = BLK // 2
+FEATURE_ROWS = BLK + HALF + 16
+
+
+def pack_three(first, second, third):
+    row, col = iotas()
+    low_row, low_col = row[:HALF], col[:HALF]
+    turned = pltpu.roll(third[HALF:], HALF, 1)
+    two = jnp.where(col >= row, first, second)
+    half = jnp.where(low_col < low_row, turned, third[:HALF])
+    tail_row = lax.broadcasted_iota(jnp.int32, (16, BLK), 0)
+    diagonal = jnp.sum(jnp.where(col == row, second, 0.0), axis=0, keepdims=True)
+    last = jnp.sum(jnp.where(low_col == low_row + HALF, third[HALF:], 0.0), axis=0, keepdims=True)
+    tail = jnp.where(tail_row == 0, diagonal, jnp.where(tail_row == 1, last, 0.0))
+    return jnp.concatenate([two, half, tail], axis=0)
+
+
+def unpack_three(packed):
+    row, col = iotas()
+    low_row, low_col = row[:HALF], col[:HALF]
+    two, half, tail = packed[:BLK], packed[BLK:BLK + HALF], packed[BLK + HALF:]
+    turned = two.T
+    first = jnp.where(col >= row, two, turned)
+    second = jnp.where(col < row, two, jnp.where(col == row, tail[0:1], turned))
+    across = jnp.concatenate([half, jnp.zeros_like(half)], axis=0).T
+    upper = jnp.where(low_col < low_row, across[:HALF], half)
+    corner = pltpu.roll(jnp.where(low_col < low_row, half, across[:HALF]), HALF, 1)
+    lower = jnp.where(low_col < HALF, across[HALF:], jnp.where(low_col == low_row + HALF, tail[1:2], corner))
+    return jnp.concatenate([first, second, upper, lower], axis=0)
+
+
+def feature_kernel(micro, scale, order_ref, me_ref, *refs):
+    in_refs, (own_ref, *out_refs) = refs[:-micro], refs[-micro:]
+    weight = batch_weight(order_ref, me_ref[0], micro) * scale
+    for mask, out_ref in enumerate([own_ref] + out_refs):
+        s = jnp.bitwise_xor(me_ref[0], mask)
+        blocks = []
+        for at in range(0, 3 * BLK, BLK):
+            feats = jnp.concatenate([ref[s, :, at:at + BLK] for ref in in_refs], axis=0)
+            blocks.append(gram(feats, feats) * weight)
+        out_ref[...] = pack_three(*blocks).astype(out_ref.dtype)
+
+
+def feature_terms(order, me, feats, micro, scale):
     return pl.pallas_call(
         functools.partial(feature_kernel, micro, scale),
-        out_shape=jax.ShapeDtypeStruct((1, own, BLK), jnp.float32),
-        in_specs=[SMEM_SPEC, VMEM_SPEC],
-        out_specs=VMEM_SPEC,
+        out_shape=(jax.ShapeDtypeStruct((FEATURE_ROWS, BLK), jnp.float32),)
+        + (jax.ShapeDtypeStruct((FEATURE_ROWS, BLK), jnp.bfloat16),) * (micro - 1),
+        in_specs=[SMEM_SPEC, SMEM_SPEC] + [VMEM_SPEC] * len(feats),
+        out_specs=(VMEM_SPEC,) * micro,
         compiler_params=params(),
-        cost_estimate=pl.CostEstimate(flops=2 * sources * rows * own * BLK, bytes_accessed=1 << 20, transcendentals=0),
-    )(order, gathered)
+        cost_estimate=pl.CostEstimate(flops=1 << 31, bytes_accessed=1 << 20, transcendentals=0),
+    )(order, me, *feats)
+
+
+def feature_sum_kernel(*refs):
+    total = refs[0][...]
+    for ref in refs[1:-1]:
+        total = total + ref[...].astype(jnp.float32)
+    refs[-1][0] = unpack_three(total)
 
 
 def fast_body(inputs, gain, repeats, order, hidden_grad):
@@ -310,19 +337,27 @@
     dp_count = lax.axis_size("dp")
     scale = 1.0 / (tok_rows * dp_count)
     gain = gain.reshape(-1, BLK)
-    plane = lax.axis_index("section").reshape(1)
+    plane, place = lax.axis_index("section").reshape(1), lax.axis_index("dp").reshape(1)
+    me = jnp.concatenate([plane, place])
     told, order = lax.optimization_barrier((messages(inputs, gain, repeats, plane), order))
     pieces = tuple(swapped(one, "section", mask) for mask, one in enumerate(told, 1))
 
-    far, near = hidden_terms(order, hidden_grad, lax.axis_index("dp").reshape(1), dp_count, scale)
+    far, near = hidden_terms(order, hidden_grad, place, dp_count, scale)
     came = swapped(far, "dp", 1)
     pieces, near = lax.optimization_barrier((pieces, near))
-    feats = relay(inputs, gain, repeats, plane, pieces, dp_count)
-    feats, near, came, order = lax.optimization_barrier((feats, near, came, order))
-    feats = feats.reshape((-1,) + feats.shape[2:])
-    feats = lax.all_to_all(feats, ("section", "dp"), 0, 0, tiled=True)
-    hidden_rows = hidden_factor(near, came)
-    feature_rows = feature_factor(order, feats, micro, scale)
+    feats = relay(inputs, gain, repeats, me, pieces, dp_count)
+    feats, near, came = lax.optimization_barrier((feats, near, came))
+    gathered = [feats[0]] + [swapped(one, "dp", mask) for mask, one in enumerate(feats[1:], 1)]
+    gathered, near = lax.optimization_barrier((gathered, near))
+    along_x, along_y, first, second = core_sum(near, came)
+    came_x, came_y = swapped(along_x, "dp", 2), swapped(along_y, "dp", 4)
+    own, *terms = feature_terms(order, plane, gathered, micro, scale)
+    own, first = lax.optimization_barrier((own, first))
+    terms = [swapped(one, "section", mask) for mask, one in enumerate(terms, 1)]
+    along_y, along_x, kept = pair_sum(first, came_x, second, came_y)
+    came_y, came_x = swapped(along_y, "dp", 4), swapped(along_x, "dp", 2)
+    hidden_rows = unpacked(kept, came_y, came_x)
+    feature_rows = small_call(feature_sum_kernel, jax.ShapeDtypeStruct((1, 3 * BLK, BLK), jnp.float32), own, *terms)
     return (feature_rows, hidden_rows)
 
 
@@ -382,7 +417,7 @@
             and inputs.shape[2] * sections % (16 * BLK) == 0
             and inputs.shape[1] % 16 == 0
             and dp_count == 8
-            and AWIN % (dp_count * BLK) == 0
+            and AWIN == dp_count * 3 * BLK
             and GWIN % (dp_count * 4 * BLK) == 0
         )
         return (fast_body if aligned else plain_body)(inputs, gain, repeats, order, hidden_grad)

time: 61.4 us -> 60.6 us (0.987)
  Pallas kernels: 24.5 us -> 15.3 us
  starting transfers between devices: 17.8 us -> 22.3 us
  waiting for transfers between devices: 14.7 us -> 18.9 us
    ppermute x8 -> x18, starting transfers between devices: 11.6 us -> 22.3 us  [swapped(): lax.ppermute(shard, axis, [(i, i ^ mask) for i in range(lax.axis_size(axi...]
    pallas_call x1, Pallas kernels: 13.1 us -> 3.47 us  [hidden_terms(): pl.pallas_call(functools.partial(hidden_kernel, micro, pairs, scale), out...]
    all_to_all x1 -> x0, starting transfers between devices: 6.15 us -> none  [fast_body(): feats = lax.all_to_all(feats, ('section', 'dp'), 0, 0, tiled=True)]
    ppermute x8 -> x18, waiting for transfers between devices: 14.7 us -> 18.9 us  [swapped(): lax.ppermute(shard, axis, [(i, i ^ mask) for i in range(lax.axis_size(axi...]
    pallas_call x3 -> x4, Pallas kernels: 1.32 us -> 2.16 us  [small_call(): pl.pallas_call(kernel, out_shape=shapes, in_specs=[VMEM_SPEC] * len(opera...]
    pallas_call x1, Pallas kernels: 1.63 us -> 1.01 us  [feature_terms(): pl.pallas_call(functools.partial(feature_kernel, micro, scale), out_shape...]
  transfers between devices with their start and end apart: 9 -> 18, of which waited for: 3 -> 8; matrix products, arithmetic and copies ran while one was open for 0% -> 0% of each run, Pallas kernels for 35% -> 20%
where the time goes in v5:
time: 60.6 us; the launch traced here: 60.5 us
  starting transfers between devices  22.3 us (37%)
  waiting for transfers between devices  18.9 us (31%)
  Pallas kernels  15.3 us (25%)
  local copies, waits for them, and re-layouts  2.56 us (4%)
  between operations  1.37 us (2%)
    ppermute x18, starting transfers between devices, swapped(): lax.ppermute(shard, axis, [(i, i ^ mask) for i in range(lax.axis_size(axi...  22.3 us
    ppermute x18, waiting for transfers between devices, swapped(): lax.ppermute(shard, axis, [(i, i ^ mask) for i in range(lax.axis_size(axi...  18.9 us
    pallas_call x1, Pallas kernels, relay(): pl.pallas_call(functools.partial(relay_kernel, sections, owners), out_sha...  6.83 us
    pallas_call x1, Pallas kernels, hidden_terms(): pl.pallas_call(functools.partial(hidden_kernel, micro, pairs, scale), out...  3.47 us
    unnamed x10, local copies, waits for them, and re-layouts  2.56 us
    pallas_call x4, Pallas kernels, small_call(): pl.pallas_call(kernel, out_shape=shapes, in_specs=[VMEM_SPEC] * len(opera...  2.16 us
    pallas_call x1, Pallas kernels, messages(): pl.pallas_call(message_kernel, out_shape=(shape,) * (micro - 1), in_specs...  1.8 us
  transfers between devices with their start and end apart: 18, of which 8 were waited for; matrix products, arithmetic and copies ran while one was open for 0% of the time, Pallas kernels for 20%

profile of v5, /device:TPU:0, one launch (start us, length us, event | category | flops | bytes accessed | tf_op | source)
XLA Modules:
  0.0 60.5 jit_solution(5975456086481956890)
XLA Ops:
  1.3 1.8 %shard_map.68 = (bf16[496,128]{1,0:T(8,128)(2,1)}, bf16[496,128]{1,0:T(8,128)(2,1)}, bf16[496,128]{1,0:T(8,128)(2,1)}) custom-call(bf16[4,32,1536]{2,1,0:T(8,128)(2,1)} %own_ref.1, f32[48,128]{1,0:T(8,128)} %bitcast.3, s32[1]{0:T(128)S(6)} %copy.7.repeats_ref, s32[1]{0:T(128)} %bitcast.1.me_ref), custom_call_target="tpu_custom_call" | custom-call | flops 1048576 | bytes 1048576 | tf_op jit(solution)/shard_map/pallas_call | solution.py:182
  3.1 3.0 %collective-permute-start = (bf16[496,128]{1,0:T(8,128)(2,1)}, bf16[496,128]{1,0:T(8,128)(2,1)S(1)}, u32[]{:S(2)}, u32[]{:S(2)}) collective-permute-start(bf16[496,128]{1,0:T(8,128)(2,1)} %get-tuple-element.59), channel_id=1, source_target_pairs={{0,8},{8,0},{16,24},{24,16},{1,9},{9,1},{17,25},{25,17},{2,10},{10... | collective-permute-start | bytes 380936 | tf_op jit(solution)/shard_map/ppermute | solution.py:159
  6.1 2.6 %collective-permute-start.1 = (bf16[496,128]{1,0:T(8,128)(2,1)}, bf16[496,128]{1,0:T(8,128)(2,1)S(1)}, u32[]{:S(2)}, u32[]{:S(2)}) collective-permute-start(bf16[496,128]{1,0:T(8,128)(2,1)} %get-tuple-element.60), channel_id=1, source_target_pairs={{0,16},{8,24},{16,0},{24,8},{1,17},{9,25},{17,1},{25,9},{2,18},{10... | collective-permute-start | bytes 380936 | tf_op jit(solution)/shard_map/ppermute | solution.py:159
  8.7 0.0 collective-permute-start.2
  8.7 0.0 copy-start.2
  8.7 1.9 %copy-done.2 = bf16[1,4,32,12288]{3,2,1,0:T(8,128)(2,1)S(1)} copy-done((bf16[1,4,32,12288]{3,2,1,0:T(8,128)(2,1)S(1)}, bf16[1,4,32,12288]{3,2,1,0:T(8,128)(2,1)}, u32[]{:S(2)}) %copy-start.2) | copy-done | bytes 3145752
  10.6 0.0 copy-start.3
  10.6 0.7 %copy-done.3 = s32[4]{0:T(128)S(1)} copy-done((s32[4]{0:T(128)S(1)}, s32[4]{0:T(128)}, u32[]{:S(2)}) %copy-start.3) | copy-done | bytes 40
  11.2 0.0 copy-start
  11.2 0.0 copy-start.1
  11.3 3.5 %shard_map.69 = (bf16[4,2,400,128]{3,2,1,0:T(8,128)(2,1)S(1)}, bf16[4,2,400,128]{3,2,1,0:T(8,128)(2,1)S(1)}) custom-call(s32[4]{0:T(128)S(1)} %copy-done.3, s32[1]{0:T(128)} %bitcast.2._, bf16[1,4,32,12288]{3,2,1,0:T(8,128)(2,1)S(1)} %copy-done.2, bf16[1,4,32,12288]{3,2,1,0:T(8,128)(2,1)S(1)} %copy-done.2), custom_call_target="tpu_custom_call" | custom-call | flops 2147483648 | bytes 1024 | tf_op jit(solution)/shard_map/pallas_call | solution.py:80
  14.7 0.1 collective-permute-start.3
  14.8 0.1 pad_add_fusion.me_ref
  14.9 0.0 collective-permute-done.refs_0_
  14.9 4.0 %collective-permute-done.1.refs_1_ = bf16[496,128]{1,0:T(8,128)(2,1)S(1)} collective-permute-done((bf16[496,128]{1,0:T(8,128)(2,1)}, bf16[496,128]{1,0:T(8,128)(2,1)S(1)}, u32[]{:S(2)}, u32[]{:S(2)}) %collective-permute-start.1) | collective-permute-done | bytes 127008 | tf_op jit(solution)/shard_map/ppermute | solution.py:159
  18.9 0.0 collective-permute-done.2.refs_2_
  18.9 0.0 copy-done
  18.9 0.0 copy-done.1
  18.9 0.0 copy-start.4
  19.0 6.8 %shard_map.70 = (bf16[4,32,384]{2,1,0:T(8,128)(2,1)S(1)}, bf16[4,32,384]{2,1,0:T(8,128)(2,1)S(1)}, bf16[4,32,384]{2,1,0:T(8,128)(2,1)S(1)}, bf16[4,32,384]{2,1,0...) custom-call(bf16[4,32,1536]{2,1,0:T(8,128)(2,1)S(1)} %copy-done, ...), custom_call_target="tpu_custom_call" | custom-call | flops 8589934592 | bytes 2097152 | tf_op jit(solution)/shard_map/pallas_call | solution.py:262
  25.8 0.0 collective-permute-done.3.came_ref
  25.8 0.1 collective-permute-start.4
  25.9 1.6 %collective-permute-start.5 = (bf16[4,32,384]{2,1,0:T(8,128)(2,1)S(1)}, bf16[4,32,384]{2,1,0:T(8,128)(2,1)S(1)}, u32[]{:S(2)}, u32[]{:S(2)}) collective-permute-start(bf16[4,32,384]{2,1,0:T(8,128)(2,1)S(1)} %get-tuple-element.78), channel_id=1, source_target_pairs={{0,2},{1,3},{2,0},{3,1},{4,6},{5,7},{6,4},{7,5},{8,10},{9,11},{10,... | collective-permute-start | bytes 294920 | tf_op jit(solution)/shard_map/ppermute | solution.py:159
  27.4 0.3 collective-permute-start.6
  27.8 1.5 %collective-permute-start.7 = (bf16[4,32,384]{2,1,0:T(8,128)(2,1)S(1)}, bf16[4,32,384]{2,1,0:T(8,128)(2,1)S(1)}, u32[]{:S(2)}, u32[]{:S(2)}) collective-permute-start(bf16[4,32,384]{2,1,0:T(8,128)(2,1)S(1)} %get-tuple-element.80), channel_id=1, source_target_pairs={{0,4},{1,5},{2,6},{3,7},{4,0},{5,1},{6,2},{7,3},{8,12},{9,13},{10,... | collective-permute-start | bytes 294920 | tf_op jit(solution)/shard_map/ppermute | solution.py:159
  29.3 0.2 collective-permute-start.8
  29.4 0.0 collective-permute-done.4.refs_1_
  29.4 2.4 %collective-permute-start.9 = (bf16[4,32,384]{2,1,0:T(8,128)(2,1)S(1)}, bf16[4,32,384]{2,1,0:T(8,128)(2,1)S(1)}, u32[]{:S(2)}, u32[]{:S(2)}) collective-permute-start(bf16[4,32,384]{2,1,0:T(8,128)(2,1)S(1)} %get-tuple-element.82), channel_id=1, source_target_pairs={{0,6},{1,7},{2,4},{3,5},{4,2},{5,3},{6,0},{7,1},{8,14},{9,15},{10,... | collective-permute-start | bytes 294920 | tf_op jit(solution)/shard_map/ppermute | solution.py:159
  31.9 0.0 collective-permute-done.5.refs_2_
  31.9 0.9 %collective-permute-start.10 = (bf16[4,32,384]{2,1,0:T(8,128)(2,1)S(1)}, bf16[4,32,384]{2,1,0:T(8,128)(2,1)S(1)}, u32[]{:S(2)}, u32[]{:S(2)}) collective-permute-start(bf16[4,32,384]{2,1,0:T(8,128)(2,1)S(1)} %get-tuple-element.83), channel_id=1, source_target_pairs={{0,7},{1,6},{2,5},{3,4},{4,3},{5,2},{6,1},{7,0},{8,15},{9,14},{10,... | collective-permute-start | bytes 294920 | tf_op jit(solution)/shard_map/ppermute | solution.py:159
  32.8 0.0 collective-permute-done.6.refs_3_
  32.8 0.5 collective-permute-done.7.refs_4_
  33.3 5.2 %collective-permute-done.8.refs_5_ = bf16[4,32,384]{2,1,0:T(8,128)(2,1)S(1)} collective-permute-done((bf16[4,32,384]{2,1,0:T(8,128)(2,1)S(1)}, bf16[4,32,384]{2,1,0:T(8,128)(2,1)S(1)}, u32[]{:S(2)}, u32[]{:S(2)}) %collective-permute-start.8) | collective-permute-done | bytes 98336 | tf_op jit(solution)/shard_map/ppermute | solution.py:159
  38.6 0.0 collective-permute-done.9.refs_6_
  38.6 0.0 collective-permute-done.10.refs_7_
  38.6 0.2 shard_map.72
  38.8 1.6 %collective-permute-start.14 = (bf16[2,400,128]{2,1,0:T(8,128)(2,1)S(1)}, bf16[2,400,128]{2,1,0:T(8,128)(2,1)S(1)}, u32[]{:S(2)}, u32[]{:S(2)}) collective-permute-start(bf16[2,400,128]{2,1,0:T(8,128)(2,1)S(1)} %get-tuple-element.102), channel_id=1, source_target_pairs={{0,2},{1,3},{2,0},{3,1},{4,6},{5,7},{6,4},{7,5},{8,10},{9,11},{10,... | collective-permute-start | bytes 614408 | tf_op jit(solution)/shard_map/ppermute | solution.py:159
  40.3 1.5 %collective-permute-start.15 = (bf16[2,400,128]{2,1,0:T(8,128)(2,1)S(1)}, bf16[2,400,128]{2,1,0:T(8,128)(2,1)S(1)}, u32[]{:S(2)}, u32[]{:S(2)}) collective-permute-start(bf16[2,400,128]{2,1,0:T(8,128)(2,1)S(1)} %get-tuple-element.104), channel_id=1, source_target_pairs={{0,4},{1,5},{2,6},{3,7},{4,0},{5,1},{6,2},{7,3},{8,12},{9,13},{10,... | collective-permute-start | bytes 614408 | tf_op jit(solution)/shard_map/ppermute | solution.py:159
  41.8 0.0 copy-done.4
  41.8 1.0 %shard_map.71 = (f32[208,128]{1,0:T(8,128)S(1)}, bf16[208,128]{1,0:T(8,128)(2,1)S(1)}, bf16[208,128]{1,0:T(8,128)(2,1)S(1)}, bf16[208,128]{1,0:T(8,128)(2,1)S(1)}) custom-call(s32[4]{0:T(128)S(1)} %copy-done.4, s32[1]{0:T(128)} %bitcast.1.me_ref, bf16[4,32,384]{2,1,0:T(8,128)(2,1)S(1)} %get-tuple-element.85.refs_0_, ...), custom_call_target="tpu_custom_call" | custom-call | flops 2147483648 | bytes 1048576 | tf_op jit(solution)/shard_map/pallas_call | solution.py:317
  42.9 3.3 %collective-permute-done.14.came_x_ref = bf16[2,400,128]{2,1,0:T(8,128)(2,1)S(1)} collective-permute-done((bf16[2,400,128]{2,1,0:T(8,128)(2,1)S(1)}, bf16[2,400,128]{2,1,0:T(8,128)(2,1)S(1)}, u32[]{:S(2)}, u32[]{:S(2)}) %collective-permute-start.14) | collective-permute-done | bytes 204832 | tf_op jit(solution)/shard_map/ppermute | solution.py:159
  46.2 1.2 %collective-permute-done.15.came_y_ref = bf16[2,400,128]{2,1,0:T(8,128)(2,1)S(1)} collective-permute-done((bf16[2,400,128]{2,1,0:T(8,128)(2,1)S(1)}, bf16[2,400,128]{2,1,0:T(8,128)(2,1)S(1)}, u32[]{:S(2)}, u32[]{:S(2)}) %collective-permute-start.15) | collective-permute-done | bytes 204832 | tf_op jit(solution)/shard_map/ppermute | solution.py:159
  47.4 0.1 shard_map.74
  47.5 1.6 %collective-permute-start.16 = (bf16[400,128]{1,0:T(8,128)(2,1)S(1)}, bf16[400,128]{1,0:T(8,128)(2,1)S(1)}, u32[]{:S(2)}, u32[]{:S(2)}) collective-permute-start(bf16[400,128]{1,0:T(8,128)(2,1)S(1)} %get-tuple-element.106), channel_id=1, source_target_pairs={{0,4},{1,5},{2,6},{3,7},{4,0},{5,1},{6,2},{7,3},{8,12},{9,13},{10,... | collective-permute-start | bytes 307208 | tf_op jit(solution)/shard_map/ppermute | solution.py:159
  49.1 0.5 collective-permute-start.17
  49.6 1.9 %collective-permute-start.11 = (bf16[208,128]{1,0:T(8,128)(2,1)S(1)}, bf16[208,128]{1,0:T(8,128)(2,1)S(1)}, u32[]{:S(2)}, u32[]{:S(2)}) collective-permute-start(bf16[208,128]{1,0:T(8,128)(2,1)S(1)} %get-tuple-element.98), channel_id=1, source_target_pairs={{0,8},{8,0},{16,24},{24,16},{1,9},{9,1},{17,25},{25,17},{2,10},{10... | collective-permute-start | bytes 159752 | tf_op jit(solution)/shard_map/ppermute | solution.py:159
  51.5 1.0 %collective-permute-start.12 = (bf16[208,128]{1,0:T(8,128)(2,1)S(1)}, bf16[208,128]{1,0:T(8,128)(2,1)S(1)}, u32[]{:S(2)}, u32[]{:S(2)}) collective-permute-start(bf16[208,128]{1,0:T(8,128)(2,1)S(1)} %get-tuple-element.99), channel_id=1, source_target_pairs={{0,16},{8,24},{16,0},{24,8},{1,17},{9,25},{17,1},{25,9},{2,18},{10... | collective-permute-start | bytes 159752 | tf_op jit(solution)/shard_map/ppermute | solution.py:159
  52.5 1.5 %collective-permute-start.13 = (bf16[208,128]{1,0:T(8,128)(2,1)S(1)}, bf16[208,128]{1,0:T(8,128)(2,1)S(1)}, u32[]{:S(2)}, u32[]{:S(2)}) collective-permute-start(bf16[208,128]{1,0:T(8,128)(2,1)S(1)} %get-tuple-element.100), channel_id=1, source_target_pairs={{0,24},{8,16},{16,8},{24,0},{1,25},{9,17},{17,9},{25,1},{2,26},{10... | collective-permute-start | bytes 159752 | tf_op jit(solution)/shard_map/ppermute | solution.py:159
  54.0 0.2 collective-permute-done.11.refs_1_
  54.2 3.1 %collective-permute-done.12.refs_2_ = bf16[208,128]{1,0:T(8,128)(2,1)S(1)} collective-permute-done((bf16[208,128]{1,0:T(8,128)(2,1)S(1)}, bf16[208,128]{1,0:T(8,128)(2,1)S(1)}, u32[]{:S(2)}, u32[]{:S(2)}) %collective-permute-start.12) | collective-permute-done | bytes 53280 | tf_op jit(solution)/shard_map/ppermute | solution.py:159
  57.3 1.2 %collective-permute-done.13.refs_3_ = bf16[208,128]{1,0:T(8,128)(2,1)S(1)} collective-permute-done((bf16[208,128]{1,0:T(8,128)(2,1)S(1)}, bf16[208,128]{1,0:T(8,128)(2,1)S(1)}, u32[]{:S(2)}, u32[]{:S(2)}) %collective-permute-start.13) | collective-permute-done | bytes 53280 | tf_op jit(solution)/shard_map/ppermute | solution.py:159
  58.5 0.8 %shard_map.73 = f32[1,384,128]{2,1,0:T(8,128)} custom-call(f32[208,128]{1,0:T(8,128)S(1)} %get-tuple-element.97.refs_0_, bf16[208,128]{1,0:T(8,128)(2,1)S(1)} %collective-permute-done.11.refs_1_, bf16[208,128]{1,0:T(8,128)(2,1)S(1)} %collective-permute-done.12.refs_2_, bf16[208,128]{1,0:T(8,128)(2,1)S(1)} %collective-permute-done.13.refs_3_), custom_call_target="tpu_custom_call" | custom-call | flops 1048576 | bytes 1024 | tf_op jit(solution)/shard_map/pallas_call | solution.py:95
  59.4 0.0 collective-permute-done.16.came_y_ref
  59.4 0.0 collective-permute-done.17.came_x_ref
  59.4 1.1 %shard_map.75 = f32[1,1536,128]{2,1,0:T(8,128)} custom-call(f32[2,400,128]{2,1,0:T(8,128)S(1)} %get-tuple-element.105.kept_ref, bf16[400,128]{1,0:T(8,128)(2,1)S(1)} %collective-permute-done.16.came_y_ref, bf16[400,128]{1,0:T(8,128)(2,1)S(1)} %collective-permute-done.17.came_x_ref), custom_call_target="tpu_custom_call" | custom-call | flops 1048576 | bytes 1024 | tf_op jit(solution)/shard_map/pallas_call | solution.py:95
Async XLA Ops:
  3.1 11.8 %collective-permute-start = (bf16[496,128]{1,0:T(8,128)(2,1)}, bf16[496,128]{1,0:T(8,128)(2,1)S(1)}, u32[]{:S(2)}, u32[]{:S(2)}) collective-permute-start(bf16[496,128]{1,0:T(8,128)(2,1)} %get-tuple-element.59), channel_id=1, source_target_pairs={{0,8},{8,0},{16,24},{24,16},{1,9},{9,1},{17,25},{25,17},{2,10},{10... | collective-permute-start | bytes 380936 | tf_op jit(solution)/shard_map/ppermute | solution.py:159
  6.1 12.8 %collective-permute-start.1 = (bf16[496,128]{1,0:T(8,128)(2,1)}, bf16[496,128]{1,0:T(8,128)(2,1)S(1)}, u32[]{:S(2)}, u32[]{:S(2)}) collective-permute-start(bf16[496,128]{1,0:T(8,128)(2,1)} %get-tuple-element.60), channel_id=1, source_target_pairs={{0,16},{8,24},{16,0},{24,8},{1,17},{9,25},{17,1},{25,9},{2,18},{10... | collective-permute-start | bytes 380936 | tf_op jit(solution)/shard_map/ppermute | solution.py:159
  8.7 10.2 %collective-permute-start.2 = (bf16[496,128]{1,0:T(8,128)(2,1)}, bf16[496,128]{1,0:T(8,128)(2,1)S(1)}, u32[]{:S(2)}, u32[]{:S(2)}) collective-permute-start(bf16[496,128]{1,0:T(8,128)(2,1)} %get-tuple-element.61), channel_id=1, source_target_pairs={{0,24},{8,16},{16,8},{24,0},{1,25},{9,17},{17,9},{25,1},{2,26},{10... | collective-permute-start | bytes 380936 | tf_op jit(solution)/shard_map/ppermute | solution.py:159
  8.7 1.9 %copy-start.2 = (bf16[1,4,32,12288]{3,2,1,0:T(8,128)(2,1)S(1)}, bf16[1,4,32,12288]{3,2,1,0:T(8,128)(2,1)}, u32[]{:S(2)}) copy-start(bf16[1,4,32,12288]{3,2,1,0:T(8,128)(2,1)} %near_grad_ref.1) | copy-start | bytes 9437188
  10.6 0.7 %copy-start.3 = (s32[4]{0:T(128)S(1)}, s32[4]{0:T(128)}, u32[]{:S(2)}) copy-start(s32[4]{0:T(128)} %order_ref.1) | copy-start | bytes 52
  11.2 7.7 %copy-start = (bf16[4,32,1536]{2,1,0:T(8,128)(2,1)S(1)}, bf16[4,32,1536]{2,1,0:T(8,128)(2,1)}, u32[]{:S(2)}) copy-start(bf16[4,32,1536]{2,1,0:T(8,128)(2,1)} %own_ref.1) | copy-start | bytes 1179652
  11.2 7.7 %copy-start.1 = (f32[1,6144]{1,0:T(1,128)S(1)}, f32[1,6144]{1,0:T(1,128)}, u32[]{:S(2)}) copy-start(f32[1,6144]{1,0:T(1,128)} %param.6) | copy-start | bytes 73732
  14.7 11.1 %collective-permute-start.3 = (bf16[4,2,400,128]{3,2,1,0:T(8,128)(2,1)S(1)}, bf16[4,2,400,128]{3,2,1,0:T(8,128)(2,1)S(1)}, u32[]{:S(2)}, u32[]{:S(2)}) collective-permute-start(bf16[4,2,400,128]{3,2,1,0:T(8,128)(2,1)S(1)} %get-tuple-element.75), channel_id=1, source_target_pairs={{0,1},{1,0},{2,3},{3,2},{4,5},{5,4},{6,7},{7,6},{8,9},{9,8},{10,11... | collective-permute-start | bytes 2457608 | tf_op jit(solution)/shard_map/ppermute | solution.py:159
  18.9 22.9 %copy-start.4 = (s32[4]{0:T(128)S(1)}, s32[4]{0:T(128)}, u32[]{:S(2)}) copy-start(s32[4]{0:T(128)} %order_ref.1) | copy-start | bytes 52
  25.8 3.6 %collective-permute-start.4 = (bf16[4,32,384]{2,1,0:T(8,128)(2,1)S(1)}, bf16[4,32,384]{2,1,0:T(8,128)(2,1)S(1)}, u32[]{:S(2)}, u32[]{:S(2)}) collective-permute-start(bf16[4,32,384]{2,1,0:T(8,128)(2,1)S(1)} %get-tuple-element.77), channel_id=1, source_target_pairs={{0,1},{1,0},{2,3},{3,2},{4,5},{5,4},{6,7},{7,6},{8,9},{9,8},{10,11... | collective-permute-start | bytes 294920 | tf_op jit(solution)/shard_map/ppermute | solution.py:159
  25.9 6.0 %collective-permute-start.5 = (bf16[4,32,384]{2,1,0:T(8,128)(2,1)S(1)}, bf16[4,32,384]{2,1,0:T(8,128)(2,1)S(1)}, u32[]{:S(2)}, u32[]{:S(2)}) collective-permute-start(bf16[4,32,384]{2,1,0:T(8,128)(2,1)S(1)} %get-tuple-element.78), channel_id=1, source_target_pairs={{0,2},{1,3},{2,0},{3,1},{4,6},{5,7},{6,4},{7,5},{8,10},{9,11},{10,... | collective-permute-start | bytes 294920 | tf_op jit(solution)/shard_map/ppermute | solution.py:159
  27.4 5.4 %collective-permute-start.6 = (bf16[4,32,384]{2,1,0:T(8,128)(2,1)S(1)}, bf16[4,32,384]{2,1,0:T(8,128)(2,1)S(1)}, u32[]{:S(2)}, u32[]{:S(2)}) collective-permute-start(bf16[4,32,384]{2,1,0:T(8,128)(2,1)S(1)} %get-tuple-element.79), channel_id=1, source_target_pairs={{0,3},{1,2},{2,1},{3,0},{4,7},{5,6},{6,5},{7,4},{8,11},{9,10},{10,... | collective-permute-start | bytes 294920 | tf_op jit(solution)/shard_map/ppermute | solution.py:159
  27.8 5.6 %collective-permute-start.7 = (bf16[4,32,384]{2,1,0:T(8,128)(2,1)S(1)}, bf16[4,32,384]{2,1,0:T(8,128)(2,1)S(1)}, u32[]{:S(2)}, u32[]{:S(2)}) collective-permute-start(bf16[4,32,384]{2,1,0:T(8,128)(2,1)S(1)} %get-tuple-element.80), channel_id=1, source_target_pairs={{0,4},{1,5},{2,6},{3,7},{4,0},{5,1},{6,2},{7,3},{8,12},{9,13},{10,... | collective-permute-start | bytes 294920 | tf_op jit(solution)/shard_map/ppermute | solution.py:159
  29.3 9.3 %collective-permute-start.8 = (bf16[4,32,384]{2,1,0:T(8,128)(2,1)S(1)}, bf16[4,32,384]{2,1,0:T(8,128)(2,1)S(1)}, u32[]{:S(2)}, u32[]{:S(2)}) collective-permute-start(bf16[4,32,384]{2,1,0:T(8,128)(2,1)S(1)} %get-tuple-element.81), channel_id=1, source_target_pairs={{0,5},{1,4},{2,7},{3,6},{4,1},{5,0},{6,3},{7,2},{8,13},{9,12},{10,... | collective-permute-start | bytes 294920 | tf_op jit(solution)/shard_map/ppermute | solution.py:159
  29.4 9.1 %collective-permute-start.9 = (bf16[4,32,384]{2,1,0:T(8,128)(2,1)S(1)}, bf16[4,32,384]{2,1,0:T(8,128)(2,1)S(1)}, u32[]{:S(2)}, u32[]{:S(2)}) collective-permute-start(bf16[4,32,384]{2,1,0:T(8,128)(2,1)S(1)} %get-tuple-element.82), channel_id=1, source_target_pairs={{0,6},{1,7},{2,4},{3,5},{4,2},{5,3},{6,0},{7,1},{8,14},{9,15},{10,... | collective-permute-start | bytes 294920 | tf_op jit(solution)/shard_map/ppermute | solution.py:159
  31.9 6.7 %collective-permute-start.10 = (bf16[4,32,384]{2,1,0:T(8,128)(2,1)S(1)}, bf16[4,32,384]{2,1,0:T(8,128)(2,1)S(1)}, u32[]{:S(2)}, u32[]{:S(2)}) collective-permute-start(bf16[4,32,384]{2,1,0:T(8,128)(2,1)S(1)} %get-tuple-element.83), channel_id=1, source_target_pairs={{0,7},{1,6},{2,5},{3,4},{4,3},{5,2},{6,1},{7,0},{8,15},{9,14},{10,... | collective-permute-start | bytes 294920 | tf_op jit(solution)/shard_map/ppermute | solution.py:159
  38.8 7.4 %collective-permute-start.14 = (bf16[2,400,128]{2,1,0:T(8,128)(2,1)S(1)}, bf16[2,400,128]{2,1,0:T(8,128)(2,1)S(1)}, u32[]{:S(2)}, u32[]{:S(2)}) collective-permute-start(bf16[2,400,128]{2,1,0:T(8,128)(2,1)S(1)} %get-tuple-element.102), channel_id=1, source_target_pairs={{0,2},{1,3},{2,0},{3,1},{4,6},{5,7},{6,4},{7,5},{8,10},{9,11},{10,... | collective-permute-start | bytes 614408 | tf_op jit(solution)/shard_map/ppermute | solution.py:159
  40.3 7.1 %collective-permute-start.15 = (bf16[2,400,128]{2,1,0:T(8,128)(2,1)S(1)}, bf16[2,400,128]{2,1,0:T(8,128)(2,1)S(1)}, u32[]{:S(2)}, u32[]{:S(2)}) collective-permute-start(bf16[2,400,128]{2,1,0:T(8,128)(2,1)S(1)} %get-tuple-element.104), channel_id=1, source_target_pairs={{0,4},{1,5},{2,6},{3,7},{4,0},{5,1},{6,2},{7,3},{8,12},{9,13},{10,... | collective-permute-start | bytes 614408 | tf_op jit(solution)/shard_map/ppermute | solution.py:159
  47.5 11.9 %collective-permute-start.16 = (bf16[400,128]{1,0:T(8,128)(2,1)S(1)}, bf16[400,128]{1,0:T(8,128)(2,1)S(1)}, u32[]{:S(2)}, u32[]{:S(2)}) collective-permute-start(bf16[400,128]{1,0:T(8,128)(2,1)S(1)} %get-tuple-element.106), channel_id=1, source_target_pairs={{0,4},{1,5},{2,6},{3,7},{4,0},{5,1},{6,2},{7,3},{8,12},{9,13},{10,... | collective-permute-start | bytes 307208 | tf_op jit(solution)/shard_map/ppermute | solution.py:159
  49.1 10.3 %collective-permute-start.17 = (bf16[400,128]{1,0:T(8,128)(2,1)S(1)}, bf16[400,128]{1,0:T(8,128)(2,1)S(1)}, u32[]{:S(2)}, u32[]{:S(2)}) collective-permute-start(bf16[400,128]{1,0:T(8,128)(2,1)S(1)} %get-tuple-element.107), channel_id=1, source_target_pairs={{0,2},{1,3},{2,0},{3,1},{4,6},{5,7},{6,4},{7,5},{8,10},{9,11},{10,... | collective-permute-start | bytes 307208 | tf_op jit(solution)/shard_map/ppermute | solution.py:159
  49.6 4.6 %collective-permute-start.11 = (bf16[208,128]{1,0:T(8,128)(2,1)S(1)}, bf16[208,128]{1,0:T(8,128)(2,1)S(1)}, u32[]{:S(2)}, u32[]{:S(2)}) collective-permute-start(bf16[208,128]{1,0:T(8,128)(2,1)S(1)} %get-tuple-element.98), channel_id=1, source_target_pairs={{0,8},{8,0},{16,24},{24,16},{1,9},{9,1},{17,25},{25,17},{2,10},{10... | collective-permute-start | bytes 159752 | tf_op jit(solution)/shard_map/ppermute | solution.py:159
  51.5 5.8 %collective-permute-start.12 = (bf16[208,128]{1,0:T(8,128)(2,1)S(1)}, bf16[208,128]{1,0:T(8,128)(2,1)S(1)}, u32[]{:S(2)}, u32[]{:S(2)}) collective-permute-start(bf16[208,128]{1,0:T(8,128)(2,1)S(1)} %get-tuple-element.99), channel_id=1, source_target_pairs={{0,16},{8,24},{16,0},{24,8},{1,17},{9,25},{17,1},{25,9},{2,18},{10... | collective-permute-start | bytes 159752 | tf_op jit(solution)/shard_map/ppermute | solution.py:159
  52.5 6.0 %collective-permute-start.13 = (bf16[208,128]{1,0:T(8,128)(2,1)S(1)}, bf16[208,128]{1,0:T(8,128)(2,1)S(1)}, u32[]{:S(2)}, u32[]{:S(2)}) collective-permute-start(bf16[208,128]{1,0:T(8,128)(2,1)S(1)} %get-tuple-element.100), channel_id=1, source_target_pairs={{0,24},{8,16},{16,8},{24,0},{1,25},{9,17},{17,9},{25,1},{2,26},{10... | collective-permute-start | bytes 159752 | tf_op jit(solution)/shard_map/ppermute | solution.py:159
